TPU v7x, 32 devices: a whole 2x2x4 slice. The times are simulated.
32 devices in a mesh: tx: 4 (over x, core), img: 8 (over z, y).
Axes of the slice: x: 2, y: 2, z: 4, core: 2. Of those that a mesh axis runs over, the one named last changes fastest.
Arguments:
- encoded: bfloat16 [1024, 1024, 512], P('tx', 'img'), may hold values from -6 to 6
- signs: int32 [1024, 64], replicated, may hold values from -1 to 1, as said below
- tx_block: int32 [64, 2048], P('tx'), may hold values from 0 to 1
- rx_block: int32 [1024, 2048], P(None, 'img'), may hold values from 0 to 2
- apodization: int32 [1024, 2048], P(None, 'img'), may hold values 0 or 1
Outputs:
- image: float32 [2048, 128], P('img', 'tx')
Inputs may be any that keep to these rules, and one draw needn't show every extreme that they name: `signs`: every entry is 1 or -1. The columns are 64 distinct columns of the Sylvester Hadamard matrix of order 1024, every row multiplied by its own sign, so that two different columns are orthogonal.
All inputs are finite; a program needn't handle non-finite values. No bound on the sum of `apodization` on one device may be relied on, other than what follows from the above.
Results may differ from a plain program's by a relative error of at most 0.0029.
Values may be sent and summed in bfloat16 or wider, within the bound.
No kernel may reach another device: no remote copies, remote signals or barrier semaphores. Data moves between devices by JAX's collectives and lax.ppermute only.
A program may use at most 192 MiB of HBM per device.

v0:
```python
import math

import jax
import jax.numpy as jnp
from jax import lax
from jax.sharding import PartitionSpec as P

E = 1024
K = 64
R = 1024
L = 128


def weights_for(rx_rows, mask_rows, tx_rows, block_count):
    total_block = tx_rows.T[:, :, None] + rx_rows.T[:, None, :]
    levels = jnp.arange(block_count, dtype=jnp.int32)
    chosen = total_block[..., None] == levels
    weight = jnp.where(
        chosen, mask_rows.T[:, None, :, None].astype(jnp.bfloat16), jnp.zeros((), jnp.bfloat16)
    )
    return weight.reshape(weight.shape[0], -1)


def on_device(encoded, signs, tx_block, rx_block, apodization):
    events_here, receivers_here, sample_count = encoded.shape
    transmits_here = tx_block.shape[0]
    lines_here = rx_block.shape[1]
    block_count = sample_count // L
    tx_index = lax.axis_index("tx")
    img_index = lax.axis_index("img")
    flat = encoded.reshape(events_here, receivers_here * sample_count)
    sign_rows = lax.dynamic_slice_in_dim(signs, tx_index * events_here, events_here, 0).astype(
        jnp.bfloat16
    )
    summed = lax.psum_scatter(
        lax.dot_general(
            sign_rows, flat, (((0,), (0,)), ((), ())), preferred_element_type=jnp.float32
        ),
        "tx",
        scatter_dimension=0,
        tiled=True,
    )
    decoded = (
        (summed * (1.0 / E))
        .astype(jnp.bfloat16)
        .reshape(transmits_here, receivers_here, sample_count)
    )
    own_tx = lax.dynamic_slice_in_dim(tx_block, img_index * lines_here, lines_here, 1)
    weight = weights_for(rx_block, apodization, own_tx, block_count)
    image = jnp.dot(
        weight,
        lax.all_gather(decoded, "img", axis=1, tiled=True).reshape(-1, L),
        preferred_element_type=jnp.float32,
    )
    scale = math.sqrt(E / (K * R))
    return lax.psum_scatter(image * scale, "tx", scatter_dimension=1, tiled=True)


def solution(mesh):
    placed = (P("tx", "img", None), P(), P("tx", None), P(None, "img"), P(None, "img"))
    return jax.shard_map(
        on_device, mesh=mesh, in_specs=placed, out_specs=P("img", "tx"), check_vma=False
    )
```

profile of v0, /device:TPU:0, one launch (start us, length us, event | category | flops | bytes accessed | tf_op | source)
XLA Modules:
  0.0 490.7 jit_solution(17281481091864063729)
XLA Ops:
  6.5 0.0 copy-start
  6.5 0.0 reduce-scatter.3.cloned.1.call-start
  6.5 31.0 %copy.9 = bf16[32,8,128,512]{3,1,2,0:T(8,128)(2,1)} copy(bf16[32,8,128,512]{3,2,1,0:T(8,128)(2,1)} %bitcast.15) | data formatting | bytes 67108864
  37.5 22.2 %fusion.1 = f32[64,65536]{1,0:T(8,128)} fusion(bf16[256,65536]{1,0:T(8,128)(2,1)} %bitcast.14, s32[1024,64]{0,1:T(8,128)} %param.6, s32[]{:T(128)S(6)} %select_n.23), kind=kOutput, calls=%fused_computation.7 | convolution fusion | flops 2147500032 | bytes 50397188 | tf_op jit(solution)/shard_map/dot_general | solution.py:36
  59.7 0.0 copy-start.3
  59.7 0.0 copy-start.2
  59.8 0.0 reduce-scatter.3.cloned.1.call-update
  59.8 0.0 all-gather.2.cloned.1.call-start
  59.8 128.9 %reduce-scatter.3.cloned.1.call-done = f32[16,65536]{1,0:T(8,128)} async-done(((f32[64,65536]{1,0:T(8,128)}), f32[16,65536]{1,0:T(8,128)}) %reduce-scatter.3.cloned.1.call-update) | async-done | bytes 4194320 | tf_op jit(solution)/shard_map/reduce_scatter | solution.py:35
  188.8 2.4 multiply_convert_fusion
  191.2 2.0 copy.10
  193.2 0.0 all-gather.2.cloned.1.call-update
  193.2 0.2 reduce-scatter.5.cloned.1.call-start
  193.5 0.0 copy-done
  193.5 0.0 copy-done.3
  193.5 0.1 convert_bitcast_fusion
  193.6 0.0 copy-done.2
  193.6 8.0 %broadcast_add_fusion = s32[256,16,1024]{0,2,1:T(8,128)} fusion(s32[256,1024]{0,1:T(8,128)S(1)} %bitcast.18, s32[256,16]{0,1:T(8,128)S(1)} %dynamic-slice_bitcast_fusion), kind=kLoop, calls=%fused_computation.2 | loop fusion | flops 4194304 | bytes 17842176 | tf_op jit(solution)/shard_map/add | solution.py:15
  201.6 21.3 %fusion = bf16[256,16,1024,4]{0,3,2,1:T(4,128)(2,1)} fusion(s32[256,16,1024]{0,2,1:T(8,128)} %broadcast_add_fusion, bf16[256,1024]{0,1:T(8,128)(2,1)S(1)} %convert_bitcast_fusion), kind=kLoop, calls=%fused_computation.1 | loop fusion | flops 33554432 | bytes 50855936 | tf_op jit(solution)/shard_map/jit(_where)/select_n | solution.py:18
  222.9 46.3 %select_n.22 = bf16[256,65536]{0,1:T(8,128)(2,1)} reshape(bf16[256,16,1024,4]{0,3,2,1:T(4,128)(2,1)} %fusion) | data formatting | bytes 67108864 | tf_op jit(solution)/shard_map/jit(_where)/select_n | solution.py:18
  269.2 151.8 %all-gather.2.cloned.1.call-done = bf16[16,1024,512]{2,1,0:T(8,128)(2,1)} async-done(((bf16[16,128,512]{2,1,0:T(8,128)(2,1)}), bf16[16,1024,512]{2,1,0:T(8,128)(2,1)}) %all-gather.2.cloned.1.call-update) | async-done | bytes 16777232 | tf_op jit(solution)/shard_map/all_gather | solution.py:52
  421.0 26.6 %reshape.55 = bf16[65536,128]{1,0:T(8,128)(2,1)} reshape(bf16[16,1024,512]{2,1,0:T(8,128)(2,1)} %all-gather.2.cloned.1.call-done) | data formatting | bytes 33554432 | tf_op jit(solution)/shard_map/reshape | solution.py:52
  447.6 0.0 copy-start.1
  447.6 18.7 %convolution_multiply_fusion = f32[256,128]{0,1:T(8,128)} fusion(bf16[256,65536]{0,1:T(8,128)(2,1)} %select_n.22, bf16[65536,128]{1,0:T(8,128)(2,1)} %reshape.55), kind=kOutput, calls=%fused_computation.4 | convolution fusion | flops 4295000064 | bytes 50462720 | tf_op jit(solution)/shard_map/dot_general | solution.py:50
  466.3 0.0 reduce-scatter.5.cloned.1.call-update
  466.3 17.9 %reduce-scatter.5.cloned.1.call-done = f32[256,32]{0,1:T(8,128)} async-done(((f32[256,128]{0,1:T(8,128)}), f32[256,32]{0,1:T(8,128)}) %reduce-scatter.5.cloned.1.call-update) | async-done | bytes 32784 | tf_op jit(solution)/shard_map/reduce_scatter | solution.py:56
  484.2 0.0 copy-done.1
  (1 shorter events, 0.0 us)
Async XLA Ops:
  6.5 186.9 %copy-start = (s32[16,2048]{1,0:T(8,128)S(1)}, s32[16,2048]{1,0:T(8,128)}, u32[]{:S(2)}) copy-start(s32[16,2048]{1,0:T(8,128)} %param.7) | copy-start | bytes 393220
  6.5 182.2 %reduce-scatter.3.cloned.1.call-start = ((), (), s32[]{:S(2)}) async-start(), calls=%async_computation.2 | async-start | bytes 20971520 | tf_op jit(solution)/shard_map/reduce_scatter | solution.py:35
  59.7 133.8 %copy-start.3 = (s32[1024,256]{1,0:T(8,128)S(1)}, s32[1024,256]{1,0:T(8,128)}, u32[]{:S(2)}) copy-start(s32[1024,256]{1,0:T(8,128)} %param.9) | copy-start | bytes 3145732
  59.7 133.9 %copy-start.2 = (s32[1024,256]{1,0:T(8,128)S(1)}, s32[1024,256]{1,0:T(8,128)}, u32[]{:S(2)}) copy-start(s32[1024,256]{1,0:T(8,128)} %param.8) | copy-start | bytes 3145732
  59.8 361.2 %all-gather.2.cloned.1.call-start = ((), (), s32[]{:S(2)}) async-start(), calls=%async_computation.3 | async-start | bytes 18874368 | tf_op jit(solution)/shard_map/all_gather | solution.py:52
  193.2 291.0 %reduce-scatter.5.cloned.1.call-start = ((), (), s32[]{:S(2)}) async-start(), calls=%async_computation.4 | async-start | bytes 163840 | tf_op jit(solution)/shard_map/reduce_scatter | solution.py:56
  447.6 36.6 %copy-start.1 = (s32[16,2048]{1,0:T(8,128)S(1)}, s32[16,2048]{1,0:T(8,128)}, u32[]{:S(2)}) copy-start(s32[16,2048]{1,0:T(8,128)} %param.7) | copy-start | bytes 393220
Sparse Core Ops, SparseCore 0:
  59.9 128.8 reduce-scatter.2
  193.4 227.5 all-gather.1
  466.4 17.7 reduce-scatter.4
where the time goes:
time: 493 us; the launch traced here: 491 us
  waiting for transfers between devices  299 us (61%)
  local copies, waits for them, and re-layouts  106 us (22%)
  matrix products  40.9 us (8%)
  other arithmetic  31.8 us (6%)
  between operations  13.2 us (3%)
    all_gather x1, waiting for transfers between devices, on_device(): lax.all_gather(decoded, 'img', axis=1, tiled=True).reshape(-1, L)  152 us
    reduce_scatter x1, waiting for transfers between devices, on_device(): lax.psum_scatter(lax.dot_general(sign_rows, flat, (((0,), (0,)), ((), ())...  129 us
    select_n x1, local copies, waits for them, and re-layouts, weights_for(): jnp.where(chosen, mask_rows.T[:, None, :, None].astype(jnp.bfloat16), jnp...  46.3 us
    unnamed x10, local copies, waits for them, and re-layouts  33 us
    reshape x1, local copies, waits for them, and re-layouts, on_device(): lax.all_gather(decoded, 'img', axis=1, tiled=True).reshape(-1, L)  26.6 us
    dot_general x1, matrix products, on_device(): lax.dot_general(sign_rows, flat, (((0,), (0,)), ((), ())), preferred_elem...  22.2 us
    select_n x1, other arithmetic, weights_for(): jnp.where(chosen, mask_rows.T[:, None, :, None].astype(jnp.bfloat16), jnp...  21.3 us
    dot_general x1, matrix products, on_device(): jnp.dot(weight, lax.all_gather(decoded, 'img', axis=1, tiled=True).reshap...  18.7 us
  transfers between devices with their start and end apart: 3, of which 3 were waited for; matrix products, arithmetic and copies ran while one was open for 15% of the time, Pallas kernels for 0%

commit v1 on v0

v1 whole, which is shorter than its diff:
```python
import functools
import math

import jax
import jax.numpy as jnp
from jax import lax
from jax.experimental import pallas as pl
from jax.experimental.pallas import tpu as pltpu
from jax.sharding import PartitionSpec as P

L = 128
G = 8
RB = 16


def decode_kernel(st_ref, enc_ref, delta_ref, dsum_ref, sk_ref, x_ref):
    transmits, events = st_ref.shape
    samples = enc_ref.shape[2]
    rows, depth = sk_ref.shape
    width = 256 // G

    @pl.when(pl.program_id(0) == 0)
    def _():
        up = (
            lax.broadcasted_iota(jnp.int32, (rows, transmits), 0) // G
            == lax.broadcasted_iota(jnp.int32, (rows, transmits), 1)
        )
        tall = jnp.dot(
            up.astype(jnp.float32).astype(jnp.bfloat16),
            st_ref[...],
            preferred_element_type=jnp.float32,
        ).astype(jnp.bfloat16)
        step = 512
        for at in range(0, depth, step):
            out = (
                lax.broadcasted_iota(jnp.int32, (events, step), 1) + at
            ) // G == lax.broadcasted_iota(jnp.int32, (events, step), 0)
            wide = jnp.dot(
                tall,
                out.astype(jnp.float32).astype(jnp.bfloat16),
                preferred_element_type=jnp.float32,
            )
            same = (
                lax.broadcasted_iota(jnp.int32, (rows, step), 0) % G
                == lax.broadcasted_iota(jnp.int32, (rows, step), 1) % G
            )
            sk_ref[:, at : at + step] = jnp.where(same, wide, 0.0).astype(jnp.bfloat16)

    for at in range(0, events, width):
        piece = enc_ref[at : at + width].astype(jnp.float32)
        for half in range(RB // G):
            x_ref[half, at * G : (at + width) * G, :] = (
                piece[:, half * G : (half + 1) * G, :]
                .reshape(width * G, samples)
                .astype(jnp.bfloat16)
            )
    for half in range(RB // G):
        d = jnp.dot(sk_ref[...], x_ref[half], preferred_element_type=jnp.float32)
        low, high = d[:, : samples - L], d[:, L:]
        delta = (high - low) * 0.5
        mean = ((high + low) * 0.5).reshape(transmits, G, samples - L)
        here = slice(half * G, (half + 1) * G)
        delta_ref[:, here, :] = delta.reshape(transmits, G, samples - L).astype(
            delta_ref.dtype
        )
        dsum_ref[here, :] = jnp.sum(mean, axis=0)


def decode(st, encoded):
    transmits, events = st.shape
    _, receivers, samples = encoded.shape
    diff = samples - L
    return pl.pallas_call(
        decode_kernel,
        grid=(receivers // RB,),
        in_specs=[
            pl.BlockSpec((transmits, events), lambda g: (0, 0)),
            pl.BlockSpec((events, RB, samples), lambda g: (0, g, 0)),
        ],
        out_specs=[
            pl.BlockSpec((transmits, RB, diff), lambda g: (0, g, 0)),
            pl.BlockSpec((RB, diff), lambda g: (g, 0)),
        ],
        out_shape=[
            jax.ShapeDtypeStruct((transmits, receivers, diff), jnp.bfloat16),
            jax.ShapeDtypeStruct((receivers, diff), jnp.float32),
        ],
        scratch_shapes=[
            pltpu.VMEM((transmits * G, events * G), jnp.bfloat16),
            pltpu.VMEM((RB // G, events * G, samples), jnp.bfloat16),
        ],
        compiler_params=pltpu.CompilerParams(vmem_limit_bytes=50 * 2**20),
        cost_estimate=pl.CostEstimate(
            flops=2 * transmits * events * receivers * samples * G,
            bytes_accessed=events * receivers * samples * 2
            + transmits * receivers * diff * 2,
            transcendentals=0,
        ),
    )(st, encoded)


def beam_kernel(
    scale, at_once, mask_ref, tx_ref, delta_ref, dsum_ref, out_ref,
    a_ref, s_ref, acc_ref, rhs_ref,
):
    levels = delta_ref.shape[2] // L
    receivers = delta_ref.shape[1]
    groups, _, _, lines_here = mask_ref.shape
    lines = groups * lines_here
    step = pl.program_id(1)
    rows = 256

    @pl.when(step == 0)
    def _():
        for g in range(groups):
            rx = mask_ref[g, 0].astype(jnp.float32).T
            on = mask_ref[g, 1].astype(jnp.float32).T
            here = slice(g * lines_here, (g + 1) * lines_here)
            parts = [jnp.where(rx == v, on, 0.0) for v in range(levels)]
            a_ref[here, :] = jnp.concatenate(parts, axis=1).astype(jnp.bfloat16)
        for v in range(levels):
            whole = dsum_ref[:, v * L : (v + 1) * L]
            first = whole.astype(jnp.bfloat16)
            here = slice(v * receivers, (v + 1) * receivers)
            rhs_ref[0, here, :L] = first
            rhs_ref[0, here, L:] = (whole - first.astype(jnp.float32)).astype(
                jnp.bfloat16
            )
        for at in range(0, lines, rows):
            here = slice(at, at + rows)
            y = jnp.dot(a_ref[here, :], rhs_ref[0], preferred_element_type=jnp.float32)
            acc_ref[here, :] = y[:, :L] + y[:, L:]
            t = tx_ref[:, here].astype(jnp.float32)
            pad = jnp.zeros((L - t.shape[0], rows), jnp.float32)
            s = (2.0 * jnp.concatenate([t, pad], axis=0) - 1.0).T
            for g in range(s_ref.shape[0]):
                s_ref[g, here, :] = s if g == 0 else pltpu.roll(s, L - g * at_once, 1)

    for pair in range(at_once // 2):
        for side in range(2):
            for v in range(levels):
                rhs_ref[
                    pair, v * receivers : (v + 1) * receivers, side * L : (side + 1) * L
                ] = delta_ref[2 * pair + side, :, v * L : (v + 1) * L]
    for at in range(0, lines, rows):
        here = slice(at, at + rows)
        acc = acc_ref[here, :]
        for pair in range(at_once // 2):
            y = jnp.dot(a_ref[here, :], rhs_ref[pair], preferred_element_type=jnp.float32)
            k = 2 * pair
            acc = acc + s_ref[step, here, k : k + 1] * y[:, :L]
            acc = acc + s_ref[step, here, k + 1 : k + 2] * y[:, L:]
        acc_ref[here, :] = acc

    @pl.when(step == pl.num_programs(1) - 1)
    def _():
        stripes, _, deep, _ = out_ref.shape
        for g in range(groups):
            turned = (acc_ref[g * lines_here : (g + 1) * lines_here, :] * scale).T
            for t in range(stripes):
                out_ref[t, g] = turned[t * deep : (t + 1) * deep, :].astype(out_ref.dtype)


def beamform(scale, stripes, masks, tx_bits, delta, dsum):
    groups, _, receivers, lines_here = masks.shape
    transmits, lines = tx_bits.shape
    diff = delta.shape[2]
    levels = diff // L
    at_once = 8
    some = min(groups, 8)
    block = some * lines_here
    return pl.pallas_call(
        functools.partial(beam_kernel, scale, at_once),
        grid=(groups // some, transmits // at_once),
        in_specs=[
            pl.BlockSpec((some, 2, receivers, lines_here), lambda p, k: (p, 0, 0, 0)),
            pl.BlockSpec((transmits, block), lambda p, k: (0, p)),
            pl.BlockSpec((at_once, receivers, diff), lambda p, k: (k, 0, 0)),
            pl.BlockSpec((receivers, diff), lambda p, k: (0, 0)),
        ],
        out_specs=pl.BlockSpec(
            (stripes, some, L // stripes, lines_here), lambda p, k: (0, p, 0, 0)
        ),
        out_shape=jax.ShapeDtypeStruct(
            (stripes, groups, L // stripes, lines_here), jnp.bfloat16
        ),
        scratch_shapes=[
            pltpu.VMEM((block, levels * receivers), jnp.bfloat16),
            pltpu.VMEM((transmits // at_once, block, L), jnp.float32),
            pltpu.VMEM((block, L), jnp.float32),
            pltpu.VMEM((at_once // 2, levels * receivers, 2 * L), jnp.bfloat16),
        ],
        compiler_params=pltpu.CompilerParams(vmem_limit_bytes=50 * 2**20),
        cost_estimate=pl.CostEstimate(
            flops=2 * transmits * levels * receivers * lines * L,
            bytes_accessed=transmits * receivers * diff * 2,
            transcendentals=0,
        ),
    )(masks, tx_bits, delta, dsum)


def on_device(sizes, encoded, signs, tx_block, rx_block, apodization):
    events_here, receivers_here, samples = encoded.shape
    lines_here = rx_block.shape[1]
    stripes, groups = sizes
    events, transmits = signs.shape
    receivers = rx_block.shape[0]
    st = lax.dynamic_slice_in_dim(
        signs.T, lax.axis_index("tx") * events_here, events_here, 1
    ).astype(jnp.bfloat16)
    split = (groups, receivers_here, lines_here)
    masks = jnp.stack(
        [rx_block.reshape(split), apodization.reshape(split)], axis=1
    ).astype(jnp.bfloat16)
    masks = lax.all_to_all(masks, "img", 0, 0, tiled=True)
    tx_bits = lax.all_gather(tx_block.astype(jnp.bfloat16), "tx", axis=0, tiled=True)
    delta, dsum = decode(st, encoded)
    scale = math.sqrt(events / (transmits * receivers)) / events
    parts = beamform(scale, stripes, masks, tx_bits, delta, dsum)
    deep = L // stripes
    parts = parts.reshape(stripes * groups, deep, lines_here)
    parts = lax.all_to_all(parts, ("tx", "img"), 0, 0, tiled=True)
    return jnp.sum(parts.astype(jnp.float32), axis=0).T


def solution(mesh):
    placed = (P("tx", "img", None), P(), P("tx", None), P(None, "img"), P(None, "img"))
    sizes = (mesh.shape["tx"], mesh.shape["img"])
    return jax.shard_map(
        functools.partial(on_device, sizes),
        mesh=mesh, in_specs=placed, out_specs=P("img", "tx"), check_vma=False,
    )
```

time: 493 us -> 89.2 us (0.18)
  waiting for transfers between devices: 299 us -> 0.01 us
  local copies, waits for them, and re-layouts: 106 us -> 0 us
  Pallas kernels: 0 us -> 47.2 us
  matrix products: 40.9 us -> 0 us
  blocking collectives: 0 us -> 28 us
  other arithmetic: 31.8 us -> 6.16 us
  between operations: 13.2 us -> 0.02 us
  starting transfers between devices: 0.27 us -> 7.28 us
    all_gather x1 -> x0, waiting for transfers between devices: 152 us -> none  [on_device(): lax.all_gather(decoded, 'img', axis=1, tiled=True).reshape(-1, L)]
    reduce_scatter x2 -> x0, waiting for transfers between devices: 147 us -> none  [the longest x1 129 us: on_device(): lax.psum_scatter(lax.dot_general(sign_rows, flat, (((0,), (0,)), ((), ())...]
    pallas_call x0 -> x2, Pallas kernels: none -> 47.2 us  [the longest x1 23.7 us: beamform(): pl.pallas_call(functools.partial(beam_kernel, scale, at_once), grid=(grou...]
    select_n x1 -> x0, local copies, waits for them, and re-layouts: 46.3 us -> none  [weights_for(): jnp.where(chosen, mask_rows.T[:, None, :, None].astype(jnp.bfloat16), jnp...]
    dot_general x2 -> x0, matrix products: 40.9 us -> none  [the longest x1 22.2 us: on_device(): lax.dot_general(sign_rows, flat, (((0,), (0,)), ((), ())), preferred_elem...]
    unnamed x10 -> x0, local copies, waits for them, and re-layouts: 33 us -> none
    reshape x1 -> x0, local copies, waits for them, and re-layouts: 26.6 us -> none  [on_device(): lax.all_gather(decoded, 'img', axis=1, tiled=True).reshape(-1, L)]
    all_to_all x0 -> x1, blocking collectives: none -> 22.2 us  [on_device(): parts = lax.all_to_all(parts, ('tx', 'img'), 0, 0, tiled=True)]
  transfers between devices with their start and end apart: 3 -> 1, of which waited for: 3 -> 0; matrix products, arithmetic and copies ran while one was open for 15% -> 2% of each run, Pallas kernels for 0% -> 27%
where the time goes in v1:
time: 89.2 us; the launch traced here: 88.6 us
  Pallas kernels  47.2 us (53%)
  blocking collectives  28 us (31%)
  starting transfers between devices  7.28 us (8%)
  other arithmetic  6.16 us (7%)
    pallas_call x1, Pallas kernels, beamform(): pl.pallas_call(functools.partial(beam_kernel, scale, at_once), grid=(grou...  23.7 us
    pallas_call x1, Pallas kernels, decode(): pl.pallas_call(decode_kernel, grid=(receivers // RB,), in_specs=[pl.Block...  23.5 us
    all_to_all x1, blocking collectives, on_device(): parts = lax.all_to_all(parts, ('tx', 'img'), 0, 0, tiled=True)  22.2 us
    all_to_all x1, starting transfers between devices, on_device(): masks = lax.all_to_all(masks, 'img', 0, 0, tiled=True)  7.28 us
    all_gather x1, blocking collectives, on_device(): lax.all_gather(tx_block.astype(jnp.bfloat16), 'tx', axis=0, tiled=True)  5.79 us
    another operation x2, other arithmetic  2.61 us
  transfers between devices with their start and end apart: 1, of which 0 were waited for; matrix products, arithmetic and copies ran while one was open for 2% of the time, Pallas kernels for 27%

profile of v1, /device:TPU:0, one launch (start us, length us, event | category | flops | bytes accessed | tf_op | source)
XLA Modules:
  0.0 88.6 jit_solution(13679470117707024307)
XLA Ops:
  0.0 1.3 %convert.8 = bf16[1024,256]{1,0:T(8,128)(2,1)S(1)} convert(s32[1024,256]{1,0:T(8,128)} %param.8) | non-fusion elementwise | flops 262144 | bytes 1572864 | tf_op jit(solution)/shard_map/convert.3
  1.3 1.3 %convert.9 = bf16[1024,256]{1,0:T(8,128)(2,1)S(1)} convert(s32[1024,256]{1,0:T(8,128)} %param.9) | non-fusion elementwise | flops 262144 | bytes 1572864 | tf_op jit(solution)/shard_map/convert.2
  2.6 1.1 %pad_maximum_fusion = bf16[8,2,128,256]{3,2,1,0:T(8,128)(2,1)} fusion(bf16[8,1,128,256]{3,2,1,0:T(8,128)(2,1)S(1)} %bitcast.8, bf16[8,1,128,256]{3,2,1,0:T(8,128)(2,1)S(1)} %bitcast.7), kind=kLoop, calls=%fused_computation | loop fusion | flops 524288 | bytes 2097152 | tf_op jit(solution)/shard_map/stack | solution.py:212
  3.7 7.3 %all-to-all-start = ((bf16[8,2,128,256]{3,2,1,0:T(8,128)(2,1)}), bf16[8,2,128,256]{3,2,1,0:T(8,128)(2,1)S(1)}, u32[]{:S(2)}, u32[]{:S(2)}) async-start(bf16[8,2,128,256]{3,2,1,0:T(8,128)(2,1)} %pad_maximum_fusion), calls=%async_computation | async-start | bytes 2097152 | tf_op jit(solution)/shard_map/all_to_all | solution.py:215
  11.0 0.9 %convert_element_type.12 = bf16[16,2048]{1,0:T(8,128)(2,1)S(1)} convert(s32[16,2048]{1,0:T(8,128)} %param.7) | non-fusion elementwise | flops 32768 | bytes 196608 | tf_op jit(solution)/shard_map/convert_element_type | solution.py:216
  11.9 5.8 %all_gather.3.tx_ref = bf16[64,2048]{1,0:T(8,128)(2,1)S(1)} all-gather(bf16[16,2048]{1,0:T(8,128)(2,1)S(1)} %convert_element_type.12), channel_id=1, replica_groups=mesh['tx'=4,'img'=8] {'tx'}, dimensions={0}, use_global_device_ids=true | all-gather | bytes 327680 | tf_op jit(solution)/shard_map/all_gather | solution.py:216
  17.7 0.8 fusion.st_ref
  18.5 23.5 %shard_map.55 = (bf16[64,128,384]{2,1,0:T(8,128)(2,1)}, f32[128,384]{1,0:T(8,128)S(1)}) custom-call(bf16[64,256]{1,0:T(8,128)(2,1)S(1)} %fusion.st_ref, bf16[256,128,512]{2,1,0:T(8,128)(2,1)} %enc_ref.1), custom_call_target="tpu_custom_call" | custom-call | flops 17179869184 | bytes 39845888 | tf_op jit(solution)/shard_map/pallas_call | solution.py:73
  42.1 0.0 all-to-all-done.mask_ref
  42.1 23.7 %shard_map.56 = bf16[4,8,32,256]{3,2,1,0:T(8,128)(2,1)S(1)} custom-call(bf16[8,2,128,256]{3,2,1,0:T(8,128)(2,1)S(1)} %all-to-all-done.mask_ref, bf16[64,2048]{1,0:T(8,128)(2,1)S(1)} %all_gather.3.tx_ref, bf16[64,128,384]{2,1,0:T(8,128)(2,1)} %get-tuple-element.7.delta_ref, f32[128,384]{1,0:T(8,128)S(1)} %get-tuple-element.8.dsum_ref), custom_call_target="tpu_custom_call" | custom-call | flops 12884901888 | bytes 6291456 | tf_op jit(solution)/shard_map/pallas_call | solution.py:172
  65.8 22.2 %all_to_all.10 = bf16[32,32,256]{2,1,0:T(8,128)(2,1)S(1)} all-to-all(bf16[32,32,256]{2,1,0:T(8,128)(2,1)S(1)} %bitcast.6), channel_id=1, replica_groups=mesh['tx'=4,'img'=8] {'tx','img'}, dimensions={0} | all-to-all | bytes 1048576 | tf_op jit(solution)/shard_map/all_to_all | solution.py:222
  87.9 0.7 convert_reduce_fusion
Async XLA Ops:
  3.7 38.3 %all-to-all-start = ((bf16[8,2,128,256]{3,2,1,0:T(8,128)(2,1)}), bf16[8,2,128,256]{3,2,1,0:T(8,128)(2,1)S(1)}, u32[]{:S(2)}, u32[]{:S(2)}) async-start(bf16[8,2,128,256]{3,2,1,0:T(8,128)(2,1)} %pad_maximum_fusion), calls=%async_computation | async-start | bytes 2097152 | tf_op jit(solution)/shard_map/all_to_all | solution.py:215

commit v2 on v1

v2 whole, which is shorter than its diff:
```python
import functools
import math

import jax
import jax.numpy as jnp
from jax import lax
from jax.experimental import pallas as pl
from jax.experimental.pallas import tpu as pltpu
from jax.sharding import PartitionSpec as P

L = 128
G = 4
HALF = 8
RB = 16
BF = jnp.bfloat16
F32 = jnp.float32


def iota(shape, axis):
    return lax.broadcasted_iota(jnp.int32, shape, axis)


def dot(a, b):
    return jnp.dot(a, b, preferred_element_type=F32)


def cast_kernel(rx_ref, on_ref, tx_ref, out_ref, bits_ref):
    out_ref[0, 0] = rx_ref[...].astype(BF)
    out_ref[0, 1] = on_ref[...].astype(BF)

    @pl.when(pl.program_id(0) == 0)
    def _():
        bits_ref[...] = tx_ref[...].astype(BF)


def cast(groups, rx_block, apodization, tx_block):
    receivers, lines_here = rx_block.shape
    here = receivers // groups
    whole = pl.BlockSpec(tx_block.shape, lambda i: (0, 0))
    part = pl.BlockSpec((here, lines_here), lambda i: (i, 0))
    return pl.pallas_call(
        cast_kernel,
        grid=(groups,),
        in_specs=[part, part, whole],
        out_specs=[
            pl.BlockSpec((1, 2, here, lines_here), lambda i: (i, 0, 0, 0)),
            whole,
        ],
        out_shape=[
            jax.ShapeDtypeStruct((groups, 2, here, lines_here), BF),
            jax.ShapeDtypeStruct(tx_block.shape, BF),
        ],
    )(rx_block, apodization, tx_block)


def decode_kernel(
    stripes, at_ref, st_ref, enc_ref, delta_ref, dsum_ref, sk_ref, even_ref, odd_ref
):
    transmits, events = st_ref.shape
    samples = enc_ref.shape[2]
    rows, depth = sk_ref.shape
    step = pl.program_id(0)
    width = 32
    first = iota((1, HALF, samples), 1) < G

    @pl.when(step == 0)
    def _():
        turn = at_ref[0] * (transmits // stripes)
        up = lax.rem(iota((rows, transmits), 0) // G + turn, transmits)
        up = (up == iota((rows, transmits), 1)).astype(F32).astype(BF)
        tall = dot(up, st_ref[...].astype(F32).astype(BF)).astype(BF)
        wide = 512
        for at in range(0, depth, wide):
            out = (iota((events, wide), 1) + at) // G == iota((events, wide), 0)
            spread = dot(tall, out.astype(F32).astype(BF))
            same = iota((rows, wide), 0) % G == iota((rows, wide), 1) % G
            sk_ref[:, at : at + wide] = jnp.where(same, spread, 0.0).astype(BF)

    def lay_out(x_ref, half, at):
        piece = enc_ref[at : at + width].astype(F32)
        piece = piece[:, half * HALF : (half + 1) * HALF, :]
        piece = piece.reshape(width // 2, 2, HALF, samples)
        a, b = piece[:, 0], piece[:, 1]
        here = slice(at * G, (at + width) * G)
        low = jnp.where(first, a, pltpu.roll(b, G, 1))
        high = jnp.where(first, pltpu.roll(a, G, 1), b)
        x_ref[0, here, :] = low.reshape(width * G, samples).astype(BF)
        x_ref[1, here, :] = high.reshape(width * G, samples).astype(BF)

    def both(x_to, half, x_from):
        count = events // width
        pieces = []
        for c in range(count):
            lay_out(x_to, half, c * width)
            for q in range(4 * c // count, 4 * (c + 1) // count):
                n = slice((q // 2) * samples // 2, (q // 2 + 1) * samples // 2)
                pieces.append(dot(sk_ref[...], x_from[q % 2, :, n]))
        whole = []
        first_half = iota((1, HALF, samples // 2), 1) < G
        for low, high in ((pieces[0], pieces[1]), (pieces[2], pieces[3])):
            low = low.reshape(transmits // 2, HALF, samples // 2)
            high = high.reshape(transmits // 2, HALF, samples // 2)
            a = jnp.where(first_half, low, pltpu.roll(high, G, 1))
            b = jnp.where(first_half, pltpu.roll(low, G, 1), high)
            whole.append((a, b))
        blocks = [
            [side[..., n * L : (n + 1) * L] for n in range(samples // 2 // L)]
            for pair in whole
            for side in pair
        ]
        half_count = samples // 2 // L
        d = [
            [blocks[2 * (n // half_count) + odd][n % half_count] for odd in range(2)]
            for n in range(samples // L)
        ]
        for v in range(samples // L - 1):
            here = slice(v * L, (v + 1) * L)
            total = 0.0
            for odd in range(2):
                delta_ref[:, odd, :, here] = (d[v + 1][odd] - d[v][odd]) * 0.5
                total = total + jnp.sum(d[v + 1][odd] + d[v][odd], axis=0)
            dsum_ref[:, here] = total * 0.5

    @pl.when(step % 2 == 0)
    def _():
        both(even_ref, 0, odd_ref)

    @pl.when(step % 2 == 1)
    def _():
        both(odd_ref, 1, even_ref)


def decode(stripes, at, signs_t, encoded):
    transmits = signs_t.shape[0]
    events, receivers, samples = encoded.shape
    diff = samples - L
    steps = receivers // HALF
    blocks = receivers // RB
    shown = pltpu.PrefetchScalarGridSpec(
        num_scalar_prefetch=1,
        grid=(steps + 1,),
        in_specs=[
            pl.BlockSpec((transmits, events), lambda g, at: (0, at[0])),
            pl.BlockSpec(
                (events, RB, samples),
                lambda g, at: (0, jnp.minimum(g // (RB // HALF), blocks - 1), 0),
            ),
        ],
        out_specs=[
            pl.BlockSpec(
                (transmits // 2, 2, HALF, diff),
                lambda g, at: (0, 0, jnp.maximum(g - 1, 0), 0),
            ),
            pl.BlockSpec((HALF, diff), lambda g, at: (jnp.maximum(g - 1, 0), 0)),
        ],
        scratch_shapes=[
            pltpu.VMEM((transmits * G, events * G), BF),
            pltpu.VMEM((HALF // G, events * G, samples), BF),
            pltpu.VMEM((HALF // G, events * G, samples), BF),
        ],
    )
    return pl.pallas_call(
        functools.partial(decode_kernel, stripes),
        grid_spec=shown,
        out_shape=[
            jax.ShapeDtypeStruct((transmits // 2, 2, receivers, diff), F32),
            jax.ShapeDtypeStruct((receivers, diff), F32),
        ],
        compiler_params=pltpu.CompilerParams(vmem_limit_bytes=50 * 2**20),
        cost_estimate=pl.CostEstimate(
            flops=2 * transmits * events * receivers * samples * G,
            bytes_accessed=events * receivers * samples * 2
            + transmits * receivers * diff * 4,
            transcendentals=0,
        ),
    )(at, signs_t, encoded)


def beam_kernel(scale, at_once, mask_ref, delta_ref, dsum_ref, *refs):
    *tx_refs, out_ref, a_ref, s_ref, acc_ref, rhs_ref = refs
    levels = delta_ref.shape[3] // L
    receivers = delta_ref.shape[2]
    groups, _, _, lines_here = mask_ref.shape
    lines = groups * lines_here
    step = pl.program_id(1)
    rows = 256

    @pl.when(step == 0)
    def _():
        for v in range(levels):
            whole = dsum_ref[:, v * L : (v + 1) * L]
            high = whole.astype(BF)
            here = slice(v * receivers, (v + 1) * receivers)
            rhs_ref[0, here, :L] = high
            rhs_ref[0, here, L:] = (whole - high.astype(F32)).astype(BF)
        for g in range(groups):
            rx, on = mask_ref[g, 0].astype(F32), mask_ref[g, 1].astype(F32)
            code = (on * (rx + 1.0)).T
            here = slice(g * lines_here, (g + 1) * lines_here)
            parts = [jnp.where(code == v + 1, 1.0, 0.0) for v in range(levels)]
            a_ref[here, :] = jnp.concatenate(parts, axis=1).astype(BF)
        for at in range(0, lines, rows):
            here = slice(at, at + rows)
            y = dot(a_ref[here, :], rhs_ref[0])
            acc_ref[here, :] = y[:, :L] + y[:, L:]
            t = jnp.concatenate([ref[:, here].astype(F32) for ref in tx_refs], axis=0)
            pad = jnp.zeros((L - t.shape[0], rows), F32)
            s_ref[here, :] = (2.0 * jnp.concatenate([t, pad], axis=0) - 1.0).T

    for pair in range(at_once // 2):
        for side in range(2):
            for v in range(levels):
                rhs_ref[
                    pair, v * receivers : (v + 1) * receivers, side * L : (side + 1) * L
                ] = delta_ref[pair, side, :, v * L : (v + 1) * L].astype(BF)
    for at in range(0, lines, rows):
        here = slice(at, at + rows)
        acc = acc_ref[here, :]
        s = pltpu.roll(s_ref[here, :], L - step * at_once, 1)
        for pair in range(at_once // 2):
            y = dot(a_ref[here, :], rhs_ref[pair])
            k = 2 * pair
            acc = acc + s[:, k : k + 1] * y[:, :L]
            acc = acc + s[:, k + 1 : k + 2] * y[:, L:]
        acc_ref[here, :] = acc

    @pl.when(step == pl.num_programs(1) - 1)
    def _():
        stripes, _, deep, _ = out_ref.shape
        for g in range(groups):
            turned = (acc_ref[g * lines_here : (g + 1) * lines_here, :] * scale).T
            for t in range(stripes):
                out_ref[t, g] = turned[t * deep : (t + 1) * deep, :].astype(BF)


def beamform(scale, stripes, masks, tx_bits, delta, dsum):
    groups, _, receivers, lines_here = masks.shape
    pairs, _, _, diff = delta.shape
    levels = diff // L
    at_once = 8
    some = min(groups, 8)
    block = some * lines_here
    return pl.pallas_call(
        functools.partial(beam_kernel, scale, at_once),
        grid=(groups // some, 2 * pairs // at_once),
        in_specs=[
            pl.BlockSpec((some, 2, receivers, lines_here), lambda p, k: (p, 0, 0, 0)),
            pl.BlockSpec((at_once // 2, 2, receivers, diff), lambda p, k: (k, 0, 0, 0)),
            pl.BlockSpec((receivers, diff), lambda p, k: (0, 0)),
        ]
        + [pl.BlockSpec((t.shape[0], block), lambda p, k: (0, p)) for t in tx_bits],
        out_specs=pl.BlockSpec(
            (stripes, some, L // stripes, lines_here), lambda p, k: (0, p, 0, 0)
        ),
        out_shape=jax.ShapeDtypeStruct(
            (stripes, groups, L // stripes, lines_here), BF
        ),
        scratch_shapes=[
            pltpu.VMEM((block, levels * receivers), BF),
            pltpu.VMEM((block, L), F32),
            pltpu.VMEM((block, L), F32),
            pltpu.VMEM((at_once // 2, levels * receivers, 2 * L), BF),
        ],
        compiler_params=pltpu.CompilerParams(vmem_limit_bytes=50 * 2**20),
        cost_estimate=pl.CostEstimate(
            flops=4 * pairs * levels * receivers * groups * lines_here * L,
            bytes_accessed=2 * pairs * receivers * diff * 4,
            transcendentals=0,
        ),
    )(masks, delta, dsum, *tx_bits)


def on_device(sizes, encoded, signs, tx_block, rx_block, apodization):
    lines_here = rx_block.shape[1]
    stripes, groups = sizes
    events, transmits = signs.shape
    receivers = rx_block.shape[0]
    masks, own = cast(groups, rx_block, apodization, tx_block)
    masks = lax.all_to_all(masks, "img", 0, 0, tiled=True)
    tx_bits = [own] + [
        lax.ppermute(own, "tx", [((t + d) % stripes, t) for t in range(stripes)])
        for d in range(1, stripes)
    ]
    at = lax.axis_index("tx").astype(jnp.int32).reshape(1)
    delta, dsum = decode(stripes, at, signs.T, encoded)
    scale = math.sqrt(events / (transmits * receivers)) / events
    parts = beamform(scale, stripes, masks, tx_bits, delta, dsum)
    parts = parts.reshape(stripes * groups, L // stripes, lines_here)
    parts = lax.all_to_all(parts, ("tx", "img"), 0, 0, tiled=True)
    return jnp.sum(parts.astype(F32), axis=0).T


def solution(mesh):
    placed = (P("tx", "img", None), P(), P("tx", None), P(None, "img"), P(None, "img"))
    sizes = (mesh.shape["tx"], mesh.shape["img"])
    return jax.shard_map(
        functools.partial(on_device, sizes),
        mesh=mesh, in_specs=placed, out_specs=P("img", "tx"), check_vma=False,
    )
```

time: 89.2 us -> 116 us (1.30)
  Pallas kernels: 47.2 us -> 82.2 us
  blocking collectives: 28 us -> 21.2 us
  other arithmetic: 6.16 us -> 0.7 us
  starting transfers between devices: 7.28 us -> 10.4 us
    pallas_call x1 -> x2, Pallas kernels: 23.5 us -> 43 us  [the longest x1 37.4 us: decode(): pl.pallas_call(functools.partial(decode_kernel, stripes), grid_spec=shown...]
    pallas_call x1, Pallas kernels: 23.7 us -> 39.2 us  [beamform(): pl.pallas_call(functools.partial(beam_kernel, scale, at_once), grid=(grou...]
    all_gather x1 -> x0, blocking collectives: 5.79 us -> none  [on_device(): lax.all_gather(tx_block.astype(jnp.bfloat16), 'tx', axis=0, tiled=True)]
    another operation x3 -> x0, other arithmetic: 3.71 us -> none
    ppermute x0 -> x3, starting transfers between devices: none -> 2.95 us  [on_device(): lax.ppermute(own, 'tx', [((t + d) % stripes, t) for t in range(stripes)])]
    convert_element_type x2 -> x0, other arithmetic: 1.76 us -> none  [the longest x1 0.91 us: on_device(): tx_block.astype(jnp.bfloat16)]
  transfers between devices with their start and end apart: 1 -> 4, of which waited for: 0 -> 0; matrix products, arithmetic and copies ran while one was open for 2% -> 0% of each run, Pallas kernels for 27% -> 32%
where the time goes in v2:
time: 116 us
  Pallas kernels  82.2 us (71%)
  blocking collectives  21.2 us (18%)
  starting transfers between devices  10.4 us (9%)
    pallas_call x1, Pallas kernels, beamform(): pl.pallas_call(functools.partial(beam_kernel, scale, at_once), grid=(grou...  39.2 us
    pallas_call x1, Pallas kernels, decode(): pl.pallas_call(functools.partial(decode_kernel, stripes), grid_spec=shown...  37.4 us
    all_to_all x1, blocking collectives, on_device(): parts = lax.all_to_all(parts, ('tx', 'img'), 0, 0, tiled=True)  21.2 us
    all_to_all x1, starting transfers between devices, on_device(): masks = lax.all_to_all(masks, 'img', 0, 0, tiled=True)  7.42 us
    pallas_call x1, Pallas kernels, cast(): pl.pallas_call(cast_kernel, grid=(groups,), in_specs=[part, part, whole],...  5.6 us
    ppermute x3, starting transfers between devices, on_device(): lax.ppermute(own, 'tx', [((t + d) % stripes, t) for t in range(stripes)])  2.95 us
  transfers between devices with their start and end apart: 4, of which 0 were waited for; matrix products, arithmetic and copies ran while one was open for 0% of the time, Pallas kernels for 32%

profile of v2, /device:TPU:0, one launch (start us, length us, event | category | flops | bytes accessed | tf_op | source)
XLA Modules:
  0.0 115.5 jit_solution(15915745219579799800)
XLA Ops:
  0.0 5.6 %shard_map.55 = (bf16[8,2,128,256]{3,2,1,0:T(8,128)(2,1)}, bf16[16,2048]{1,0:T(8,128)(2,1)}) custom-call(s32[1024,256]{1,0:T(8,128)} %rx_ref.1, s32[1024,256]{1,0:T(8,128)} %on_ref.1, s32[16,2048]{1,0:T(8,128)} %tx_ref.1), custom_call_target="tpu_custom_call" | custom-call | tf_op jit(solution)/shard_map/pallas_call | solution.py:41
  5.6 0.0 copy-start.1
  5.6 7.4 %all-to-all-start = ((bf16[8,2,128,256]{3,2,1,0:T(8,128)(2,1)}), bf16[8,2,128,256]{3,2,1,0:T(8,128)(2,1)S(1)}, u32[]{:S(2)}, u32[]{:S(2)}) async-start(bf16[8,2,128,256]{3,2,1,0:T(8,128)(2,1)} %get-tuple-element.9), calls=%async_computation | async-start | bytes 2097152 | tf_op jit(solution)/shard_map/all_to_all | solution.py:279
  13.0 0.0 collective-permute-start.2
  13.0 1.6 %collective-permute-start.1 = (bf16[16,2048]{1,0:T(8,128)(2,1)}, bf16[16,2048]{1,0:T(8,128)(2,1)S(1)}, u32[]{:S(2)}, u32[]{:S(2)}) collective-permute-start(bf16[16,2048]{1,0:T(8,128)(2,1)} %get-tuple-element.12.refs_0_), channel_id=1, source_target_pairs={{16,0},{24,8},{0,16},{8,24},{17,1},{25,9},{1,17},{9,25},{18,2},{26... | collective-permute-start | bytes 196616 | tf_op jit(solution)/shard_map/ppermute | solution.py:281
  14.6 1.4 %collective-permute-start = (bf16[16,2048]{1,0:T(8,128)(2,1)}, bf16[16,2048]{1,0:T(8,128)(2,1)S(1)}, u32[]{:S(2)}, u32[]{:S(2)}) collective-permute-start(bf16[16,2048]{1,0:T(8,128)(2,1)} %get-tuple-element.12.refs_0_), channel_id=1, source_target_pairs={{8,0},{16,8},{24,16},{0,24},{9,1},{17,9},{25,17},{1,25},{10,2},{18... | collective-permute-start | bytes 196616 | tf_op jit(solution)/shard_map/ppermute | solution.py:281
  16.0 0.0 copy-start
  16.0 0.9 copy-done
  16.9 37.4 %shard_map.56 = (f32[32,2,128,384]{3,2,1,0:T(8,128)}, f32[128,384]{1,0:T(8,128)S(1)}) custom-call(s32[1]{0:T(128)} %bitcast.at_ref, s32[64,1024]{1,0:T(8,128)S(1)} %bitcast.5, bf16[256,128,512]{2,1,0:T(8,128)(2,1)} %enc_ref.1), custom_call_target="tpu_custom_call" | custom-call | flops 8589934592 | bytes 46137344 | tf_op jit(solution)/shard_map/pallas_call | solution.py:162
  54.3 0.0 collective-permute-done.2.refs_3_
  54.3 0.0 collective-permute-done.1.refs_2_
  54.3 0.0 collective-permute-done.refs_1_
  54.3 0.0 all-to-all-done.mask_ref
  54.4 0.0 copy-done.1
  54.4 39.2 %shard_map.57 = bf16[4,8,32,256]{3,2,1,0:T(8,128)(2,1)S(1)} custom-call(bf16[8,2,128,256]{3,2,1,0:T(8,128)(2,1)S(1)} %all-to-all-done.mask_ref, f32[32,2,128,384]{3,2,1,0:T(8,128)} %get-tuple-element.10.delta_ref, f32[128,384]{1,0:T(8,128)S(1)} %get-tuple-element.11.dsum_ref, bf16[16,2048]{1,0:T(8,128)(2,1)S(1)} %copy-done.1, ...), custom_call_target="tpu_custom_call" | custom-call | flops 12884901888 | bytes 12582912 | tf_op jit(solution)/shard_map/pallas_call | solution.py:243
  93.6 21.2 %all_to_all.10 = bf16[32,32,256]{2,1,0:T(8,128)(2,1)S(1)} all-to-all(bf16[32,32,256]{2,1,0:T(8,128)(2,1)S(1)} %bitcast.4), channel_id=1, replica_groups=mesh['tx'=4,'img'=8] {'tx','img'}, dimensions={0} | all-to-all | bytes 1048576 | tf_op jit(solution)/shard_map/all_to_all | solution.py:289
  114.8 0.7 convert_reduce_fusion
Async XLA Ops:
  5.6 48.8 %copy-start.1 = (bf16[16,2048]{1,0:T(8,128)(2,1)S(1)}, bf16[16,2048]{1,0:T(8,128)(2,1)}, u32[]{:S(2)}) copy-start(bf16[16,2048]{1,0:T(8,128)(2,1)} %get-tuple-element.12.refs_0_) | copy-start | bytes 196612
  5.6 48.8 %all-to-all-start = ((bf16[8,2,128,256]{3,2,1,0:T(8,128)(2,1)}), bf16[8,2,128,256]{3,2,1,0:T(8,128)(2,1)S(1)}, u32[]{:S(2)}, u32[]{:S(2)}) async-start(bf16[8,2,128,256]{3,2,1,0:T(8,128)(2,1)} %get-tuple-element.9), calls=%async_computation | async-start | bytes 2097152 | tf_op jit(solution)/shard_map/all_to_all | solution.py:279
  13.0 41.3 %collective-permute-start.2 = (bf16[16,2048]{1,0:T(8,128)(2,1)}, bf16[16,2048]{1,0:T(8,128)(2,1)S(1)}, u32[]{:S(2)}, u32[]{:S(2)}) collective-permute-start(bf16[16,2048]{1,0:T(8,128)(2,1)} %get-tuple-element.12.refs_0_), channel_id=1, source_target_pairs={{24,0},{0,8},{8,16},{16,24},{25,1},{1,9},{9,17},{17,25},{26,2},{2,... | collective-permute-start | bytes 196616 | tf_op jit(solution)/shard_map/ppermute | solution.py:281
  13.0 41.3 %collective-permute-start.1 = (bf16[16,2048]{1,0:T(8,128)(2,1)}, bf16[16,2048]{1,0:T(8,128)(2,1)S(1)}, u32[]{:S(2)}, u32[]{:S(2)}) collective-permute-start(bf16[16,2048]{1,0:T(8,128)(2,1)} %get-tuple-element.12.refs_0_), channel_id=1, source_target_pairs={{16,0},{24,8},{0,16},{8,24},{17,1},{25,9},{1,17},{9,25},{18,2},{26... | collective-permute-start | bytes 196616 | tf_op jit(solution)/shard_map/ppermute | solution.py:281
  14.6 39.8 %collective-permute-start = (bf16[16,2048]{1,0:T(8,128)(2,1)}, bf16[16,2048]{1,0:T(8,128)(2,1)S(1)}, u32[]{:S(2)}, u32[]{:S(2)}) collective-permute-start(bf16[16,2048]{1,0:T(8,128)(2,1)} %get-tuple-element.12.refs_0_), channel_id=1, source_target_pairs={{8,0},{16,8},{24,16},{0,24},{9,1},{17,9},{25,17},{1,25},{10,2},{18... | collective-permute-start | bytes 196616 | tf_op jit(solution)/shard_map/ppermute | solution.py:281
  16.0 0.9 copy-start

commit v3 on v2

v3 whole, which is shorter than its diff:
```python
import functools
import math

import jax
import jax.numpy as jnp
from jax import lax
from jax.experimental import pallas as pl
from jax.experimental.pallas import tpu as pltpu
from jax.sharding import PartitionSpec as P

L = 128
G = 8
RB = 16
BF = jnp.bfloat16
F32 = jnp.float32


def iota(shape, axis):
    return lax.broadcasted_iota(jnp.int32, shape, axis)


def dot(a, b):
    return jnp.dot(a, b, preferred_element_type=F32)


def cast_kernel(rx_ref, on_ref, tx_ref, out_ref, bits_ref):
    out_ref[:, 0] = rx_ref[...].astype(F32).astype(BF)
    out_ref[:, 1] = on_ref[...].astype(F32).astype(BF)

    @pl.when(pl.program_id(0) == 0)
    def _():
        bits_ref[...] = tx_ref[...].astype(F32).astype(BF)


def cast(groups, rx_block, apodization, tx_block):
    receivers, lines_here = rx_block.shape
    here = receivers // groups
    split = (groups, here, lines_here)
    whole = pl.BlockSpec(tx_block.shape, lambda i: (0, 0))
    part = pl.BlockSpec((groups // 2, here, lines_here), lambda i: (i, 0, 0))
    return pl.pallas_call(
        cast_kernel,
        grid=(2,),
        in_specs=[part, part, whole],
        out_specs=[
            pl.BlockSpec((groups // 2, 2, here, lines_here), lambda i: (i, 0, 0, 0)),
            whole,
        ],
        out_shape=[
            jax.ShapeDtypeStruct((groups, 2, here, lines_here), BF),
            jax.ShapeDtypeStruct(tx_block.shape, BF),
        ],
    )(rx_block.reshape(split), apodization.reshape(split), tx_block)


def decode_kernel(
    stripes, at_ref, st_ref, enc_ref, delta_ref, dsum_ref,
    sk_ref, even_ref, odd_ref, held_ref,
):
    transmits, events = st_ref.shape
    samples = enc_ref.shape[2]
    rows, depth = sk_ref.shape
    step, last = pl.program_id(0), pl.num_programs(0) - 1
    width = 32
    count = events // width
    levels = samples // L - 1

    def lay_out(x_ref, half, c):
        piece = enc_ref[c * width : (c + 1) * width].astype(F32)
        piece = piece[:, half * G : (half + 1) * G, :]
        here = slice(c * width * G, (c + 1) * width * G)
        x_ref[here, :] = piece.reshape(width * G, samples).astype(BF)

    def product(x_to, half, x_from):
        blocks = []
        for c in range(count):
            lay_out(x_to, half, c)
            for q in range(2 * c // count, 2 * (c + 1) // count):
                n = slice(q * samples // 2, (q + 1) * samples // 2)
                d = dot(sk_ref[...], x_from[:, n]).reshape(transmits, G, samples // 2)
                blocks += [d[..., at : at + L] for at in range(0, samples // 2, L)]
        delta = [(blocks[v + 1] - blocks[v]) * 0.5 for v in range(levels)]
        mean = [
            jnp.sum(blocks[v + 1] + blocks[v], axis=0) * 0.5 for v in range(levels)
        ]
        return delta, mean

    @pl.when(step == 0)
    def _():
        turn = at_ref[0] * (transmits // stripes)
        up = lax.rem(iota((rows, transmits), 0) // G + turn, transmits)
        up = (up == iota((rows, transmits), 1)).astype(F32).astype(BF)
        tall = dot(up, st_ref[...].astype(F32).astype(BF)).astype(BF)
        wide = 512
        for at in range(0, depth, wide):
            out = (iota((events, wide), 1) + at) // G == iota((events, wide), 0)
            spread = dot(tall, out.astype(F32).astype(BF))
            same = iota((rows, wide), 0) % G == iota((rows, wide), 1) % G
            sk_ref[:, at : at + wide] = jnp.where(same, spread, 0.0).astype(BF)
        for c in range(count):
            lay_out(even_ref, 0, c)

    @pl.when(step > 0)
    def _():
        delta, mean = product(even_ref, 0, odd_ref)
        for v in range(levels):
            here = slice(v * L, (v + 1) * L)
            delta_ref[:, :, here] = jnp.concatenate(
                [held_ref[:transmits, :, here], delta[v]], axis=1
            ).astype(BF)
            dsum_ref[:G, here] = held_ref[transmits, :, here]
            dsum_ref[G:, here] = mean[v]

    @pl.when(step < last)
    def _():
        delta, mean = product(odd_ref, 1, even_ref)
        for v in range(levels):
            here = slice(v * L, (v + 1) * L)
            held_ref[:transmits, :, here] = delta[v]
            held_ref[transmits, :, here] = mean[v]


def decode(stripes, at, signs_t, encoded):
    transmits = signs_t.shape[0]
    events, receivers, samples = encoded.shape
    diff = samples - L
    blocks = receivers // RB
    shown = pltpu.PrefetchScalarGridSpec(
        num_scalar_prefetch=1,
        grid=(blocks + 1,),
        in_specs=[
            pl.BlockSpec((transmits, events), lambda g, at: (0, at[0])),
            pl.BlockSpec(
                (events, RB, samples), lambda g, at: (0, jnp.minimum(g, blocks - 1), 0)
            ),
        ],
        out_specs=[
            pl.BlockSpec(
                (transmits, RB, diff), lambda g, at: (0, jnp.maximum(g - 1, 0), 0)
            ),
            pl.BlockSpec((RB, diff), lambda g, at: (jnp.maximum(g - 1, 0), 0)),
        ],
        scratch_shapes=[
            pltpu.VMEM((transmits * G, events * G), BF),
            pltpu.VMEM((events * G, samples), BF),
            pltpu.VMEM((events * G, samples), BF),
            pltpu.VMEM((transmits + 1, G, diff), F32),
        ],
    )
    return pl.pallas_call(
        functools.partial(decode_kernel, stripes),
        grid_spec=shown,
        out_shape=[
            jax.ShapeDtypeStruct((transmits, receivers, diff), BF),
            jax.ShapeDtypeStruct((receivers, diff), F32),
        ],
        compiler_params=pltpu.CompilerParams(vmem_limit_bytes=50 * 2**20),
        cost_estimate=pl.CostEstimate(
            flops=2 * transmits * events * receivers * samples * G,
            bytes_accessed=events * receivers * samples * 2
            + transmits * receivers * diff * 2,
            transcendentals=0,
        ),
    )(at, signs_t, encoded)


def beam_kernel(scale, mask_ref, delta_ref, dsum_ref, *refs):
    *tx_refs, out_ref, a_ref, s_ref, acc_ref, even_ref, odd_ref = refs
    block, receivers, diff = delta_ref.shape
    levels = diff // L
    half = block // 2
    groups, _, _, wide = mask_ref.shape
    step, last = pl.program_id(1), pl.num_programs(1) - 1

    def turn(x_to, side, k):
        for v in range(levels):
            x_to[k * L : (k + 1) * L, v * receivers : (v + 1) * receivers] = delta_ref[
                side * half + k, :, v * L : (v + 1) * L
            ].T

    def product(x_from, k0, beside):
        for g in range(groups):
            for k in range(g * half // groups, (g + 1) * half // groups):
                beside(k)
            here = slice(g * wide, (g + 1) * wide)
            y = dot(x_from[...], a_ref[:, here]).reshape(half, L // 8, 8, wide)
            acc = acc_ref[:, :, here]
            for k in range(half):
                acc = acc + s_ref[k0 + k, :, here] * y[k]
            acc_ref[:, :, here] = acc

    @pl.when(step == 0)
    def _():
        for v in range(levels):
            whole = dsum_ref[:, v * L : (v + 1) * L]
            high = whole.astype(BF)
            here = slice(v * receivers, (v + 1) * receivers)
            odd_ref[:L, here] = high.T
            odd_ref[L : 2 * L, here] = (whole - high.astype(F32)).astype(BF).T
        for g in range(groups):
            here = slice(g * wide, (g + 1) * wide)
            rx, on = mask_ref[g, 0].astype(F32), mask_ref[g, 1].astype(F32)
            for v in range(levels):
                a_ref[v * receivers : (v + 1) * receivers, here] = jnp.where(
                    rx == v, on, 0.0
                ).astype(BF)
            y = dot(odd_ref[: 2 * L, :], a_ref[:, here])
            acc_ref[:, :, here] = (y[:L] + y[L:]).reshape(L // 8, 8, wide)
            at = 0
            for ref in tx_refs:
                s = 2.0 * ref[:, here].astype(F32) - 1.0
                for k in range(ref.shape[0]):
                    s_ref[at + k, :, here] = jnp.broadcast_to(s[k : k + 1], (8, wide))
                at += ref.shape[0]
        for k in range(half):
            turn(even_ref, 0, k)

    @pl.when(step > 0)
    def _():
        product(odd_ref, step * block - half, functools.partial(turn, even_ref, 0))

    @pl.when(step < last)
    def _():
        product(even_ref, step * block, functools.partial(turn, odd_ref, 1))

    @pl.when(step == last)
    def _():
        stripes, _, deep, _ = out_ref.shape
        for g in range(groups):
            here = slice(g * wide, (g + 1) * wide)
            whole = (acc_ref[:, :, here] * scale).reshape(L, wide)
            for t in range(stripes):
                out_ref[t, g] = whole[t * deep : (t + 1) * deep, :].astype(BF)


def beamform(scale, stripes, masks, tx_bits, delta, dsum):
    groups, _, receivers, wide = masks.shape
    transmits, _, diff = delta.shape
    levels = diff // L
    block = 16
    some = min(groups, 8)
    steps = transmits // block
    return pl.pallas_call(
        functools.partial(beam_kernel, scale),
        grid=(groups // some, steps + 1),
        in_specs=[
            pl.BlockSpec((some, 2, receivers, wide), lambda p, k: (p, 0, 0, 0)),
            pl.BlockSpec(
                (block, receivers, diff), lambda p, k: (jnp.minimum(k, steps - 1), 0, 0)
            ),
            pl.BlockSpec((receivers, diff), lambda p, k: (0, 0)),
        ]
        + [
            pl.BlockSpec((t.shape[0], some * wide), lambda p, k: (0, p))
            for t in tx_bits
        ],
        out_specs=pl.BlockSpec(
            (stripes, some, L // stripes, wide), lambda p, k: (0, p, 0, 0)
        ),
        out_shape=jax.ShapeDtypeStruct((stripes, groups, L // stripes, wide), BF),
        scratch_shapes=[
            pltpu.VMEM((levels * receivers, some * wide), BF),
            pltpu.VMEM((transmits, 8, some * wide), F32),
            pltpu.VMEM((L // 8, 8, some * wide), F32),
            pltpu.VMEM((block // 2 * L, levels * receivers), BF),
            pltpu.VMEM((block // 2 * L, levels * receivers), BF),
        ],
        compiler_params=pltpu.CompilerParams(vmem_limit_bytes=50 * 2**20),
        cost_estimate=pl.CostEstimate(
            flops=2 * transmits * levels * receivers * groups * wide * L,
            bytes_accessed=transmits * receivers * diff * 2,
            transcendentals=0,
        ),
    )(masks, delta, dsum, *tx_bits)


def on_device(sizes, encoded, signs, tx_block, rx_block, apodization):
    lines_here = rx_block.shape[1]
    stripes, groups = sizes
    events, transmits = signs.shape
    receivers = rx_block.shape[0]
    masks, own = cast(groups, rx_block, apodization, tx_block)
    masks = lax.all_to_all(masks, "img", 0, 0, tiled=True)
    tx_bits = [own] + [
        lax.ppermute(own, "tx", [((t + d) % stripes, t) for t in range(stripes)])
        for d in range(1, stripes)
    ]
    at = lax.axis_index("tx").astype(jnp.int32).reshape(1)
    delta, dsum = decode(stripes, at, signs.T, encoded)
    scale = math.sqrt(events / (transmits * receivers)) / events
    parts = beamform(scale, stripes, masks, tx_bits, delta, dsum)
    parts = parts.reshape(stripes * groups, L // stripes, lines_here)
    parts = lax.all_to_all(parts, ("tx", "img"), 0, 0, tiled=True)
    return jnp.sum(parts.astype(F32), axis=0).T


def solution(mesh):
    placed = (P("tx", "img", None), P(), P("tx", None), P(None, "img"), P(None, "img"))
    sizes = (mesh.shape["tx"], mesh.shape["img"])
    return jax.shard_map(
        functools.partial(on_device, sizes),
        mesh=mesh, in_specs=placed, out_specs=P("img", "tx"), check_vma=False,
    )
```

time: 116 us -> 84.5 us (0.73)
  Pallas kernels: 82.2 us -> 50.9 us
    pallas_call x2, Pallas kernels: 44.8 us -> 23.9 us  [the longest x1 21.5 us: beamform(): pl.pallas_call(functools.partial(beam_kernel, scale), grid=(groups // som...]
    pallas_call x1, Pallas kernels: 37.4 us -> 27 us  [decode(): pl.pallas_call(functools.partial(decode_kernel, stripes), grid_spec=shown...]
where the time goes in v3:
time: 84.5 us; the launch traced here: 84.2 us
  Pallas kernels  50.9 us (60%)
  blocking collectives  21.2 us (25%)
  starting transfers between devices  10.4 us (12%)
  local copies, waits for them, and re-layouts  0.95 us (1%)
    pallas_call x1, Pallas kernels, decode(): pl.pallas_call(functools.partial(decode_kernel, stripes), grid_spec=shown...  27 us
    pallas_call x1, Pallas kernels, beamform(): pl.pallas_call(functools.partial(beam_kernel, scale), grid=(groups // som...  21.5 us
    all_to_all x1, blocking collectives, on_device(): parts = lax.all_to_all(parts, ('tx', 'img'), 0, 0, tiled=True)  21.2 us
    all_to_all x1, starting transfers between devices, on_device(): masks = lax.all_to_all(masks, 'img', 0, 0, tiled=True)  7.42 us
    ppermute x3, starting transfers between devices, on_device(): lax.ppermute(own, 'tx', [((t + d) % stripes, t) for t in range(stripes)])  2.95 us
    pallas_call x1, Pallas kernels, cast(): pl.pallas_call(cast_kernel, grid=(2,), in_specs=[part, part, whole], out_...  2.44 us
  transfers between devices with their start and end apart: 4, of which 0 were waited for; matrix products, arithmetic and copies ran while one was open for 0% of the time, Pallas kernels for 32%

profile of v3, /device:TPU:0, one launch (start us, length us, event | category | flops | bytes accessed | tf_op | source)
XLA Modules:
  0.0 84.2 jit_solution(2566728653466745318)
XLA Ops:
  0.0 2.4 %shard_map.55 = (bf16[8,2,128,256]{3,2,1,0:T(8,128)(2,1)}, bf16[16,2048]{1,0:T(8,128)(2,1)}) custom-call(s32[8,128,256]{2,1,0:T(8,128)} %bitcast.8, s32[8,128,256]{2,1,0:T(8,128)} %bitcast.9, s32[16,2048]{1,0:T(8,128)} %tx_ref.1), custom_call_target="tpu_custom_call" | custom-call | tf_op jit(solution)/shard_map/pallas_call | solution.py:41
  2.4 0.0 copy-start.1
  2.4 7.4 %all-to-all-start = ((bf16[8,2,128,256]{3,2,1,0:T(8,128)(2,1)}), bf16[8,2,128,256]{3,2,1,0:T(8,128)(2,1)S(1)}, u32[]{:S(2)}, u32[]{:S(2)}) async-start(bf16[8,2,128,256]{3,2,1,0:T(8,128)(2,1)} %get-tuple-element.9), calls=%async_computation | async-start | bytes 2097152 | tf_op jit(solution)/shard_map/all_to_all | solution.py:283
  9.9 0.0 collective-permute-start.2
  9.9 1.6 %collective-permute-start.1 = (bf16[16,2048]{1,0:T(8,128)(2,1)}, bf16[16,2048]{1,0:T(8,128)(2,1)S(1)}, u32[]{:S(2)}, u32[]{:S(2)}) collective-permute-start(bf16[16,2048]{1,0:T(8,128)(2,1)} %get-tuple-element.12.refs_0_), channel_id=1, source_target_pairs={{16,0},{24,8},{0,16},{8,24},{17,1},{25,9},{1,17},{9,25},{18,2},{26... | collective-permute-start | bytes 196616 | tf_op jit(solution)/shard_map/ppermute | solution.py:285
  11.4 1.4 %collective-permute-start = (bf16[16,2048]{1,0:T(8,128)(2,1)}, bf16[16,2048]{1,0:T(8,128)(2,1)S(1)}, u32[]{:S(2)}, u32[]{:S(2)}) collective-permute-start(bf16[16,2048]{1,0:T(8,128)(2,1)} %get-tuple-element.12.refs_0_), channel_id=1, source_target_pairs={{8,0},{16,8},{24,16},{0,24},{9,1},{17,9},{25,17},{1,25},{10,2},{18... | collective-permute-start | bytes 196616 | tf_op jit(solution)/shard_map/ppermute | solution.py:285
  12.8 0.0 copy-start
  12.8 0.9 %copy-done = s32[1024,64]{0,1:T(8,128)S(1)} copy-done((s32[1024,64]{0,1:T(8,128)S(1)}, s32[1024,64]{0,1:T(8,128)}, u32[]{:S(2)}) %copy-start) | copy-done | bytes 262168
  13.8 27.0 %shard_map.56 = (bf16[64,128,384]{2,1,0:T(8,128)(2,1)}, f32[128,384]{1,0:T(8,128)S(1)}) custom-call(s32[1]{0:T(128)} %bitcast.2.at_ref, s32[64,1024]{1,0:T(8,128)S(1)} %bitcast.7, bf16[256,128,512]{2,1,0:T(8,128)(2,1)} %enc_ref.1), custom_call_target="tpu_custom_call" | custom-call | flops 17179869184 | bytes 39845888 | tf_op jit(solution)/shard_map/pallas_call | solution.py:150
  40.7 0.0 collective-permute-done.2.refs_3_
  40.7 0.0 collective-permute-done.1.refs_2_
  40.8 0.0 collective-permute-done.refs_1_
  40.8 0.0 all-to-all-done.mask_ref
  40.8 0.0 copy-done.1
  40.8 21.5 %shard_map.57 = bf16[4,8,32,256]{3,2,1,0:T(8,128)(2,1)S(1)} custom-call(bf16[8,2,128,256]{3,2,1,0:T(8,128)(2,1)S(1)} %all-to-all-done.mask_ref, bf16[64,128,384]{2,1,0:T(8,128)(2,1)} %get-tuple-element.10.delta_ref, f32[128,384]{1,0:T(8,128)S(1)} %get-tuple-element.11.dsum_ref, bf16[16,2048]{1,0:T(8,128)(2,1)S(1)} %copy-done.1, ...), custom_call_target="tpu_custom_call" | custom-call | flops 12884901888 | bytes 6291456 | tf_op jit(solution)/shard_map/pallas_call | solution.py:243
  62.3 21.2 %all_to_all.10 = bf16[32,32,256]{2,1,0:T(8,128)(2,1)S(1)} all-to-all(bf16[32,32,256]{2,1,0:T(8,128)(2,1)S(1)} %bitcast.6), channel_id=1, replica_groups=mesh['tx'=4,'img'=8] {'tx','img'}, dimensions={0} | all-to-all | bytes 1048576 | tf_op jit(solution)/shard_map/all_to_all | solution.py:293
  83.5 0.7 convert_reduce_fusion
Async XLA Ops:
  2.4 38.3 %copy-start.1 = (bf16[16,2048]{1,0:T(8,128)(2,1)S(1)}, bf16[16,2048]{1,0:T(8,128)(2,1)}, u32[]{:S(2)}) copy-start(bf16[16,2048]{1,0:T(8,128)(2,1)} %get-tuple-element.12.refs_0_) | copy-start | bytes 196612
  2.4 38.3 %all-to-all-start = ((bf16[8,2,128,256]{3,2,1,0:T(8,128)(2,1)}), bf16[8,2,128,256]{3,2,1,0:T(8,128)(2,1)S(1)}, u32[]{:S(2)}, u32[]{:S(2)}) async-start(bf16[8,2,128,256]{3,2,1,0:T(8,128)(2,1)} %get-tuple-element.9), calls=%async_computation | async-start | bytes 2097152 | tf_op jit(solution)/shard_map/all_to_all | solution.py:283
  9.9 30.9 %collective-permute-start.2 = (bf16[16,2048]{1,0:T(8,128)(2,1)}, bf16[16,2048]{1,0:T(8,128)(2,1)S(1)}, u32[]{:S(2)}, u32[]{:S(2)}) collective-permute-start(bf16[16,2048]{1,0:T(8,128)(2,1)} %get-tuple-element.12.refs_0_), channel_id=1, source_target_pairs={{24,0},{0,8},{8,16},{16,24},{25,1},{1,9},{9,17},{17,25},{26,2},{2,... | collective-permute-start | bytes 196616 | tf_op jit(solution)/shard_map/ppermute | solution.py:285
  9.9 30.9 %collective-permute-start.1 = (bf16[16,2048]{1,0:T(8,128)(2,1)}, bf16[16,2048]{1,0:T(8,128)(2,1)S(1)}, u32[]{:S(2)}, u32[]{:S(2)}) collective-permute-start(bf16[16,2048]{1,0:T(8,128)(2,1)} %get-tuple-element.12.refs_0_), channel_id=1, source_target_pairs={{16,0},{24,8},{0,16},{8,24},{17,1},{25,9},{1,17},{9,25},{18,2},{26... | collective-permute-start | bytes 196616 | tf_op jit(solution)/shard_map/ppermute | solution.py:285
  11.4 29.3 %collective-permute-start = (bf16[16,2048]{1,0:T(8,128)(2,1)}, bf16[16,2048]{1,0:T(8,128)(2,1)S(1)}, u32[]{:S(2)}, u32[]{:S(2)}) collective-permute-start(bf16[16,2048]{1,0:T(8,128)(2,1)} %get-tuple-element.12.refs_0_), channel_id=1, source_target_pairs={{8,0},{16,8},{24,16},{0,24},{9,1},{17,9},{25,17},{1,25},{10,2},{18... | collective-permute-start | bytes 196616 | tf_op jit(solution)/shard_map/ppermute | solution.py:285
  12.8 0.9 %copy-start = (s32[1024,64]{0,1:T(8,128)S(1)}, s32[1024,64]{0,1:T(8,128)}, u32[]{:S(2)}) copy-start(s32[1024,64]{0,1:T(8,128)} %param.6) | copy-start | bytes 786436

commit v4 on v3

--- a/solution.py
+++ b/solution.py
@@ -54,42 +54,20 @@
 
 
 def decode_kernel(
-    stripes, at_ref, st_ref, enc_ref, delta_ref, dsum_ref,
-    sk_ref, even_ref, odd_ref, held_ref,
+    stripes, at_ref, st_ref, enc_ref, delta_ref, dsum_ref, sk_ref, x_ref
 ):
-    transmits, events = st_ref.shape
+    transmits = delta_ref.shape[0]
+    every, events = st_ref.shape
     samples = enc_ref.shape[2]
     rows, depth = sk_ref.shape
-    step, last = pl.program_id(0), pl.num_programs(0) - 1
     width = 32
-    count = events // width
-    levels = samples // L - 1
-
-    def lay_out(x_ref, half, c):
-        piece = enc_ref[c * width : (c + 1) * width].astype(F32)
-        piece = piece[:, half * G : (half + 1) * G, :]
-        here = slice(c * width * G, (c + 1) * width * G)
-        x_ref[here, :] = piece.reshape(width * G, samples).astype(BF)
-
-    def product(x_to, half, x_from):
-        blocks = []
-        for c in range(count):
-            lay_out(x_to, half, c)
-            for q in range(2 * c // count, 2 * (c + 1) // count):
-                n = slice(q * samples // 2, (q + 1) * samples // 2)
-                d = dot(sk_ref[...], x_from[:, n]).reshape(transmits, G, samples // 2)
-                blocks += [d[..., at : at + L] for at in range(0, samples // 2, L)]
-        delta = [(blocks[v + 1] - blocks[v]) * 0.5 for v in range(levels)]
-        mean = [
-            jnp.sum(blocks[v + 1] + blocks[v], axis=0) * 0.5 for v in range(levels)
-        ]
-        return delta, mean
-
-    @pl.when(step == 0)
-    def _():
-        turn = at_ref[0] * (transmits // stripes)
-        up = lax.rem(iota((rows, transmits), 0) // G + turn, transmits)
-        up = (up == iota((rows, transmits), 1)).astype(F32).astype(BF)
+
+    @pl.when(pl.program_id(0) == 0)
+    def _():
+        group = every // stripes
+        row = iota((rows, every), 0) // G
+        wanted = lax.rem(at_ref[1] + 2 * (row // group), stripes) * group + row % group
+        up = (wanted == iota((rows, every), 1)).astype(F32).astype(BF)
         tall = dot(up, st_ref[...].astype(F32).astype(BF)).astype(BF)
         wide = 512
         for at in range(0, depth, wide):
@@ -97,76 +75,66 @@
             spread = dot(tall, out.astype(F32).astype(BF))
             same = iota((rows, wide), 0) % G == iota((rows, wide), 1) % G
             sk_ref[:, at : at + wide] = jnp.where(same, spread, 0.0).astype(BF)
-        for c in range(count):
-            lay_out(even_ref, 0, c)
-
-    @pl.when(step > 0)
-    def _():
-        delta, mean = product(even_ref, 0, odd_ref)
-        for v in range(levels):
-            here = slice(v * L, (v + 1) * L)
-            delta_ref[:, :, here] = jnp.concatenate(
-                [held_ref[:transmits, :, here], delta[v]], axis=1
-            ).astype(BF)
-            dsum_ref[:G, here] = held_ref[transmits, :, here]
-            dsum_ref[G:, here] = mean[v]
-
-    @pl.when(step < last)
-    def _():
-        delta, mean = product(odd_ref, 1, even_ref)
-        for v in range(levels):
-            here = slice(v * L, (v + 1) * L)
-            held_ref[:transmits, :, here] = delta[v]
-            held_ref[transmits, :, here] = mean[v]
-
-
-def decode(stripes, at, signs_t, encoded):
-    transmits = signs_t.shape[0]
+
+    for at in range(0, events, width):
+        piece = enc_ref[at : at + width].astype(F32)
+        for half in range(RB // G):
+            x_ref[half, at * G : (at + width) * G, :] = (
+                piece[:, half * G : (half + 1) * G, :]
+                .reshape(width * G, samples)
+                .astype(BF)
+            )
+    deltas = []
+    for half in range(RB // G):
+        d = dot(sk_ref[...], x_ref[half])
+        low, high = d[:, : samples - L], d[:, L:]
+        deltas.append(((high - low) * 0.5).reshape(transmits, G, samples - L))
+        mean = (high + low).reshape(transmits, G, samples - L)
+        dsum_ref[half * G : (half + 1) * G, :] = jnp.sum(mean, axis=0) * 0.5
+    delta_ref[...] = jnp.concatenate(deltas, axis=1).astype(delta_ref.dtype)
+
+
+def decode(stripes, kept, at, signs_t, encoded):
+    every = signs_t.shape[0]
+    transmits = every // 2
     events, receivers, samples = encoded.shape
     diff = samples - L
-    blocks = receivers // RB
     shown = pltpu.PrefetchScalarGridSpec(
         num_scalar_prefetch=1,
-        grid=(blocks + 1,),
+        grid=(receivers // RB,),
         in_specs=[
-            pl.BlockSpec((transmits, events), lambda g, at: (0, at[0])),
-            pl.BlockSpec(
-                (events, RB, samples), lambda g, at: (0, jnp.minimum(g, blocks - 1), 0)
-            ),
+            pl.BlockSpec((every, events), lambda g, at: (0, at[0])),
+            pl.BlockSpec((events, RB, samples), lambda g, at: (0, g, 0)),
         ],
         out_specs=[
-            pl.BlockSpec(
-                (transmits, RB, diff), lambda g, at: (0, jnp.maximum(g - 1, 0), 0)
-            ),
-            pl.BlockSpec((RB, diff), lambda g, at: (jnp.maximum(g - 1, 0), 0)),
+            pl.BlockSpec((transmits, RB, diff), lambda g, at: (0, g, 0)),
+            pl.BlockSpec((RB, diff), lambda g, at: (g, 0)),
         ],
         scratch_shapes=[
             pltpu.VMEM((transmits * G, events * G), BF),
-            pltpu.VMEM((events * G, samples), BF),
-            pltpu.VMEM((events * G, samples), BF),
-            pltpu.VMEM((transmits + 1, G, diff), F32),
+            pltpu.VMEM((RB // G, events * G, samples), BF),
         ],
     )
     return pl.pallas_call(
         functools.partial(decode_kernel, stripes),
         grid_spec=shown,
         out_shape=[
-            jax.ShapeDtypeStruct((transmits, receivers, diff), BF),
+            jax.ShapeDtypeStruct((transmits, receivers, diff), kept),
             jax.ShapeDtypeStruct((receivers, diff), F32),
         ],
         compiler_params=pltpu.CompilerParams(vmem_limit_bytes=50 * 2**20),
         cost_estimate=pl.CostEstimate(
             flops=2 * transmits * events * receivers * samples * G,
             bytes_accessed=events * receivers * samples * 2
-            + transmits * receivers * diff * 2,
+            + transmits * receivers * diff * 4,
             transcendentals=0,
         ),
     )(at, signs_t, encoded)
 
 
-def beam_kernel(scale, mask_ref, delta_ref, dsum_ref, *refs):
+def beam_kernel(scale, mask_ref, own_ref, other_ref, mean1_ref, mean2_ref, *refs):
     *tx_refs, out_ref, a_ref, s_ref, acc_ref, even_ref, odd_ref = refs
-    block, receivers, diff = delta_ref.shape
+    block, receivers, diff = own_ref.shape
     levels = diff // L
     half = block // 2
     groups, _, _, wide = mask_ref.shape
@@ -174,9 +142,13 @@
 
     def turn(x_to, side, k):
         for v in range(levels):
-            x_to[k * L : (k + 1) * L, v * receivers : (v + 1) * receivers] = delta_ref[
-                side * half + k, :, v * L : (v + 1) * L
-            ].T
+            here = slice(v * L, (v + 1) * L)
+            whole = own_ref[side * half + k, :, here] + other_ref[
+                side * half + k, :, here
+            ].astype(F32)
+            x_to[k * L : (k + 1) * L, v * receivers : (v + 1) * receivers] = (
+                whole.astype(BF).T
+            )
 
     def product(x_from, k0, beside):
         for g in range(groups):
@@ -192,7 +164,8 @@
     @pl.when(step == 0)
     def _():
         for v in range(levels):
-            whole = dsum_ref[:, v * L : (v + 1) * L]
+            here = slice(v * L, (v + 1) * L)
+            whole = mean1_ref[:, here] + mean2_ref[:, here]
             high = whole.astype(BF)
             here = slice(v * receivers, (v + 1) * receivers)
             odd_ref[:L, here] = high.T
@@ -233,22 +206,26 @@
                 out_ref[t, g] = whole[t * deep : (t + 1) * deep, :].astype(BF)
 
 
-def beamform(scale, stripes, masks, tx_bits, delta, dsum):
+def beamform(scale, stripes, masks, tx_bits, own, other, mean1, mean2):
     groups, _, receivers, wide = masks.shape
-    transmits, _, diff = delta.shape
+    transmits, _, diff = own.shape
     levels = diff // L
     block = 16
     some = min(groups, 8)
     steps = transmits // block
+    part = pl.BlockSpec(
+        (block, receivers, diff), lambda p, k: (jnp.minimum(k, steps - 1), 0, 0)
+    )
+    mean = pl.BlockSpec((receivers, diff), lambda p, k: (0, 0))
     return pl.pallas_call(
         functools.partial(beam_kernel, scale),
         grid=(groups // some, steps + 1),
         in_specs=[
             pl.BlockSpec((some, 2, receivers, wide), lambda p, k: (p, 0, 0, 0)),
-            pl.BlockSpec(
-                (block, receivers, diff), lambda p, k: (jnp.minimum(k, steps - 1), 0, 0)
-            ),
-            pl.BlockSpec((receivers, diff), lambda p, k: (0, 0)),
+            part,
+            part,
+            mean,
+            mean,
         ]
         + [
             pl.BlockSpec((t.shape[0], some * wide), lambda p, k: (0, p))
@@ -268,10 +245,10 @@
         compiler_params=pltpu.CompilerParams(vmem_limit_bytes=50 * 2**20),
         cost_estimate=pl.CostEstimate(
             flops=2 * transmits * levels * receivers * groups * wide * L,
-            bytes_accessed=transmits * receivers * diff * 2,
+            bytes_accessed=transmits * receivers * diff * 6,
             transcendentals=0,
         ),
-    )(masks, delta, dsum, *tx_bits)
+    )(masks, own, other, mean1, mean2, *tx_bits)
 
 
 def on_device(sizes, encoded, signs, tx_block, rx_block, apodization):
@@ -283,12 +260,16 @@
     masks = lax.all_to_all(masks, "img", 0, 0, tiled=True)
     tx_bits = [own] + [
         lax.ppermute(own, "tx", [((t + d) % stripes, t) for t in range(stripes)])
-        for d in range(1, stripes)
+        for d in range(2, stripes, 2)
     ]
-    at = lax.axis_index("tx").astype(jnp.int32).reshape(1)
-    delta, dsum = decode(stripes, at, signs.T, encoded)
+    t = lax.axis_index("tx").astype(jnp.int32)
+    pair = t + 1 - 2 * lax.rem(t, 2)
+    signs_t = signs.T
+    theirs, mean1 = decode(stripes, BF, jnp.stack([t, pair]), signs_t, encoded)
+    theirs = lax.ppermute(theirs, "tx", [(t, t ^ 1) for t in range(stripes)])
+    ours, mean2 = decode(stripes, F32, jnp.stack([t, t]), signs_t, encoded)
     scale = math.sqrt(events / (transmits * receivers)) / events
-    parts = beamform(scale, stripes, masks, tx_bits, delta, dsum)
+    parts = beamform(scale, stripes, masks, tx_bits, ours, theirs, mean1, mean2)
     parts = parts.reshape(stripes * groups, L // stripes, lines_here)
     parts = lax.all_to_all(parts, ("tx", "img"), 0, 0, tiled=True)
     return jnp.sum(parts.astype(F32), axis=0).T

time: 84.5 us -> 89.8 us (1.063)
  waiting for transfers between devices: 0.01 us -> 5.78 us
  Pallas kernels: 50.9 us -> 53.1 us
  starting transfers between devices: 10.4 us -> 8.79 us
  blocking collectives: 21.2 us -> 19.8 us
    pallas_call x1 -> x2, Pallas kernels: 27 us -> 37.5 us  [decode(): pl.pallas_call(functools.partial(decode_kernel, stripes), grid_spec=shown...]
    pallas_call x1, Pallas kernels: 21.5 us -> 13.1 us  [beamform(): pl.pallas_call(functools.partial(beam_kernel, scale), grid=(groups // som...]
    all_to_all x1, waiting for transfers between devices: 0.01 us -> 5.77 us  [on_device(): masks = lax.all_to_all(masks, 'img', 0, 0, tiled=True)]
    ppermute x3 -> x1, starting transfers between devices: 2.95 us -> 1.49 us  [on_device(): lax.ppermute(own, 'tx', [((t + d) % stripes, t) for t in range(stripes)])]
    all_to_all x1, blocking collectives: 21.2 us -> 19.8 us  [on_device(): parts = lax.all_to_all(parts, ('tx', 'img'), 0, 0, tiled=True)]
  transfers between devices with their start and end apart: 4 -> 3, of which waited for: 0 -> 1; matrix products, arithmetic and copies ran while one was open for 0% -> 0% of each run, Pallas kernels for 32% -> 24%
where the time goes in v4:
time: 89.8 us; the launch traced here: 89.2 us
  Pallas kernels  53.1 us (59%)
  blocking collectives  19.8 us (22%)
  starting transfers between devices  8.79 us (10%)
  waiting for transfers between devices  5.78 us (6%)
  local copies, waits for them, and re-layouts  0.96 us (1%)
    pallas_call x2, Pallas kernels, decode(): pl.pallas_call(functools.partial(decode_kernel, stripes), grid_spec=shown...  37.5 us
    all_to_all x1, blocking collectives, on_device(): parts = lax.all_to_all(parts, ('tx', 'img'), 0, 0, tiled=True)  19.8 us
    pallas_call x1, Pallas kernels, beamform(): pl.pallas_call(functools.partial(beam_kernel, scale), grid=(groups // som...  13.1 us
    all_to_all x1, starting transfers between devices, on_device(): masks = lax.all_to_all(masks, 'img', 0, 0, tiled=True)  6.85 us
    all_to_all x1, waiting for transfers between devices, on_device(): masks = lax.all_to_all(masks, 'img', 0, 0, tiled=True)  5.77 us
    pallas_call x1, Pallas kernels, cast(): pl.pallas_call(cast_kernel, grid=(2,), in_specs=[part, part, whole], out_...  2.47 us
  transfers between devices with their start and end apart: 3, of which 1 were waited for; matrix products, arithmetic and copies ran while one was open for 0% of the time, Pallas kernels for 24%

profile of v4, /device:TPU:0, one launch (start us, length us, event | category | flops | bytes accessed | tf_op | source)
XLA Modules:
  0.0 89.2 jit_solution(11465841898858508252)
XLA Ops:
  0.0 0.1 pad_add_fusion
  0.1 0.0 copy-start
  0.1 0.9 %copy-done = s32[1024,64]{0,1:T(8,128)S(1)} copy-done((s32[1024,64]{0,1:T(8,128)S(1)}, s32[1024,64]{0,1:T(8,128)}, u32[]{:S(2)}) %copy-start) | copy-done | bytes 262168
  1.0 0.0 copy-start.1
  1.0 18.4 %shard_map.57 = (bf16[32,128,384]{2,1,0:T(8,128)(2,1)}, f32[128,384]{1,0:T(8,128)S(1)}) custom-call(s32[2]{0:T(128)S(1)} %get-tuple-element.18.at_ref, s32[64,1024]{1,0:T(8,128)S(1)} %bitcast.7, bf16[256,128,512]{2,1,0:T(8,128)(2,1)} %enc_ref.3), custom_call_target="tpu_custom_call" | custom-call | flops 8589934592 | bytes 39845888 | tf_op jit(solution)/shard_map/pallas_call | solution.py:118
  19.4 0.5 collective-permute-start
  19.9 2.5 %shard_map.55 = (bf16[8,2,128,256]{3,2,1,0:T(8,128)(2,1)}, bf16[16,2048]{1,0:T(8,128)(2,1)}) custom-call(s32[8,128,256]{2,1,0:T(8,128)} %bitcast.10, s32[8,128,256]{2,1,0:T(8,128)} %bitcast.11, s32[16,2048]{1,0:T(8,128)} %tx_ref.1), custom_call_target="tpu_custom_call" | custom-call | tf_op jit(solution)/shard_map/pallas_call | solution.py:41
  22.3 6.9 %all-to-all-start = ((bf16[8,2,128,256]{3,2,1,0:T(8,128)(2,1)}), bf16[8,2,128,256]{3,2,1,0:T(8,128)(2,1)S(1)}, u32[]{:S(2)}, u32[]{:S(2)}) async-start(bf16[8,2,128,256]{3,2,1,0:T(8,128)(2,1)} %get-tuple-element.11), calls=%async_computation | async-start | bytes 2097152 | tf_op jit(solution)/shard_map/all_to_all | solution.py:260
  29.2 1.5 %collective-permute-start.1 = (bf16[16,2048]{1,0:T(8,128)(2,1)}, bf16[16,2048]{1,0:T(8,128)(2,1)S(1)}, u32[]{:S(2)}, u32[]{:S(2)}) collective-permute-start(bf16[16,2048]{1,0:T(8,128)(2,1)} %get-tuple-element.16.refs_0_), channel_id=1, source_target_pairs={{16,0},{24,8},{0,16},{8,24},{17,1},{25,9},{1,17},{9,25},{18,2},{26... | collective-permute-start | bytes 196616 | tf_op jit(solution)/shard_map/ppermute | solution.py:262
  30.7 0.0 copy-done.1
  30.7 0.0 copy-start.2
  30.7 19.2 %shard_map.56 = (f32[32,128,384]{2,1,0:T(8,128)}, f32[128,384]{1,0:T(8,128)S(1)}) custom-call(s32[2]{0:T(128)S(1)} %get-tuple-element.17.at_ref, s32[64,1024]{1,0:T(8,128)S(1)} %bitcast.8, bf16[256,128,512]{2,1,0:T(8,128)(2,1)} %enc_ref.3), custom_call_target="tpu_custom_call" | custom-call | flops 8589934592 | bytes 39845888 | tf_op jit(solution)/shard_map/pallas_call | solution.py:118
  49.8 0.0 collective-permute-done.1.refs_1_
  49.8 5.8 %all-to-all-done.mask_ref = bf16[8,2,128,256]{3,2,1,0:T(8,128)(2,1)S(1)} async-done(((bf16[8,2,128,256]{3,2,1,0:T(8,128)(2,1)}), bf16[8,2,128,256]{3,2,1,0:T(8,128)(2,1)S(1)}, u32[]{:S(2)}, u32[]{:S(2)}) %all-to-all-start) | async-done | bytes 1048608 | tf_op jit(solution)/shard_map/all_to_all | solution.py:260
  55.6 0.0 collective-permute-done.other_ref
  55.6 0.0 copy-done.2
  55.6 13.1 %shard_map.58 = bf16[4,8,32,256]{3,2,1,0:T(8,128)(2,1)S(1)} custom-call(bf16[8,2,128,256]{3,2,1,0:T(8,128)(2,1)S(1)} %all-to-all-done.mask_ref, f32[32,128,384]{2,1,0:T(8,128)} %get-tuple-element.12.own_ref, bf16[32,128,384]{2,1,0:T(8,128)(2,1)} %collective-permute-done.other_ref, f32[128,384]{1,0:T(8,128)S(1)} %get-tuple-element.14.mean1_ref, ...), custom_call_target="tpu_custom_call" | custom-call | flops 6442450944 | bytes 9437184 | tf_op jit(solution)/shard_map/pallas_call | solution.py:220
  68.7 19.8 %all_to_all.10 = bf16[32,32,256]{2,1,0:T(8,128)(2,1)S(1)} all-to-all(bf16[32,32,256]{2,1,0:T(8,128)(2,1)S(1)} %bitcast.9), channel_id=1, replica_groups=mesh['tx'=4,'img'=8] {'tx','img'}, dimensions={0} | all-to-all | bytes 1048576 | tf_op jit(solution)/shard_map/all_to_all | solution.py:274
  88.5 0.7 convert_reduce_fusion
Async XLA Ops:
  0.1 1.0 %copy-start = (s32[1024,64]{0,1:T(8,128)S(1)}, s32[1024,64]{0,1:T(8,128)}, u32[]{:S(2)}) copy-start(s32[1024,64]{0,1:T(8,128)} %param.6) | copy-start | bytes 786436
  1.0 29.7 %copy-start.1 = (s32[1024,64]{0,1:T(8,128)S(1)}, s32[1024,64]{0,1:T(8,128)}, u32[]{:S(2)}) copy-start(s32[1024,64]{0,1:T(8,128)} %param.6) | copy-start | bytes 786436
  19.4 36.2 %collective-permute-start = (bf16[32,128,384]{2,1,0:T(8,128)(2,1)}, bf16[32,128,384]{2,1,0:T(8,128)(2,1)}, u32[]{:S(2)}, u32[]{:S(2)}) collective-permute-start(bf16[32,128,384]{2,1,0:T(8,128)(2,1)} %get-tuple-element.13), channel_id=1, source_target_pairs={{0,8},{8,0},{16,24},{24,16},{1,9},{9,1},{17,25},{25,17},{2,10},{10... | collective-permute-start | bytes 9437192 | tf_op jit(solution)/shard_map/ppermute | solution.py:269
  22.3 33.3 %all-to-all-start = ((bf16[8,2,128,256]{3,2,1,0:T(8,128)(2,1)}), bf16[8,2,128,256]{3,2,1,0:T(8,128)(2,1)S(1)}, u32[]{:S(2)}, u32[]{:S(2)}) async-start(bf16[8,2,128,256]{3,2,1,0:T(8,128)(2,1)} %get-tuple-element.11), calls=%async_computation | async-start | bytes 2097152 | tf_op jit(solution)/shard_map/all_to_all | solution.py:260
  29.2 20.7 %collective-permute-start.1 = (bf16[16,2048]{1,0:T(8,128)(2,1)}, bf16[16,2048]{1,0:T(8,128)(2,1)S(1)}, u32[]{:S(2)}, u32[]{:S(2)}) collective-permute-start(bf16[16,2048]{1,0:T(8,128)(2,1)} %get-tuple-element.16.refs_0_), channel_id=1, source_target_pairs={{16,0},{24,8},{0,16},{8,24},{17,1},{25,9},{1,17},{9,25},{18,2},{26... | collective-permute-start | bytes 196616 | tf_op jit(solution)/shard_map/ppermute | solution.py:262
  30.7 24.9 %copy-start.2 = (bf16[16,2048]{1,0:T(8,128)(2,1)S(1)}, bf16[16,2048]{1,0:T(8,128)(2,1)}, u32[]{:S(2)}) copy-start(bf16[16,2048]{1,0:T(8,128)(2,1)} %get-tuple-element.16.refs_0_) | copy-start | bytes 196612

commit v5 on v3

--- a/solution.py
+++ b/solution.py
@@ -9,7 +9,7 @@
 from jax.sharding import PartitionSpec as P
 
 L = 128
-G = 8
+PITCH = 24
 RB = 16
 BF = jnp.bfloat16
 F32 = jnp.float32
@@ -23,145 +23,118 @@
     return jnp.dot(a, b, preferred_element_type=F32)
 
 
-def cast_kernel(rx_ref, on_ref, tx_ref, out_ref, bits_ref):
+def cast_kernel(
+    stripes, at_ref, rx_ref, on_ref, tx_ref, sign_ref, out_ref, bits_ref, st_ref
+):
     out_ref[:, 0] = rx_ref[...].astype(F32).astype(BF)
     out_ref[:, 1] = on_ref[...].astype(F32).astype(BF)
 
     @pl.when(pl.program_id(0) == 0)
     def _():
         bits_ref[...] = tx_ref[...].astype(F32).astype(BF)
-
-
-def cast(groups, rx_block, apodization, tx_block):
+        every = st_ref.shape[0]
+        turn = at_ref[0] * (every // stripes)
+        row = lax.rem(iota((every, every), 0) + turn, every)
+        up = (row == iota((every, every), 1)).astype(F32).astype(BF)
+        st_ref[...] = dot(up, sign_ref[...].astype(F32).astype(BF)).astype(BF)
+
+
+def cast(sizes, at, rx_block, apodization, tx_block, signs_t):
+    stripes, groups = sizes
     receivers, lines_here = rx_block.shape
+    every, events = signs_t.shape
     here = receivers // groups
     split = (groups, here, lines_here)
-    whole = pl.BlockSpec(tx_block.shape, lambda i: (0, 0))
-    part = pl.BlockSpec((groups // 2, here, lines_here), lambda i: (i, 0, 0))
+    whole = pl.BlockSpec(tx_block.shape, lambda i, at: (0, 0))
+    part = pl.BlockSpec((groups // 2, here, lines_here), lambda i, at: (i, 0, 0))
     return pl.pallas_call(
-        cast_kernel,
-        grid=(2,),
-        in_specs=[part, part, whole],
-        out_specs=[
-            pl.BlockSpec((groups // 2, 2, here, lines_here), lambda i: (i, 0, 0, 0)),
-            whole,
-        ],
+        functools.partial(cast_kernel, stripes),
+        grid_spec=pltpu.PrefetchScalarGridSpec(
+            num_scalar_prefetch=1,
+            grid=(2,),
+            in_specs=[
+                part,
+                part,
+                whole,
+                pl.BlockSpec((every, events // stripes), lambda i, at: (0, at[0])),
+            ],
+            out_specs=[
+                pl.BlockSpec(
+                    (groups // 2, 2, here, lines_here), lambda i, at: (i, 0, 0, 0)
+                ),
+                whole,
+                pl.BlockSpec((every, events // stripes), lambda i, at: (0, 0)),
+            ],
+        ),
         out_shape=[
             jax.ShapeDtypeStruct((groups, 2, here, lines_here), BF),
             jax.ShapeDtypeStruct(tx_block.shape, BF),
-        ],
-    )(rx_block.reshape(split), apodization.reshape(split), tx_block)
-
-
-def decode_kernel(
-    stripes, at_ref, st_ref, enc_ref, delta_ref, dsum_ref,
-    sk_ref, even_ref, odd_ref, held_ref,
-):
+            jax.ShapeDtypeStruct((every, events // stripes), BF),
+        ],
+    )(at, rx_block.reshape(split), apodization.reshape(split), tx_block, signs_t)
+
+
+def decode_kernel(st_ref, enc_ref, delta_ref, dsum_ref, rows_ref, turn_ref):
     transmits, events = st_ref.shape
     samples = enc_ref.shape[2]
-    rows, depth = sk_ref.shape
-    step, last = pl.program_id(0), pl.num_programs(0) - 1
-    width = 32
-    count = events // width
-    levels = samples // L - 1
-
-    def lay_out(x_ref, half, c):
-        piece = enc_ref[c * width : (c + 1) * width].astype(F32)
-        piece = piece[:, half * G : (half + 1) * G, :]
-        here = slice(c * width * G, (c + 1) * width * G)
-        x_ref[here, :] = piece.reshape(width * G, samples).astype(BF)
-
-    def product(x_to, half, x_from):
-        blocks = []
-        for c in range(count):
-            lay_out(x_to, half, c)
-            for q in range(2 * c // count, 2 * (c + 1) // count):
-                n = slice(q * samples // 2, (q + 1) * samples // 2)
-                d = dot(sk_ref[...], x_from[:, n]).reshape(transmits, G, samples // 2)
-                blocks += [d[..., at : at + L] for at in range(0, samples // 2, L)]
-        delta = [(blocks[v + 1] - blocks[v]) * 0.5 for v in range(levels)]
-        mean = [
-            jnp.sum(blocks[v + 1] + blocks[v], axis=0) * 0.5 for v in range(levels)
+    parts, levels = samples // L, samples // L - 1
+    for e in range(events):
+        piece = enc_ref[e].astype(F32)
+        for c in range(parts):
+            rows_ref[c, e * PITCH : e * PITCH + RB, :] = piece[:, c * L : (c + 1) * L]
+    for r in range(RB):
+        d = [
+            dot(
+                st_ref[...],
+                rows_ref[c, pl.ds(r, events, stride=PITCH), :].astype(BF),
+            )
+            for c in range(parts)
         ]
-        return delta, mean
-
-    @pl.when(step == 0)
-    def _():
-        turn = at_ref[0] * (transmits // stripes)
-        up = lax.rem(iota((rows, transmits), 0) // G + turn, transmits)
-        up = (up == iota((rows, transmits), 1)).astype(F32).astype(BF)
-        tall = dot(up, st_ref[...].astype(F32).astype(BF)).astype(BF)
-        wide = 512
-        for at in range(0, depth, wide):
-            out = (iota((events, wide), 1) + at) // G == iota((events, wide), 0)
-            spread = dot(tall, out.astype(F32).astype(BF))
-            same = iota((rows, wide), 0) % G == iota((rows, wide), 1) % G
-            sk_ref[:, at : at + wide] = jnp.where(same, spread, 0.0).astype(BF)
-        for c in range(count):
-            lay_out(even_ref, 0, c)
-
-    @pl.when(step > 0)
-    def _():
-        delta, mean = product(even_ref, 0, odd_ref)
-        for v in range(levels):
-            here = slice(v * L, (v + 1) * L)
-            delta_ref[:, :, here] = jnp.concatenate(
-                [held_ref[:transmits, :, here], delta[v]], axis=1
-            ).astype(BF)
-            dsum_ref[:G, here] = held_ref[transmits, :, here]
-            dsum_ref[G:, here] = mean[v]
-
-    @pl.when(step < last)
-    def _():
-        delta, mean = product(odd_ref, 1, even_ref)
-        for v in range(levels):
-            here = slice(v * L, (v + 1) * L)
-            held_ref[:transmits, :, here] = delta[v]
-            held_ref[transmits, :, here] = mean[v]
-
-
-def decode(stripes, at, signs_t, encoded):
-    transmits = signs_t.shape[0]
-    events, receivers, samples = encoded.shape
+        for v in range(levels):
+            turn_ref[v, r * transmits : (r + 1) * transmits, :] = (
+                d[v + 1] - d[v]
+            ) * 0.5
+            dsum_ref[r : r + 1, v * L : (v + 1) * L] = (
+                jnp.sum(d[v + 1] + d[v], axis=0, keepdims=True) * 0.5
+            )
+    for k in range(transmits):
+        for v in range(levels):
+            delta_ref[k, :, v * L : (v + 1) * L] = turn_ref[
+                v, pl.ds(k, RB, stride=transmits), :
+            ].astype(BF)
+
+
+def decode(st, encoded):
+    transmits, events = st.shape
+    _, receivers, samples = encoded.shape
     diff = samples - L
-    blocks = receivers // RB
-    shown = pltpu.PrefetchScalarGridSpec(
-        num_scalar_prefetch=1,
-        grid=(blocks + 1,),
+    return pl.pallas_call(
+        decode_kernel,
+        grid=(receivers // RB,),
         in_specs=[
-            pl.BlockSpec((transmits, events), lambda g, at: (0, at[0])),
-            pl.BlockSpec(
-                (events, RB, samples), lambda g, at: (0, jnp.minimum(g, blocks - 1), 0)
-            ),
+            pl.BlockSpec((transmits, events), lambda g: (0, 0)),
+            pl.BlockSpec((events, RB, samples), lambda g: (0, g, 0)),
         ],
         out_specs=[
-            pl.BlockSpec(
-                (transmits, RB, diff), lambda g, at: (0, jnp.maximum(g - 1, 0), 0)
-            ),
-            pl.BlockSpec((RB, diff), lambda g, at: (jnp.maximum(g - 1, 0), 0)),
-        ],
-        scratch_shapes=[
-            pltpu.VMEM((transmits * G, events * G), BF),
-            pltpu.VMEM((events * G, samples), BF),
-            pltpu.VMEM((events * G, samples), BF),
-            pltpu.VMEM((transmits + 1, G, diff), F32),
-        ],
-    )
-    return pl.pallas_call(
-        functools.partial(decode_kernel, stripes),
-        grid_spec=shown,
+            pl.BlockSpec((transmits, RB, diff), lambda g: (0, g, 0)),
+            pl.BlockSpec((RB, diff), lambda g: (g, 0)),
+        ],
         out_shape=[
             jax.ShapeDtypeStruct((transmits, receivers, diff), BF),
             jax.ShapeDtypeStruct((receivers, diff), F32),
         ],
+        scratch_shapes=[
+            pltpu.VMEM((samples // L, events * PITCH, L), F32),
+            pltpu.VMEM((diff // L, RB * transmits, L), F32),
+        ],
         compiler_params=pltpu.CompilerParams(vmem_limit_bytes=50 * 2**20),
         cost_estimate=pl.CostEstimate(
-            flops=2 * transmits * events * receivers * samples * G,
+            flops=16 * transmits * events * receivers * samples,
             bytes_accessed=events * receivers * samples * 2
             + transmits * receivers * diff * 2,
             transcendentals=0,
         ),
-    )(at, signs_t, encoded)
+    )(st, encoded)
 
 
 def beam_kernel(scale, mask_ref, delta_ref, dsum_ref, *refs):
@@ -279,14 +252,14 @@
     stripes, groups = sizes
     events, transmits = signs.shape
     receivers = rx_block.shape[0]
-    masks, own = cast(groups, rx_block, apodization, tx_block)
+    at = lax.axis_index("tx").astype(jnp.int32).reshape(1)
+    masks, own, st = cast(sizes, at, rx_block, apodization, tx_block, signs.T)
     masks = lax.all_to_all(masks, "img", 0, 0, tiled=True)
     tx_bits = [own] + [
         lax.ppermute(own, "tx", [((t + d) % stripes, t) for t in range(stripes)])
         for d in range(1, stripes)
     ]
-    at = lax.axis_index("tx").astype(jnp.int32).reshape(1)
-    delta, dsum = decode(stripes, at, signs.T, encoded)
+    delta, dsum = decode(st, encoded)
     scale = math.sqrt(events / (transmits * receivers)) / events
     parts = beamform(scale, stripes, masks, tx_bits, delta, dsum)
     parts = parts.reshape(stripes * groups, L // stripes, lines_here)

time: 84.5 us -> 94.3 us (1.12)
  Pallas kernels: 50.9 us -> 60.8 us
    pallas_call x2, Pallas kernels: 29.4 us -> 39.3 us  [the longest x1 36.8 us: decode(): pl.pallas_call(decode_kernel, grid=(receivers // RB,), in_specs=[pl.Block...]
  transfers between devices with their start and end apart: 4 -> 4, of which waited for: 0 -> 0; matrix products, arithmetic and copies ran while one was open for 0% -> 0% of each run, Pallas kernels for 32% -> 39%
where the time goes in v5:
time: 94.3 us; the launch traced here: 93.9 us
  Pallas kernels  60.8 us (64%)
  blocking collectives  21.2 us (22%)
  starting transfers between devices  10.4 us (11%)
    pallas_call x1, Pallas kernels, decode(): pl.pallas_call(decode_kernel, grid=(receivers // RB,), in_specs=[pl.Block...  36.8 us
    pallas_call x1, Pallas kernels, beamform(): pl.pallas_call(functools.partial(beam_kernel, scale), grid=(groups // som...  21.5 us
    all_to_all x1, blocking collectives, on_device(): parts = lax.all_to_all(parts, ('tx', 'img'), 0, 0, tiled=True)  21.2 us
    all_to_all x1, starting transfers between devices, on_device(): masks = lax.all_to_all(masks, 'img', 0, 0, tiled=True)  7.44 us
    ppermute x3, starting transfers between devices, on_device(): lax.ppermute(own, 'tx', [((t + d) % stripes, t) for t in range(stripes)])  2.95 us
    pallas_call x1, Pallas kernels, cast(): pl.pallas_call(functools.partial(cast_kernel, stripes), grid_spec=pltpu.P...  2.46 us
  transfers between devices with their start and end apart: 4, of which 0 were waited for; matrix products, arithmetic and copies ran while one was open for 0% of the time, Pallas kernels for 39%

profile of v5, /device:TPU:0, one launch (start us, length us, event | category | flops | bytes accessed | tf_op | source)
XLA Modules:
  0.0 93.9 jit_solution(8952985672893534327)
XLA Ops:
  0.0 2.5 %shard_map.55 = (bf16[8,2,128,256]{3,2,1,0:T(8,128)(2,1)}, bf16[16,2048]{1,0:T(8,128)(2,1)}, bf16[64,256]{1,0:T(8,128)(2,1)}) custom-call(s32[1]{0:T(128)} %bitcast.at_ref, s32[8,128,256]{2,1,0:T(8,128)} %bitcast.7, s32[8,128,256]{2,1,0:T(8,128)} %bitcast.8, s32[16,2048]{1,0:T(8,128)} %tx_ref.1, s32[64,1024]{1,0:T(8,128)} %bitcast.9), custom_call_target="tpu_custom_call" | custom-call | tf_op jit(solution)/shard_map/pallas_call | solution.py:50
  2.5 0.0 copy-start
  2.5 7.4 %all-to-all-start = ((bf16[8,2,128,256]{3,2,1,0:T(8,128)(2,1)}), bf16[8,2,128,256]{3,2,1,0:T(8,128)(2,1)S(1)}, u32[]{:S(2)}, u32[]{:S(2)}) async-start(bf16[8,2,128,256]{3,2,1,0:T(8,128)(2,1)} %get-tuple-element.10), calls=%async_computation | async-start | bytes 2097152 | tf_op jit(solution)/shard_map/all_to_all | solution.py:257
  9.9 0.0 collective-permute-start.2
  9.9 1.6 %collective-permute-start.1 = (bf16[16,2048]{1,0:T(8,128)(2,1)}, bf16[16,2048]{1,0:T(8,128)(2,1)S(1)}, u32[]{:S(2)}, u32[]{:S(2)}) collective-permute-start(bf16[16,2048]{1,0:T(8,128)(2,1)} %get-tuple-element.14.refs_0_), channel_id=1, source_target_pairs={{16,0},{24,8},{0,16},{8,24},{17,1},{25,9},{1,17},{9,25},{18,2},{26... | collective-permute-start | bytes 196616 | tf_op jit(solution)/shard_map/ppermute | solution.py:259
  11.5 1.4 %collective-permute-start = (bf16[16,2048]{1,0:T(8,128)(2,1)}, bf16[16,2048]{1,0:T(8,128)(2,1)S(1)}, u32[]{:S(2)}, u32[]{:S(2)}) collective-permute-start(bf16[16,2048]{1,0:T(8,128)(2,1)} %get-tuple-element.14.refs_0_), channel_id=1, source_target_pairs={{8,0},{16,8},{24,16},{0,24},{9,1},{17,9},{25,17},{1,25},{10,2},{18... | collective-permute-start | bytes 196616 | tf_op jit(solution)/shard_map/ppermute | solution.py:259
  12.9 0.0 copy-start.1
  12.9 0.8 copy-done.1
  13.6 36.8 %shard_map.56 = (bf16[64,128,384]{2,1,0:T(8,128)(2,1)}, f32[128,384]{1,0:T(8,128)S(1)}) custom-call(bf16[64,256]{1,0:T(8,128)(2,1)S(1)} %copy-done.1, bf16[256,128,512]{2,1,0:T(8,128)(2,1)} %enc_ref.1), custom_call_target="tpu_custom_call" | custom-call | flops 17179869184 | bytes 39845888 | tf_op jit(solution)/shard_map/pallas_call | solution.py:111
  50.5 0.0 collective-permute-done.2.refs_3_
  50.5 0.0 collective-permute-done.1.refs_2_
  50.5 0.0 collective-permute-done.refs_1_
  50.5 0.0 all-to-all-done.mask_ref
  50.5 0.0 copy-done
  50.5 21.5 %shard_map.57 = bf16[4,8,32,256]{3,2,1,0:T(8,128)(2,1)S(1)} custom-call(bf16[8,2,128,256]{3,2,1,0:T(8,128)(2,1)S(1)} %all-to-all-done.mask_ref, bf16[64,128,384]{2,1,0:T(8,128)(2,1)} %get-tuple-element.12.delta_ref, f32[128,384]{1,0:T(8,128)S(1)} %get-tuple-element.13.dsum_ref, bf16[16,2048]{1,0:T(8,128)(2,1)S(1)} %copy-done, ...), custom_call_target="tpu_custom_call" | custom-call | flops 12884901888 | bytes 6291456 | tf_op jit(solution)/shard_map/pallas_call | solution.py:216
  72.0 21.2 %all_to_all.10 = bf16[32,32,256]{2,1,0:T(8,128)(2,1)S(1)} all-to-all(bf16[32,32,256]{2,1,0:T(8,128)(2,1)S(1)} %bitcast.6), channel_id=1, replica_groups=mesh['tx'=4,'img'=8] {'tx','img'}, dimensions={0} | all-to-all | bytes 1048576 | tf_op jit(solution)/shard_map/all_to_all | solution.py:266
  93.2 0.7 convert_reduce_fusion
Async XLA Ops:
  2.5 48.0 %copy-start = (bf16[16,2048]{1,0:T(8,128)(2,1)S(1)}, bf16[16,2048]{1,0:T(8,128)(2,1)}, u32[]{:S(2)}) copy-start(bf16[16,2048]{1,0:T(8,128)(2,1)} %get-tuple-element.14.refs_0_) | copy-start | bytes 196612
  2.5 48.0 %all-to-all-start = ((bf16[8,2,128,256]{3,2,1,0:T(8,128)(2,1)}), bf16[8,2,128,256]{3,2,1,0:T(8,128)(2,1)S(1)}, u32[]{:S(2)}, u32[]{:S(2)}) async-start(bf16[8,2,128,256]{3,2,1,0:T(8,128)(2,1)} %get-tuple-element.10), calls=%async_computation | async-start | bytes 2097152 | tf_op jit(solution)/shard_map/all_to_all | solution.py:257
  9.9 40.6 %collective-permute-start.2 = (bf16[16,2048]{1,0:T(8,128)(2,1)}, bf16[16,2048]{1,0:T(8,128)(2,1)S(1)}, u32[]{:S(2)}, u32[]{:S(2)}) collective-permute-start(bf16[16,2048]{1,0:T(8,128)(2,1)} %get-tuple-element.14.refs_0_), channel_id=1, source_target_pairs={{24,0},{0,8},{8,16},{16,24},{25,1},{1,9},{9,17},{17,25},{26,2},{2,... | collective-permute-start | bytes 196616 | tf_op jit(solution)/shard_map/ppermute | solution.py:259
  9.9 40.6 %collective-permute-start.1 = (bf16[16,2048]{1,0:T(8,128)(2,1)}, bf16[16,2048]{1,0:T(8,128)(2,1)S(1)}, u32[]{:S(2)}, u32[]{:S(2)}) collective-permute-start(bf16[16,2048]{1,0:T(8,128)(2,1)} %get-tuple-element.14.refs_0_), channel_id=1, source_target_pairs={{16,0},{24,8},{0,16},{8,24},{17,1},{25,9},{1,17},{9,25},{18,2},{26... | collective-permute-start | bytes 196616 | tf_op jit(solution)/shard_map/ppermute | solution.py:259
  11.5 39.0 %collective-permute-start = (bf16[16,2048]{1,0:T(8,128)(2,1)}, bf16[16,2048]{1,0:T(8,128)(2,1)S(1)}, u32[]{:S(2)}, u32[]{:S(2)}) collective-permute-start(bf16[16,2048]{1,0:T(8,128)(2,1)} %get-tuple-element.14.refs_0_), channel_id=1, source_target_pairs={{8,0},{16,8},{24,16},{0,24},{9,1},{17,9},{25,17},{1,25},{10,2},{18... | collective-permute-start | bytes 196616 | tf_op jit(solution)/shard_map/ppermute | solution.py:259
  12.9 0.8 copy-start.1

commit v6 on v5

--- a/solution.py
+++ b/solution.py
@@ -9,7 +9,7 @@
 from jax.sharding import PartitionSpec as P
 
 L = 128
-PITCH = 24
+G = 8
 RB = 16
 BF = jnp.bfloat16
 F32 = jnp.float32
@@ -74,34 +74,41 @@
     )(at, rx_block.reshape(split), apodization.reshape(split), tx_block, signs_t)
 
 
-def decode_kernel(st_ref, enc_ref, delta_ref, dsum_ref, rows_ref, turn_ref):
+def decode_kernel(st_ref, enc_ref, delta_ref, dsum_ref, sk_ref, low_ref, high_ref):
     transmits, events = st_ref.shape
     samples = enc_ref.shape[2]
-    parts, levels = samples // L, samples // L - 1
-    for e in range(events):
-        piece = enc_ref[e].astype(F32)
-        for c in range(parts):
-            rows_ref[c, e * PITCH : e * PITCH + RB, :] = piece[:, c * L : (c + 1) * L]
-    for r in range(RB):
-        d = [
-            dot(
-                st_ref[...],
-                rows_ref[c, pl.ds(r, events, stride=PITCH), :].astype(BF),
-            )
-            for c in range(parts)
-        ]
-        for v in range(levels):
-            turn_ref[v, r * transmits : (r + 1) * transmits, :] = (
-                d[v + 1] - d[v]
-            ) * 0.5
-            dsum_ref[r : r + 1, v * L : (v + 1) * L] = (
-                jnp.sum(d[v + 1] + d[v], axis=0, keepdims=True) * 0.5
-            )
-    for k in range(transmits):
-        for v in range(levels):
-            delta_ref[k, :, v * L : (v + 1) * L] = turn_ref[
-                v, pl.ds(k, RB, stride=transmits), :
-            ].astype(BF)
+    rows, depth = sk_ref.shape
+    levels = samples // L - 1
+    width = 32
+
+    @pl.when(pl.program_id(0) == 0)
+    def _():
+        up = iota((rows, transmits), 0) // G == iota((rows, transmits), 1)
+        tall = dot(up.astype(F32).astype(BF), st_ref[...]).astype(BF)
+        wide = 512
+        for at in range(0, depth, wide):
+            out = (iota((events, wide), 1) + at) // G == iota((events, wide), 0)
+            spread = dot(tall, out.astype(F32).astype(BF))
+            same = iota((rows, wide), 0) % G == iota((rows, wide), 1) % G
+            sk_ref[:, at : at + wide] = jnp.where(same, spread, 0.0).astype(BF)
+
+    first = iota((1, RB, samples), 1) < G
+    for at in range(0, events, width):
+        piece = enc_ref[at : at + width].reshape(width // 2, 2, RB, samples)
+        a, b = piece[:, 0], piece[:, 1]
+        here = slice(at * G, (at + width) * G)
+        low = jnp.where(first, a, pltpu.roll(b, G, 1))
+        high = jnp.where(first, pltpu.roll(a, G, 1), b)
+        low_ref[here, :] = low.reshape(width * G, samples)
+        high_ref[here, :] = high.reshape(width * G, samples)
+    deltas = []
+    for half, x_ref in enumerate((low_ref, high_ref)):
+        d = dot(sk_ref[...], x_ref[...])
+        low, high = d[:, : samples - L], d[:, L:]
+        deltas.append(((high - low) * 0.5).reshape(transmits, G, samples - L))
+        mean = (high + low).reshape(transmits, G, samples - L)
+        dsum_ref[half * G : (half + 1) * G, :] = jnp.sum(mean, axis=0) * 0.5
+    delta_ref[...] = jnp.concatenate(deltas, axis=1).astype(BF)
 
 
 def decode(st, encoded):
@@ -124,8 +131,9 @@
             jax.ShapeDtypeStruct((receivers, diff), F32),
         ],
         scratch_shapes=[
-            pltpu.VMEM((samples // L, events * PITCH, L), F32),
-            pltpu.VMEM((diff // L, RB * transmits, L), F32),
+            pltpu.VMEM((transmits * G, events * G), BF),
+            pltpu.VMEM((events * G, samples), BF),
+            pltpu.VMEM((events * G, samples), BF),
         ],
         compiler_params=pltpu.CompilerParams(vmem_limit_bytes=50 * 2**20),
         cost_estimate=pl.CostEstimate(
@@ -210,7 +218,7 @@
     groups, _, receivers, wide = masks.shape
     transmits, _, diff = delta.shape
     levels = diff // L
-    block = 16
+    block = min(32, transmits)
     some = min(groups, 8)
     steps = transmits // block
     return pl.pallas_call(

time: 94.3 us -> 81.1 us (0.86)
  Pallas kernels: 60.8 us -> 47.4 us
    pallas_call x1, Pallas kernels: 36.8 us -> 23.4 us  [decode(): pl.pallas_call(decode_kernel, grid=(receivers // RB,), in_specs=[pl.Block...]
  transfers between devices with their start and end apart: 4 -> 4, of which waited for: 0 -> 0; matrix products, arithmetic and copies ran while one was open for 0% -> 0% of each run, Pallas kernels for 39% -> 29%
where the time goes in v6:
time: 81.1 us; the launch traced here: 80.5 us
  Pallas kernels  47.4 us (58%)
  blocking collectives  21.2 us (26%)
  starting transfers between devices  10.4 us (13%)
    pallas_call x1, Pallas kernels, decode(): pl.pallas_call(decode_kernel, grid=(receivers // RB,), in_specs=[pl.Block...  23.4 us
    pallas_call x1, Pallas kernels, beamform(): pl.pallas_call(functools.partial(beam_kernel, scale), grid=(groups // som...  21.5 us
    all_to_all x1, blocking collectives, on_device(): parts = lax.all_to_all(parts, ('tx', 'img'), 0, 0, tiled=True)  21.2 us
    all_to_all x1, starting transfers between devices, on_device(): masks = lax.all_to_all(masks, 'img', 0, 0, tiled=True)  7.44 us
    ppermute x3, starting transfers between devices, on_device(): lax.ppermute(own, 'tx', [((t + d) % stripes, t) for t in range(stripes)])  2.95 us
    pallas_call x1, Pallas kernels, cast(): pl.pallas_call(functools.partial(cast_kernel, stripes), grid_spec=pltpu.P...  2.46 us
  transfers between devices with their start and end apart: 4, of which 0 were waited for; matrix products, arithmetic and copies ran while one was open for 0% of the time, Pallas kernels for 29%

profile of v6, /device:TPU:0, one launch (start us, length us, event | category | flops | bytes accessed | tf_op | source)
XLA Modules:
  0.0 80.5 jit_solution(4835043338217519547)
XLA Ops:
  0.0 2.5 %shard_map.55 = (bf16[8,2,128,256]{3,2,1,0:T(8,128)(2,1)}, bf16[16,2048]{1,0:T(8,128)(2,1)}, bf16[64,256]{1,0:T(8,128)(2,1)}) custom-call(s32[1]{0:T(128)} %bitcast.at_ref, s32[8,128,256]{2,1,0:T(8,128)} %bitcast.7, s32[8,128,256]{2,1,0:T(8,128)} %bitcast.8, s32[16,2048]{1,0:T(8,128)} %tx_ref.1, s32[64,1024]{1,0:T(8,128)} %bitcast.9), custom_call_target="tpu_custom_call" | custom-call | tf_op jit(solution)/shard_map/pallas_call | solution.py:50
  2.5 0.0 copy-start
  2.5 7.4 %all-to-all-start = ((bf16[8,2,128,256]{3,2,1,0:T(8,128)(2,1)}), bf16[8,2,128,256]{3,2,1,0:T(8,128)(2,1)S(1)}, u32[]{:S(2)}, u32[]{:S(2)}) async-start(bf16[8,2,128,256]{3,2,1,0:T(8,128)(2,1)} %get-tuple-element.10), calls=%async_computation | async-start | bytes 2097152 | tf_op jit(solution)/shard_map/all_to_all | solution.py:265
  9.9 0.0 collective-permute-start.2
  9.9 1.6 %collective-permute-start.1 = (bf16[16,2048]{1,0:T(8,128)(2,1)}, bf16[16,2048]{1,0:T(8,128)(2,1)S(1)}, u32[]{:S(2)}, u32[]{:S(2)}) collective-permute-start(bf16[16,2048]{1,0:T(8,128)(2,1)} %get-tuple-element.14.refs_0_), channel_id=1, source_target_pairs={{16,0},{24,8},{0,16},{8,24},{17,1},{25,9},{1,17},{9,25},{18,2},{26... | collective-permute-start | bytes 196616 | tf_op jit(solution)/shard_map/ppermute | solution.py:267
  11.5 1.4 %collective-permute-start = (bf16[16,2048]{1,0:T(8,128)(2,1)}, bf16[16,2048]{1,0:T(8,128)(2,1)S(1)}, u32[]{:S(2)}, u32[]{:S(2)}) collective-permute-start(bf16[16,2048]{1,0:T(8,128)(2,1)} %get-tuple-element.14.refs_0_), channel_id=1, source_target_pairs={{8,0},{16,8},{24,16},{0,24},{9,1},{17,9},{25,17},{1,25},{10,2},{18... | collective-permute-start | bytes 196616 | tf_op jit(solution)/shard_map/ppermute | solution.py:267
  12.9 0.0 copy-start.1
  12.9 0.8 copy-done.1
  13.6 23.4 %shard_map.56 = (bf16[64,128,384]{2,1,0:T(8,128)(2,1)}, f32[128,384]{1,0:T(8,128)S(1)}) custom-call(bf16[64,256]{1,0:T(8,128)(2,1)S(1)} %copy-done.1, bf16[256,128,512]{2,1,0:T(8,128)(2,1)} %enc_ref.1), custom_call_target="tpu_custom_call" | custom-call | flops 17179869184 | bytes 39845888 | tf_op jit(solution)/shard_map/pallas_call | solution.py:118
  37.0 0.0 collective-permute-done.2.refs_3_
  37.0 0.0 collective-permute-done.1.refs_2_
  37.0 0.0 collective-permute-done.refs_1_
  37.0 0.0 all-to-all-done.mask_ref
  37.0 0.0 copy-done
  37.0 21.5 %shard_map.57 = bf16[4,8,32,256]{3,2,1,0:T(8,128)(2,1)S(1)} custom-call(bf16[8,2,128,256]{3,2,1,0:T(8,128)(2,1)S(1)} %all-to-all-done.mask_ref, bf16[64,128,384]{2,1,0:T(8,128)(2,1)} %get-tuple-element.12.delta_ref, f32[128,384]{1,0:T(8,128)S(1)} %get-tuple-element.13.dsum_ref, bf16[16,2048]{1,0:T(8,128)(2,1)S(1)} %copy-done, ...), custom_call_target="tpu_custom_call" | custom-call | flops 12884901888 | bytes 6291456 | tf_op jit(solution)/shard_map/pallas_call | solution.py:224
  58.6 21.2 %all_to_all.10 = bf16[32,32,256]{2,1,0:T(8,128)(2,1)S(1)} all-to-all(bf16[32,32,256]{2,1,0:T(8,128)(2,1)S(1)} %bitcast.6), channel_id=1, replica_groups=mesh['tx'=4,'img'=8] {'tx','img'}, dimensions={0} | all-to-all | bytes 1048576 | tf_op jit(solution)/shard_map/all_to_all | solution.py:274
  79.8 0.7 convert_reduce_fusion
Async XLA Ops:
  2.5 34.6 %copy-start = (bf16[16,2048]{1,0:T(8,128)(2,1)S(1)}, bf16[16,2048]{1,0:T(8,128)(2,1)}, u32[]{:S(2)}) copy-start(bf16[16,2048]{1,0:T(8,128)(2,1)} %get-tuple-element.14.refs_0_) | copy-start | bytes 196612
  2.5 34.5 %all-to-all-start = ((bf16[8,2,128,256]{3,2,1,0:T(8,128)(2,1)}), bf16[8,2,128,256]{3,2,1,0:T(8,128)(2,1)S(1)}, u32[]{:S(2)}, u32[]{:S(2)}) async-start(bf16[8,2,128,256]{3,2,1,0:T(8,128)(2,1)} %get-tuple-element.10), calls=%async_computation | async-start | bytes 2097152 | tf_op jit(solution)/shard_map/all_to_all | solution.py:265
  9.9 27.1 %collective-permute-start.2 = (bf16[16,2048]{1,0:T(8,128)(2,1)}, bf16[16,2048]{1,0:T(8,128)(2,1)S(1)}, u32[]{:S(2)}, u32[]{:S(2)}) collective-permute-start(bf16[16,2048]{1,0:T(8,128)(2,1)} %get-tuple-element.14.refs_0_), channel_id=1, source_target_pairs={{24,0},{0,8},{8,16},{16,24},{25,1},{1,9},{9,17},{17,25},{26,2},{2,... | collective-permute-start | bytes 196616 | tf_op jit(solution)/shard_map/ppermute | solution.py:267
  9.9 27.1 %collective-permute-start.1 = (bf16[16,2048]{1,0:T(8,128)(2,1)}, bf16[16,2048]{1,0:T(8,128)(2,1)S(1)}, u32[]{:S(2)}, u32[]{:S(2)}) collective-permute-start(bf16[16,2048]{1,0:T(8,128)(2,1)} %get-tuple-element.14.refs_0_), channel_id=1, source_target_pairs={{16,0},{24,8},{0,16},{8,24},{17,1},{25,9},{1,17},{9,25},{18,2},{26... | collective-permute-start | bytes 196616 | tf_op jit(solution)/shard_map/ppermute | solution.py:267
  11.5 25.5 %collective-permute-start = (bf16[16,2048]{1,0:T(8,128)(2,1)}, bf16[16,2048]{1,0:T(8,128)(2,1)S(1)}, u32[]{:S(2)}, u32[]{:S(2)}) collective-permute-start(bf16[16,2048]{1,0:T(8,128)(2,1)} %get-tuple-element.14.refs_0_), channel_id=1, source_target_pairs={{8,0},{16,8},{24,16},{0,24},{9,1},{17,9},{25,17},{1,25},{10,2},{18... | collective-permute-start | bytes 196616 | tf_op jit(solution)/shard_map/ppermute | solution.py:267
  12.9 0.8 copy-start.1

commit v7 on v6

--- a/solution.py
+++ b/solution.py
@@ -9,7 +9,7 @@
 from jax.sharding import PartitionSpec as P
 
 L = 128
-G = 8
+G = 4
 RB = 16
 BF = jnp.bfloat16
 F32 = jnp.float32
@@ -74,41 +74,58 @@
     )(at, rx_block.reshape(split), apodization.reshape(split), tx_block, signs_t)
 
 
-def decode_kernel(st_ref, enc_ref, delta_ref, dsum_ref, sk_ref, low_ref, high_ref):
+def decode_kernel(st_ref, enc_ref, delta_ref, dsum_ref, sk_ref, x_ref):
     transmits, events = st_ref.shape
     samples = enc_ref.shape[2]
     rows, depth = sk_ref.shape
-    levels = samples // L - 1
+    diff = samples - L
     width = 32
 
     @pl.when(pl.program_id(0) == 0)
     def _():
         up = iota((rows, transmits), 0) // G == iota((rows, transmits), 1)
         tall = dot(up.astype(F32).astype(BF), st_ref[...]).astype(BF)
-        wide = 512
+        wide = 256
         for at in range(0, depth, wide):
-            out = (iota((events, wide), 1) + at) // G == iota((events, wide), 0)
+            row = iota((events, wide), 1) + at
+            event = row // RB * 4 + row // G % 2 * 2 + row // (2 * G) % 2
+            out = event == iota((events, wide), 0)
             spread = dot(tall, out.astype(F32).astype(BF))
             same = iota((rows, wide), 0) % G == iota((rows, wide), 1) % G
             sk_ref[:, at : at + wide] = jnp.where(same, spread, 0.0).astype(BF)
 
-    first = iota((1, RB, samples), 1) < G
+    row = iota((1, RB, samples), 1)
+    first, inner = row < 2 * G, row % (2 * G) < G
     for at in range(0, events, width):
-        piece = enc_ref[at : at + width].reshape(width // 2, 2, RB, samples)
-        a, b = piece[:, 0], piece[:, 1]
+        piece = enc_ref[at : at + width].reshape(width // 4, 4, RB, samples)
+        a, b, c, d = (piece[:, e] for e in range(4))
         here = slice(at * G, (at + width) * G)
-        low = jnp.where(first, a, pltpu.roll(b, G, 1))
-        high = jnp.where(first, pltpu.roll(a, G, 1), b)
-        low_ref[here, :] = low.reshape(width * G, samples)
-        high_ref[here, :] = high.reshape(width * G, samples)
+        for side in range(2):
+            if side == 0:
+                ab = jnp.where(first, a, pltpu.roll(b, 2 * G, 1))
+                cd = jnp.where(first, c, pltpu.roll(d, 2 * G, 1))
+            else:
+                ab = jnp.where(first, pltpu.roll(a, 2 * G, 1), b)
+                cd = jnp.where(first, pltpu.roll(c, 2 * G, 1), d)
+            low = jnp.where(inner, ab, pltpu.roll(cd, G, 1))
+            high = jnp.where(inner, pltpu.roll(ab, RB - G, 1), cd)
+            x_ref[2 * side, here, :] = low.reshape(width * G, samples)
+            x_ref[2 * side + 1, here, :] = high.reshape(width * G, samples)
     deltas = []
-    for half, x_ref in enumerate((low_ref, high_ref)):
-        d = dot(sk_ref[...], x_ref[...])
-        low, high = d[:, : samples - L], d[:, L:]
-        deltas.append(((high - low) * 0.5).reshape(transmits, G, samples - L))
-        mean = (high + low).reshape(transmits, G, samples - L)
-        dsum_ref[half * G : (half + 1) * G, :] = jnp.sum(mean, axis=0) * 0.5
-    delta_ref[...] = jnp.concatenate(deltas, axis=1).astype(BF)
+    for q in range(RB // G):
+        d = dot(sk_ref[...], x_ref[q])
+        low, high = d[:, :diff], d[:, L:]
+        deltas.append(((high - low) * 0.5).reshape(transmits // 2, 2 * G, diff))
+        mean = jnp.sum((high + low).reshape(transmits // 2, 2 * G, diff), axis=0)
+        dsum_ref[q * G : (q + 1) * G, :] = (mean[:G] + mean[G:]) * 0.5
+    upper = iota((1, 2 * G, diff), 1) < G
+    evens, odds = [], []
+    for side in range(2):
+        low, high = deltas[2 * side], deltas[2 * side + 1]
+        evens.append(jnp.where(upper, low, pltpu.roll(high, G, 1)))
+        odds.append(jnp.where(upper, pltpu.roll(low, G, 1), high))
+    delta_ref[:, 0] = jnp.concatenate(evens, axis=1).astype(BF)
+    delta_ref[:, 1] = jnp.concatenate(odds, axis=1).astype(BF)
 
 
 def decode(st, encoded):
@@ -123,17 +140,16 @@
             pl.BlockSpec((events, RB, samples), lambda g: (0, g, 0)),
         ],
         out_specs=[
-            pl.BlockSpec((transmits, RB, diff), lambda g: (0, g, 0)),
+            pl.BlockSpec((transmits // 2, 2, RB, diff), lambda g: (0, 0, g, 0)),
             pl.BlockSpec((RB, diff), lambda g: (g, 0)),
         ],
         out_shape=[
-            jax.ShapeDtypeStruct((transmits, receivers, diff), BF),
+            jax.ShapeDtypeStruct((transmits // 2, 2, receivers, diff), BF),
             jax.ShapeDtypeStruct((receivers, diff), F32),
         ],
         scratch_shapes=[
             pltpu.VMEM((transmits * G, events * G), BF),
-            pltpu.VMEM((events * G, samples), BF),
-            pltpu.VMEM((events * G, samples), BF),
+            pltpu.VMEM((RB // G, events * G, samples), BF),
         ],
         compiler_params=pltpu.CompilerParams(vmem_limit_bytes=50 * 2**20),
         cost_estimate=pl.CostEstimate(
@@ -218,7 +234,7 @@
     groups, _, receivers, wide = masks.shape
     transmits, _, diff = delta.shape
     levels = diff // L
-    block = min(32, transmits)
+    block = min(16, transmits)
     some = min(groups, 8)
     steps = transmits // block
     return pl.pallas_call(
@@ -268,6 +284,7 @@
         for d in range(1, stripes)
     ]
     delta, dsum = decode(st, encoded)
+    delta = delta.reshape(transmits, *delta.shape[2:])
     scale = math.sqrt(events / (transmits * receivers)) / events
     parts = beamform(scale, stripes, masks, tx_bits, delta, dsum)
     parts = parts.reshape(stripes * groups, L // stripes, lines_here)

time: 81.1 us -> 78.1 us (0.963)
  Pallas kernels: 47.4 us -> 43.5 us
  waiting for transfers between devices: 0.01 us -> 2.49 us
  blocking collectives: 21.2 us -> 19.8 us
    pallas_call x1, Pallas kernels: 23.4 us -> 19.6 us  [decode(): pl.pallas_call(decode_kernel, grid=(receivers // RB,), in_specs=[pl.Block...]
    all_to_all x1, waiting for transfers between devices: 0.01 us -> 2.48 us  [on_device(): masks = lax.all_to_all(masks, 'img', 0, 0, tiled=True)]
    all_to_all x1, blocking collectives: 21.2 us -> 19.8 us  [on_device(): parts = lax.all_to_all(parts, ('tx', 'img'), 0, 0, tiled=True)]
  transfers between devices with their start and end apart: 4 -> 4, of which waited for: 0 -> 1; matrix products, arithmetic and copies ran while one was open for 0% -> 0% of each run, Pallas kernels for 29% -> 25%
where the time goes in v7:
time: 78.1 us; the launch traced here: 77.6 us
  Pallas kernels  43.5 us (56%)
  blocking collectives  19.8 us (25%)
  starting transfers between devices  10.4 us (13%)
  waiting for transfers between devices  2.49 us (3%)
    pallas_call x1, Pallas kernels, beamform(): pl.pallas_call(functools.partial(beam_kernel, scale), grid=(groups // som...  21.5 us
    all_to_all x1, blocking collectives, on_device(): parts = lax.all_to_all(parts, ('tx', 'img'), 0, 0, tiled=True)  19.8 us
    pallas_call x1, Pallas kernels, decode(): pl.pallas_call(decode_kernel, grid=(receivers // RB,), in_specs=[pl.Block...  19.6 us
    all_to_all x1, starting transfers between devices, on_device(): masks = lax.all_to_all(masks, 'img', 0, 0, tiled=True)  7.44 us
    ppermute x3, starting transfers between devices, on_device(): lax.ppermute(own, 'tx', [((t + d) % stripes, t) for t in range(stripes)])  2.95 us
    all_to_all x1, waiting for transfers between devices, on_device(): masks = lax.all_to_all(masks, 'img', 0, 0, tiled=True)  2.48 us
    pallas_call x1, Pallas kernels, cast(): pl.pallas_call(functools.partial(cast_kernel, stripes), grid_spec=pltpu.P...  2.46 us
  transfers between devices with their start and end apart: 4, of which 1 were waited for; matrix products, arithmetic and copies ran while one was open for 0% of the time, Pallas kernels for 25%

profile of v7, /device:TPU:0, one launch (start us, length us, event | category | flops | bytes accessed | tf_op | source)
XLA Modules:
  0.0 77.6 jit_solution(18100500638110453513)
XLA Ops:
  0.0 2.5 %shard_map.55 = (bf16[8,2,128,256]{3,2,1,0:T(8,128)(2,1)}, bf16[16,2048]{1,0:T(8,128)(2,1)}, bf16[64,256]{1,0:T(8,128)(2,1)}) custom-call(s32[1]{0:T(128)} %bitcast.at_ref, s32[8,128,256]{2,1,0:T(8,128)} %bitcast.8, s32[8,128,256]{2,1,0:T(8,128)} %bitcast.9, s32[16,2048]{1,0:T(8,128)} %tx_ref.1, s32[64,1024]{1,0:T(8,128)} %bitcast.10), custom_call_target="tpu_custom_call" | custom-call | tf_op jit(solution)/shard_map/pallas_call | solution.py:50
  2.5 0.0 copy-start
  2.5 7.4 %all-to-all-start = ((bf16[8,2,128,256]{3,2,1,0:T(8,128)(2,1)}), bf16[8,2,128,256]{3,2,1,0:T(8,128)(2,1)S(1)}, u32[]{:S(2)}, u32[]{:S(2)}) async-start(bf16[8,2,128,256]{3,2,1,0:T(8,128)(2,1)} %get-tuple-element.10), calls=%async_computation | async-start | bytes 2097152 | tf_op jit(solution)/shard_map/all_to_all | solution.py:281
  9.9 0.0 collective-permute-start.2
  9.9 1.6 %collective-permute-start.1 = (bf16[16,2048]{1,0:T(8,128)(2,1)}, bf16[16,2048]{1,0:T(8,128)(2,1)S(1)}, u32[]{:S(2)}, u32[]{:S(2)}) collective-permute-start(bf16[16,2048]{1,0:T(8,128)(2,1)} %get-tuple-element.14.refs_0_), channel_id=1, source_target_pairs={{16,0},{24,8},{0,16},{8,24},{17,1},{25,9},{1,17},{9,25},{18,2},{26... | collective-permute-start | bytes 196616 | tf_op jit(solution)/shard_map/ppermute | solution.py:283
  11.5 1.4 %collective-permute-start = (bf16[16,2048]{1,0:T(8,128)(2,1)}, bf16[16,2048]{1,0:T(8,128)(2,1)S(1)}, u32[]{:S(2)}, u32[]{:S(2)}) collective-permute-start(bf16[16,2048]{1,0:T(8,128)(2,1)} %get-tuple-element.14.refs_0_), channel_id=1, source_target_pairs={{8,0},{16,8},{24,16},{0,24},{9,1},{17,9},{25,17},{1,25},{10,2},{18... | collective-permute-start | bytes 196616 | tf_op jit(solution)/shard_map/ppermute | solution.py:283
  12.9 0.0 copy-start.1
  12.9 0.8 copy-done.1
  13.6 19.6 %shard_map.56 = (bf16[32,2,128,384]{3,2,1,0:T(8,128)(2,1)}, f32[128,384]{1,0:T(8,128)S(1)}) custom-call(bf16[64,256]{1,0:T(8,128)(2,1)S(1)} %copy-done.1, bf16[256,128,512]{2,1,0:T(8,128)(2,1)} %enc_ref.1), custom_call_target="tpu_custom_call" | custom-call | flops 17179869184 | bytes 39845888 | tf_op jit(solution)/shard_map/pallas_call | solution.py:135
  33.2 0.0 collective-permute-done.2.refs_3_
  33.2 0.0 collective-permute-done.1.refs_2_
  33.2 0.0 collective-permute-done.refs_1_
  33.2 2.5 %all-to-all-done.mask_ref = bf16[8,2,128,256]{3,2,1,0:T(8,128)(2,1)S(1)} async-done(((bf16[8,2,128,256]{3,2,1,0:T(8,128)(2,1)}), bf16[8,2,128,256]{3,2,1,0:T(8,128)(2,1)S(1)}, u32[]{:S(2)}, u32[]{:S(2)}) %all-to-all-start) | async-done | bytes 1048608 | tf_op jit(solution)/shard_map/all_to_all | solution.py:281
  35.7 0.0 copy-done
  35.7 21.5 %shard_map.57 = bf16[4,8,32,256]{3,2,1,0:T(8,128)(2,1)S(1)} custom-call(bf16[8,2,128,256]{3,2,1,0:T(8,128)(2,1)S(1)} %all-to-all-done.mask_ref, bf16[64,128,384]{2,1,0:T(8,128)(2,1)} %bitcast.11, f32[128,384]{1,0:T(8,128)S(1)} %get-tuple-element.13.dsum_ref, bf16[16,2048]{1,0:T(8,128)(2,1)S(1)} %copy-done, ...), custom_call_target="tpu_custom_call" | custom-call | flops 12884901888 | bytes 6291456 | tf_op jit(solution)/shard_map/pallas_call | solution.py:240
  57.2 19.8 %all_to_all.10 = bf16[32,32,256]{2,1,0:T(8,128)(2,1)S(1)} all-to-all(bf16[32,32,256]{2,1,0:T(8,128)(2,1)S(1)} %bitcast.7), channel_id=1, replica_groups=mesh['tx'=4,'img'=8] {'tx','img'}, dimensions={0} | all-to-all | bytes 1048576 | tf_op jit(solution)/shard_map/all_to_all | solution.py:291
  76.9 0.7 convert_reduce_fusion
Async XLA Ops:
  2.5 33.2 %copy-start = (bf16[16,2048]{1,0:T(8,128)(2,1)S(1)}, bf16[16,2048]{1,0:T(8,128)(2,1)}, u32[]{:S(2)}) copy-start(bf16[16,2048]{1,0:T(8,128)(2,1)} %get-tuple-element.14.refs_0_) | copy-start | bytes 196612
  2.5 33.2 %all-to-all-start = ((bf16[8,2,128,256]{3,2,1,0:T(8,128)(2,1)}), bf16[8,2,128,256]{3,2,1,0:T(8,128)(2,1)S(1)}, u32[]{:S(2)}, u32[]{:S(2)}) async-start(bf16[8,2,128,256]{3,2,1,0:T(8,128)(2,1)} %get-tuple-element.10), calls=%async_computation | async-start | bytes 2097152 | tf_op jit(solution)/shard_map/all_to_all | solution.py:281
  9.9 23.3 %collective-permute-start.2 = (bf16[16,2048]{1,0:T(8,128)(2,1)}, bf16[16,2048]{1,0:T(8,128)(2,1)S(1)}, u32[]{:S(2)}, u32[]{:S(2)}) collective-permute-start(bf16[16,2048]{1,0:T(8,128)(2,1)} %get-tuple-element.14.refs_0_), channel_id=1, source_target_pairs={{24,0},{0,8},{8,16},{16,24},{25,1},{1,9},{9,17},{17,25},{26,2},{2,... | collective-permute-start | bytes 196616 | tf_op jit(solution)/shard_map/ppermute | solution.py:283
  9.9 23.3 %collective-permute-start.1 = (bf16[16,2048]{1,0:T(8,128)(2,1)}, bf16[16,2048]{1,0:T(8,128)(2,1)S(1)}, u32[]{:S(2)}, u32[]{:S(2)}) collective-permute-start(bf16[16,2048]{1,0:T(8,128)(2,1)} %get-tuple-element.14.refs_0_), channel_id=1, source_target_pairs={{16,0},{24,8},{0,16},{8,24},{17,1},{25,9},{1,17},{9,25},{18,2},{26... | collective-permute-start | bytes 196616 | tf_op jit(solution)/shard_map/ppermute | solution.py:283
  11.5 21.7 %collective-permute-start = (bf16[16,2048]{1,0:T(8,128)(2,1)}, bf16[16,2048]{1,0:T(8,128)(2,1)S(1)}, u32[]{:S(2)}, u32[]{:S(2)}) collective-permute-start(bf16[16,2048]{1,0:T(8,128)(2,1)} %get-tuple-element.14.refs_0_), channel_id=1, source_target_pairs={{8,0},{16,8},{24,16},{0,24},{9,1},{17,9},{25,17},{1,25},{10,2},{18... | collective-permute-start | bytes 196616 | tf_op jit(solution)/shard_map/ppermute | solution.py:283
  12.9 0.8 copy-start.1

commit v8 on v7

--- a/solution.py
+++ b/solution.py
@@ -24,14 +24,13 @@
 
 
 def cast_kernel(
-    stripes, at_ref, rx_ref, on_ref, tx_ref, sign_ref, out_ref, bits_ref, st_ref
+    stripes, at_ref, rx_ref, on_ref, sign_ref, out_ref, st_ref
 ):
     out_ref[:, 0] = rx_ref[...].astype(F32).astype(BF)
     out_ref[:, 1] = on_ref[...].astype(F32).astype(BF)
 
     @pl.when(pl.program_id(0) == 0)
     def _():
-        bits_ref[...] = tx_ref[...].astype(F32).astype(BF)
         every = st_ref.shape[0]
         turn = at_ref[0] * (every // stripes)
         row = lax.rem(iota((every, every), 0) + turn, every)
@@ -39,13 +38,12 @@
         st_ref[...] = dot(up, sign_ref[...].astype(F32).astype(BF)).astype(BF)
 
 
-def cast(sizes, at, rx_block, apodization, tx_block, signs_t):
+def cast(sizes, at, rx_block, apodization, signs_t):
     stripes, groups = sizes
     receivers, lines_here = rx_block.shape
     every, events = signs_t.shape
     here = receivers // groups
     split = (groups, here, lines_here)
-    whole = pl.BlockSpec(tx_block.shape, lambda i, at: (0, 0))
     part = pl.BlockSpec((groups // 2, here, lines_here), lambda i, at: (i, 0, 0))
     return pl.pallas_call(
         functools.partial(cast_kernel, stripes),
@@ -55,44 +53,46 @@
             in_specs=[
                 part,
                 part,
-                whole,
                 pl.BlockSpec((every, events // stripes), lambda i, at: (0, at[0])),
             ],
             out_specs=[
                 pl.BlockSpec(
                     (groups // 2, 2, here, lines_here), lambda i, at: (i, 0, 0, 0)
                 ),
-                whole,
                 pl.BlockSpec((every, events // stripes), lambda i, at: (0, 0)),
             ],
         ),
         out_shape=[
             jax.ShapeDtypeStruct((groups, 2, here, lines_here), BF),
-            jax.ShapeDtypeStruct(tx_block.shape, BF),
             jax.ShapeDtypeStruct((every, events // stripes), BF),
         ],
-    )(at, rx_block.reshape(split), apodization.reshape(split), tx_block, signs_t)
+    )(at, rx_block.reshape(split), apodization.reshape(split), signs_t)
 
 
 def decode_kernel(st_ref, enc_ref, delta_ref, dsum_ref, sk_ref, x_ref):
     transmits, events = st_ref.shape
     samples = enc_ref.shape[2]
-    rows, depth = sk_ref.shape
+    _, rows, depth = sk_ref.shape
     diff = samples - L
     width = 32
 
     @pl.when(pl.program_id(0) == 0)
     def _():
-        up = iota((rows, transmits), 0) // G == iota((rows, transmits), 1)
-        tall = dot(up.astype(F32).astype(BF), st_ref[...]).astype(BF)
+        k = iota((rows, transmits), 0) // G
+        talls = []
+        for swap in (k, k + 1 - 2 * (k % 2)):
+            up = (swap == iota((rows, transmits), 1)).astype(F32).astype(BF)
+            talls.append(dot(up, st_ref[...]).astype(BF))
         wide = 256
         for at in range(0, depth, wide):
             row = iota((events, wide), 1) + at
             event = row // RB * 4 + row // G % 2 * 2 + row // (2 * G) % 2
             out = event == iota((events, wide), 0)
-            spread = dot(tall, out.astype(F32).astype(BF))
+            out = out.astype(F32).astype(BF)
             same = iota((rows, wide), 0) % G == iota((rows, wide), 1) % G
-            sk_ref[:, at : at + wide] = jnp.where(same, spread, 0.0).astype(BF)
+            for side, tall in enumerate(talls):
+                spread = jnp.where(same, dot(tall, out), 0.0)
+                sk_ref[side, :, at : at + wide] = spread.astype(BF)
 
     row = iota((1, RB, samples), 1)
     first, inner = row < 2 * G, row % (2 * G) < G
@@ -113,7 +113,7 @@
             x_ref[2 * side + 1, here, :] = high.reshape(width * G, samples)
     deltas = []
     for q in range(RB // G):
-        d = dot(sk_ref[...], x_ref[q])
+        d = dot(sk_ref[q % 2], x_ref[q])
         low, high = d[:, :diff], d[:, L:]
         deltas.append(((high - low) * 0.5).reshape(transmits // 2, 2 * G, diff))
         mean = jnp.sum((high + low).reshape(transmits // 2, 2 * G, diff), axis=0)
@@ -122,10 +122,14 @@
     evens, odds = [], []
     for side in range(2):
         low, high = deltas[2 * side], deltas[2 * side + 1]
-        evens.append(jnp.where(upper, low, pltpu.roll(high, G, 1)))
-        odds.append(jnp.where(upper, pltpu.roll(low, G, 1), high))
+        evens.append(jnp.where(upper, low, high))
+        odds.append(jnp.where(upper, high, low))
     delta_ref[:, 0] = jnp.concatenate(evens, axis=1).astype(BF)
-    delta_ref[:, 1] = jnp.concatenate(odds, axis=1).astype(BF)
+    swapped = jnp.concatenate(odds, axis=1).astype(BF)
+    inner = iota((1, RB, diff), 1) % (2 * G) < G
+    delta_ref[:, 1] = jnp.where(
+        inner, pltpu.roll(swapped, RB - G, 1), pltpu.roll(swapped, G, 1)
+    )
 
 
 def decode(st, encoded):
@@ -148,7 +152,7 @@
             jax.ShapeDtypeStruct((receivers, diff), F32),
         ],
         scratch_shapes=[
-            pltpu.VMEM((transmits * G, events * G), BF),
+            pltpu.VMEM((2, transmits * G, events * G), BF),
             pltpu.VMEM((RB // G, events * G, samples), BF),
         ],
         compiler_params=pltpu.CompilerParams(vmem_limit_bytes=50 * 2**20),
@@ -277,10 +281,10 @@
     events, transmits = signs.shape
     receivers = rx_block.shape[0]
     at = lax.axis_index("tx").astype(jnp.int32).reshape(1)
-    masks, own, st = cast(sizes, at, rx_block, apodization, tx_block, signs.T)
+    masks, st = cast(sizes, at, rx_block, apodization, signs.T)
     masks = lax.all_to_all(masks, "img", 0, 0, tiled=True)
-    tx_bits = [own] + [
-        lax.ppermute(own, "tx", [((t + d) % stripes, t) for t in range(stripes)])
+    tx_bits = [tx_block] + [
+        lax.ppermute(tx_block, "tx", [((t + d) % stripes, t) for t in range(stripes)])
         for d in range(1, stripes)
     ]
     delta, dsum = decode(st, encoded)

time: 78.1 us -> 77.9 us (level)
  starting transfers between devices: 10.4 us -> 9.29 us
    ppermute x3, starting transfers between devices: 2.95 us -> 2 us  [on_device(): lax.ppermute(tx_block, 'tx', [((t + d) % stripes, t) for t in range(strip...]
  transfers between devices with their start and end apart: 4 -> 4, of which waited for: 1 -> 1; matrix products, arithmetic and copies ran while one was open for 0% -> 0% of each run, Pallas kernels for 25% -> 26%
where the time goes in v8:
time: 77.9 us; the launch traced here: 77.4 us
  Pallas kernels  43.7 us (56%)
  blocking collectives  19.8 us (25%)
  starting transfers between devices  9.29 us (12%)
  waiting for transfers between devices  3.21 us (4%)
    pallas_call x1, Pallas kernels, beamform(): pl.pallas_call(functools.partial(beam_kernel, scale), grid=(groups // som...  21.5 us
    pallas_call x1, Pallas kernels, decode(): pl.pallas_call(decode_kernel, grid=(receivers // RB,), in_specs=[pl.Block...  19.8 us
    all_to_all x1, blocking collectives, on_device(): parts = lax.all_to_all(parts, ('tx', 'img'), 0, 0, tiled=True)  19.8 us
    all_to_all x1, starting transfers between devices, on_device(): masks = lax.all_to_all(masks, 'img', 0, 0, tiled=True)  7.29 us
    all_to_all x1, waiting for transfers between devices, on_device(): masks = lax.all_to_all(masks, 'img', 0, 0, tiled=True)  3.2 us
    pallas_call x1, Pallas kernels, cast(): pl.pallas_call(functools.partial(cast_kernel, stripes), grid_spec=pltpu.P...  2.44 us
    ppermute x3, starting transfers between devices, on_device(): lax.ppermute(tx_block, 'tx', [((t + d) % stripes, t) for t in range(strip...  2 us
  transfers between devices with their start and end apart: 4, of which 1 were waited for; matrix products, arithmetic and copies ran while one was open for 0% of the time, Pallas kernels for 26%

profile of v8, /device:TPU:0, one launch (start us, length us, event | category | flops | bytes accessed | tf_op | source)
XLA Modules:
  0.0 77.4 jit_solution(11807011526288241397)
XLA Ops:
  0.0 0.0 copy-start
  0.0 2.4 %shard_map.55 = (bf16[8,2,128,256]{3,2,1,0:T(8,128)(2,1)}, bf16[64,256]{1,0:T(8,128)(2,1)}) custom-call(s32[1]{0:T(128)} %bitcast.at_ref, s32[8,128,256]{2,1,0:T(8,128)} %bitcast.8, s32[8,128,256]{2,1,0:T(8,128)} %bitcast.9, s32[64,1024]{1,0:T(8,128)} %bitcast.10), custom_call_target="tpu_custom_call" | custom-call | tf_op jit(solution)/shard_map/pallas_call | solution.py:48
  2.4 7.3 %all-to-all-start = ((bf16[8,2,128,256]{3,2,1,0:T(8,128)(2,1)}), bf16[8,2,128,256]{3,2,1,0:T(8,128)(2,1)S(1)}, u32[]{:S(2)}, u32[]{:S(2)}) async-start(bf16[8,2,128,256]{3,2,1,0:T(8,128)(2,1)} %get-tuple-element.9), calls=%async_computation | async-start | bytes 2097152 | tf_op jit(solution)/shard_map/all_to_all | solution.py:285
  9.7 1.5 %collective-permute-start.1 = (s32[16,2048]{1,0:T(8,128)}, s32[16,2048]{1,0:T(8,128)S(1)}, u32[]{:S(2)}, u32[]{:S(2)}) collective-permute-start(s32[16,2048]{1,0:T(8,128)} %refs_0_.1), channel_id=1, source_target_pairs={{16,0},{24,8},{0,16},{8,24},{17,1},{25,9},{1,17},{9,25},{18,2},{26... | collective-permute-start | bytes 393224 | tf_op jit(solution)/shard_map/ppermute | solution.py:287
  11.2 0.0 collective-permute-start
  11.2 0.5 collective-permute-start.2
  11.7 0.0 copy-start.1
  11.7 0.8 copy-done.1
  12.5 19.8 %shard_map.56 = (bf16[32,2,128,384]{3,2,1,0:T(8,128)(2,1)}, f32[128,384]{1,0:T(8,128)S(1)}) custom-call(bf16[64,256]{1,0:T(8,128)(2,1)S(1)} %copy-done.1, bf16[256,128,512]{2,1,0:T(8,128)(2,1)} %enc_ref.1), custom_call_target="tpu_custom_call" | custom-call | flops 17179869184 | bytes 39845888 | tf_op jit(solution)/shard_map/pallas_call | solution.py:139
  32.3 0.0 collective-permute-done.1.refs_2_
  32.3 0.0 collective-permute-done.refs_1_
  32.3 0.0 collective-permute-done.2.refs_3_
  32.3 3.2 %all-to-all-done.mask_ref = bf16[8,2,128,256]{3,2,1,0:T(8,128)(2,1)S(1)} async-done(((bf16[8,2,128,256]{3,2,1,0:T(8,128)(2,1)}), bf16[8,2,128,256]{3,2,1,0:T(8,128)(2,1)S(1)}, u32[]{:S(2)}, u32[]{:S(2)}) %all-to-all-start) | async-done | bytes 1048608 | tf_op jit(solution)/shard_map/all_to_all | solution.py:285
  35.5 0.0 copy-done
  35.5 21.5 %shard_map.57 = bf16[4,8,32,256]{3,2,1,0:T(8,128)(2,1)S(1)} custom-call(bf16[8,2,128,256]{3,2,1,0:T(8,128)(2,1)S(1)} %all-to-all-done.mask_ref, bf16[64,128,384]{2,1,0:T(8,128)(2,1)} %bitcast.11, f32[128,384]{1,0:T(8,128)S(1)} %get-tuple-element.12.dsum_ref, s32[16,2048]{1,0:T(8,128)S(1)} %copy-done, s32[16,2048]{1,0:T(8,128)S(1)} %collective-permute-done.refs_1_, ...), custom_call_target="tpu_custom_call" | custom-call | flops 12884901888 | bytes 6291456 | tf_op jit(solution)/shard_map/pallas_call | solution.py:244
  57.0 19.8 %all_to_all.10 = bf16[32,32,256]{2,1,0:T(8,128)(2,1)S(1)} all-to-all(bf16[32,32,256]{2,1,0:T(8,128)(2,1)S(1)} %bitcast.7), channel_id=1, replica_groups=mesh['tx'=4,'img'=8] {'tx','img'}, dimensions={0} | all-to-all | bytes 1048576 | tf_op jit(solution)/shard_map/all_to_all | solution.py:295
  76.7 0.7 convert_reduce_fusion
Async XLA Ops:
  0.0 35.5 %copy-start = (s32[16,2048]{1,0:T(8,128)S(1)}, s32[16,2048]{1,0:T(8,128)}, u32[]{:S(2)}) copy-start(s32[16,2048]{1,0:T(8,128)} %refs_0_.1) | copy-start | bytes 393220
  2.4 33.1 %all-to-all-start = ((bf16[8,2,128,256]{3,2,1,0:T(8,128)(2,1)}), bf16[8,2,128,256]{3,2,1,0:T(8,128)(2,1)S(1)}, u32[]{:S(2)}, u32[]{:S(2)}) async-start(bf16[8,2,128,256]{3,2,1,0:T(8,128)(2,1)} %get-tuple-element.9), calls=%async_computation | async-start | bytes 2097152 | tf_op jit(solution)/shard_map/all_to_all | solution.py:285
  9.7 22.6 %collective-permute-start.1 = (s32[16,2048]{1,0:T(8,128)}, s32[16,2048]{1,0:T(8,128)S(1)}, u32[]{:S(2)}, u32[]{:S(2)}) collective-permute-start(s32[16,2048]{1,0:T(8,128)} %refs_0_.1), channel_id=1, source_target_pairs={{16,0},{24,8},{0,16},{8,24},{17,1},{25,9},{1,17},{9,25},{18,2},{26... | collective-permute-start | bytes 393224 | tf_op jit(solution)/shard_map/ppermute | solution.py:287
  11.2 21.1 %collective-permute-start = (s32[16,2048]{1,0:T(8,128)}, s32[16,2048]{1,0:T(8,128)S(1)}, u32[]{:S(2)}, u32[]{:S(2)}) collective-permute-start(s32[16,2048]{1,0:T(8,128)} %refs_0_.1), channel_id=1, source_target_pairs={{8,0},{16,8},{24,16},{0,24},{9,1},{17,9},{25,17},{1,25},{10,2},{18... | collective-permute-start | bytes 393224 | tf_op jit(solution)/shard_map/ppermute | solution.py:287
  11.2 21.1 %collective-permute-start.2 = (s32[16,2048]{1,0:T(8,128)}, s32[16,2048]{1,0:T(8,128)S(1)}, u32[]{:S(2)}, u32[]{:S(2)}) collective-permute-start(s32[16,2048]{1,0:T(8,128)} %refs_0_.1), channel_id=1, source_target_pairs={{24,0},{0,8},{8,16},{16,24},{25,1},{1,9},{9,17},{17,25},{26,2},{2,... | collective-permute-start | bytes 393224 | tf_op jit(solution)/shard_map/ppermute | solution.py:287
  11.7 0.8 copy-start.1

commit v9 on v7

--- a/solution.py
+++ b/solution.py
@@ -74,7 +74,9 @@
     )(at, rx_block.reshape(split), apodization.reshape(split), tx_block, signs_t)
 
 
-def decode_kernel(st_ref, enc_ref, delta_ref, dsum_ref, sk_ref, x_ref):
+def decode_kernel(
+    st_ref, enc_ref, delta_ref, dsum_ref, sk_ref, lower_ref, upper_ref
+):
     transmits, events = st_ref.shape
     samples = enc_ref.shape[2]
     rows, depth = sk_ref.shape
@@ -96,28 +98,39 @@
 
     row = iota((1, RB, samples), 1)
     first, inner = row < 2 * G, row % (2 * G) < G
-    for at in range(0, events, width):
+
+    def lay_out(x_ref, side, at):
         piece = enc_ref[at : at + width].reshape(width // 4, 4, RB, samples)
         a, b, c, d = (piece[:, e] for e in range(4))
         here = slice(at * G, (at + width) * G)
-        for side in range(2):
-            if side == 0:
-                ab = jnp.where(first, a, pltpu.roll(b, 2 * G, 1))
-                cd = jnp.where(first, c, pltpu.roll(d, 2 * G, 1))
-            else:
-                ab = jnp.where(first, pltpu.roll(a, 2 * G, 1), b)
-                cd = jnp.where(first, pltpu.roll(c, 2 * G, 1), d)
-            low = jnp.where(inner, ab, pltpu.roll(cd, G, 1))
-            high = jnp.where(inner, pltpu.roll(ab, RB - G, 1), cd)
-            x_ref[2 * side, here, :] = low.reshape(width * G, samples)
-            x_ref[2 * side + 1, here, :] = high.reshape(width * G, samples)
+        if side == 0:
+            ab = jnp.where(first, a, pltpu.roll(b, 2 * G, 1))
+            cd = jnp.where(first, c, pltpu.roll(d, 2 * G, 1))
+        else:
+            ab = jnp.where(first, pltpu.roll(a, 2 * G, 1), b)
+            cd = jnp.where(first, pltpu.roll(c, 2 * G, 1), d)
+        low = jnp.where(inner, ab, pltpu.roll(cd, G, 1))
+        high = jnp.where(inner, pltpu.roll(ab, RB - G, 1), cd)
+        x_ref[0, here, :] = low.reshape(width * G, samples)
+        x_ref[1, here, :] = high.reshape(width * G, samples)
+
     deltas = []
-    for q in range(RB // G):
-        d = dot(sk_ref[...], x_ref[q])
+
+    def product(q, x):
+        d = dot(sk_ref[...], x)
         low, high = d[:, :diff], d[:, L:]
         deltas.append(((high - low) * 0.5).reshape(transmits // 2, 2 * G, diff))
         mean = jnp.sum((high + low).reshape(transmits // 2, 2 * G, diff), axis=0)
         dsum_ref[q * G : (q + 1) * G, :] = (mean[:G] + mean[G:]) * 0.5
+
+    for at in range(0, events, width):
+        lay_out(lower_ref, 0, at)
+    for q in range(2):
+        for at in range(q * events // 2, (q + 1) * events // 2, width):
+            lay_out(upper_ref, 1, at)
+        product(q, lower_ref[q])
+    for q in range(2):
+        product(2 + q, upper_ref[q])
     upper = iota((1, 2 * G, diff), 1) < G
     evens, odds = [], []
     for side in range(2):
@@ -149,7 +162,8 @@
         ],
         scratch_shapes=[
             pltpu.VMEM((transmits * G, events * G), BF),
-            pltpu.VMEM((RB // G, events * G, samples), BF),
+            pltpu.VMEM((2, events * G, samples), BF),
+            pltpu.VMEM((2, events * G, samples), BF),
         ],
         compiler_params=pltpu.CompilerParams(vmem_limit_bytes=50 * 2**20),
         cost_estimate=pl.CostEstimate(

time: 78.1 us -> 78.1 us (level)
  no operation moved by 1% of the time
where the time goes in v9:
time: 78.1 us; the launch traced here: 77.6 us
  Pallas kernels  43.5 us (56%)
  blocking collectives  19.8 us (25%)
  starting transfers between devices  10.4 us (13%)
  waiting for transfers between devices  2.45 us (3%)
    pallas_call x1, Pallas kernels, beamform(): pl.pallas_call(functools.partial(beam_kernel, scale), grid=(groups // som...  21.5 us
    all_to_all x1, blocking collectives, on_device(): parts = lax.all_to_all(parts, ('tx', 'img'), 0, 0, tiled=True)  19.8 us
    pallas_call x1, Pallas kernels, decode(): pl.pallas_call(decode_kernel, grid=(receivers // RB,), in_specs=[pl.Block...  19.6 us
    all_to_all x1, starting transfers between devices, on_device(): masks = lax.all_to_all(masks, 'img', 0, 0, tiled=True)  7.44 us
    ppermute x3, starting transfers between devices, on_device(): lax.ppermute(own, 'tx', [((t + d) % stripes, t) for t in range(stripes)])  2.95 us
    pallas_call x1, Pallas kernels, cast(): pl.pallas_call(functools.partial(cast_kernel, stripes), grid_spec=pltpu.P...  2.46 us
    all_to_all x1, waiting for transfers between devices, on_device(): masks = lax.all_to_all(masks, 'img', 0, 0, tiled=True)  2.44 us
  transfers between devices with their start and end apart: 4, of which 1 were waited for; matrix products, arithmetic and copies ran while one was open for 0% of the time, Pallas kernels for 25%

profile of v9, /device:TPU:0, one launch (start us, length us, event | category | flops | bytes accessed | tf_op | source)
XLA Modules:
  0.0 77.6 jit_solution(671069785112088850)
XLA Ops:
  0.0 2.5 %shard_map.55 = (bf16[8,2,128,256]{3,2,1,0:T(8,128)(2,1)}, bf16[16,2048]{1,0:T(8,128)(2,1)}, bf16[64,256]{1,0:T(8,128)(2,1)}) custom-call(s32[1]{0:T(128)} %bitcast.at_ref, s32[8,128,256]{2,1,0:T(8,128)} %bitcast.8, s32[8,128,256]{2,1,0:T(8,128)} %bitcast.9, s32[16,2048]{1,0:T(8,128)} %tx_ref.1, s32[64,1024]{1,0:T(8,128)} %bitcast.10), custom_call_target="tpu_custom_call" | custom-call | tf_op jit(solution)/shard_map/pallas_call | solution.py:50
  2.5 0.0 copy-start
  2.5 7.4 %all-to-all-start = ((bf16[8,2,128,256]{3,2,1,0:T(8,128)(2,1)}), bf16[8,2,128,256]{3,2,1,0:T(8,128)(2,1)S(1)}, u32[]{:S(2)}, u32[]{:S(2)}) async-start(bf16[8,2,128,256]{3,2,1,0:T(8,128)(2,1)} %get-tuple-element.10), calls=%async_computation | async-start | bytes 2097152 | tf_op jit(solution)/shard_map/all_to_all | solution.py:295
  9.9 0.0 collective-permute-start.2
  9.9 1.6 %collective-permute-start.1 = (bf16[16,2048]{1,0:T(8,128)(2,1)}, bf16[16,2048]{1,0:T(8,128)(2,1)S(1)}, u32[]{:S(2)}, u32[]{:S(2)}) collective-permute-start(bf16[16,2048]{1,0:T(8,128)(2,1)} %get-tuple-element.14.refs_0_), channel_id=1, source_target_pairs={{16,0},{24,8},{0,16},{8,24},{17,1},{25,9},{1,17},{9,25},{18,2},{26... | collective-permute-start | bytes 196616 | tf_op jit(solution)/shard_map/ppermute | solution.py:297
  11.5 1.4 %collective-permute-start = (bf16[16,2048]{1,0:T(8,128)(2,1)}, bf16[16,2048]{1,0:T(8,128)(2,1)S(1)}, u32[]{:S(2)}, u32[]{:S(2)}) collective-permute-start(bf16[16,2048]{1,0:T(8,128)(2,1)} %get-tuple-element.14.refs_0_), channel_id=1, source_target_pairs={{8,0},{16,8},{24,16},{0,24},{9,1},{17,9},{25,17},{1,25},{10,2},{18... | collective-permute-start | bytes 196616 | tf_op jit(solution)/shard_map/ppermute | solution.py:297
  12.9 0.0 copy-start.1
  12.9 0.8 copy-done.1
  13.6 19.6 %shard_map.56 = (bf16[32,2,128,384]{3,2,1,0:T(8,128)(2,1)}, f32[128,384]{1,0:T(8,128)S(1)}) custom-call(bf16[64,256]{1,0:T(8,128)(2,1)S(1)} %copy-done.1, bf16[256,128,512]{2,1,0:T(8,128)(2,1)} %enc_ref.1), custom_call_target="tpu_custom_call" | custom-call | flops 17179869184 | bytes 39845888 | tf_op jit(solution)/shard_map/pallas_call | solution.py:148
  33.2 0.0 collective-permute-done.2.refs_3_
  33.2 0.0 collective-permute-done.1.refs_2_
  33.2 0.0 collective-permute-done.refs_1_
  33.2 2.4 %all-to-all-done.mask_ref = bf16[8,2,128,256]{3,2,1,0:T(8,128)(2,1)S(1)} async-done(((bf16[8,2,128,256]{3,2,1,0:T(8,128)(2,1)}), bf16[8,2,128,256]{3,2,1,0:T(8,128)(2,1)S(1)}, u32[]{:S(2)}, u32[]{:S(2)}) %all-to-all-start) | async-done | bytes 1048608 | tf_op jit(solution)/shard_map/all_to_all | solution.py:295
  35.7 0.0 copy-done
  35.7 21.5 %shard_map.57 = bf16[4,8,32,256]{3,2,1,0:T(8,128)(2,1)S(1)} custom-call(bf16[8,2,128,256]{3,2,1,0:T(8,128)(2,1)S(1)} %all-to-all-done.mask_ref, bf16[64,128,384]{2,1,0:T(8,128)(2,1)} %bitcast.11, f32[128,384]{1,0:T(8,128)S(1)} %get-tuple-element.13.dsum_ref, bf16[16,2048]{1,0:T(8,128)(2,1)S(1)} %copy-done, ...), custom_call_target="tpu_custom_call" | custom-call | flops 12884901888 | bytes 6291456 | tf_op jit(solution)/shard_map/pallas_call | solution.py:254
  57.2 19.8 %all_to_all.10 = bf16[32,32,256]{2,1,0:T(8,128)(2,1)S(1)} all-to-all(bf16[32,32,256]{2,1,0:T(8,128)(2,1)S(1)} %bitcast.7), channel_id=1, replica_groups=mesh['tx'=4,'img'=8] {'tx','img'}, dimensions={0} | all-to-all | bytes 1048576 | tf_op jit(solution)/shard_map/all_to_all | solution.py:305
  76.9 0.7 convert_reduce_fusion
Async XLA Ops:
  2.5 33.2 %copy-start = (bf16[16,2048]{1,0:T(8,128)(2,1)S(1)}, bf16[16,2048]{1,0:T(8,128)(2,1)}, u32[]{:S(2)}) copy-start(bf16[16,2048]{1,0:T(8,128)(2,1)} %get-tuple-element.14.refs_0_) | copy-start | bytes 196612
  2.5 33.2 %all-to-all-start = ((bf16[8,2,128,256]{3,2,1,0:T(8,128)(2,1)}), bf16[8,2,128,256]{3,2,1,0:T(8,128)(2,1)S(1)}, u32[]{:S(2)}, u32[]{:S(2)}) async-start(bf16[8,2,128,256]{3,2,1,0:T(8,128)(2,1)} %get-tuple-element.10), calls=%async_computation | async-start | bytes 2097152 | tf_op jit(solution)/shard_map/all_to_all | solution.py:295
  9.9 23.3 %collective-permute-start.2 = (bf16[16,2048]{1,0:T(8,128)(2,1)}, bf16[16,2048]{1,0:T(8,128)(2,1)S(1)}, u32[]{:S(2)}, u32[]{:S(2)}) collective-permute-start(bf16[16,2048]{1,0:T(8,128)(2,1)} %get-tuple-element.14.refs_0_), channel_id=1, source_target_pairs={{24,0},{0,8},{8,16},{16,24},{25,1},{1,9},{9,17},{17,25},{26,2},{2,... | collective-permute-start | bytes 196616 | tf_op jit(solution)/shard_map/ppermute | solution.py:297
  9.9 23.3 %collective-permute-start.1 = (bf16[16,2048]{1,0:T(8,128)(2,1)}, bf16[16,2048]{1,0:T(8,128)(2,1)S(1)}, u32[]{:S(2)}, u32[]{:S(2)}) collective-permute-start(bf16[16,2048]{1,0:T(8,128)(2,1)} %get-tuple-element.14.refs_0_), channel_id=1, source_target_pairs={{16,0},{24,8},{0,16},{8,24},{17,1},{25,9},{1,17},{9,25},{18,2},{26... | collective-permute-start | bytes 196616 | tf_op jit(solution)/shard_map/ppermute | solution.py:297
  11.5 21.8 %collective-permute-start = (bf16[16,2048]{1,0:T(8,128)(2,1)}, bf16[16,2048]{1,0:T(8,128)(2,1)S(1)}, u32[]{:S(2)}, u32[]{:S(2)}) collective-permute-start(bf16[16,2048]{1,0:T(8,128)(2,1)} %get-tuple-element.14.refs_0_), channel_id=1, source_target_pairs={{8,0},{16,8},{24,16},{0,24},{9,1},{17,9},{25,17},{1,25},{10,2},{18... | collective-permute-start | bytes 196616 | tf_op jit(solution)/shard_map/ppermute | solution.py:297
  12.9 0.8 copy-start.1

commit v10 on v7

--- a/solution.py
+++ b/solution.py
@@ -10,6 +10,7 @@
 
 L = 128
 G = 4
+COPIES = 4
 RB = 16
 BF = jnp.bfloat16
 F32 = jnp.float32
@@ -74,9 +75,10 @@
     )(at, rx_block.reshape(split), apodization.reshape(split), tx_block, signs_t)
 
 
-def decode_kernel(st_ref, enc_ref, delta_ref, dsum_ref, sk_ref, x_ref):
+def decode_kernel(st_ref, *refs):
+    *enc_refs, delta_ref, dsum_ref, sk_ref, x_ref = refs
     transmits, events = st_ref.shape
-    samples = enc_ref.shape[2]
+    share, _, samples = enc_refs[0].shape
     rows, depth = sk_ref.shape
     diff = samples - L
     width = 32
@@ -97,7 +99,8 @@
     row = iota((1, RB, samples), 1)
     first, inner = row < 2 * G, row % (2 * G) < G
     for at in range(0, events, width):
-        piece = enc_ref[at : at + width].reshape(width // 4, 4, RB, samples)
+        piece = enc_refs[at // share][at % share : at % share + width]
+        piece = piece.reshape(width // 4, 4, RB, samples)
         a, b, c, d = (piece[:, e] for e in range(4))
         here = slice(at * G, (at + width) * G)
         for side in range(2):
@@ -137,7 +140,12 @@
         grid=(receivers // RB,),
         in_specs=[
             pl.BlockSpec((transmits, events), lambda g: (0, 0)),
-            pl.BlockSpec((events, RB, samples), lambda g: (0, g, 0)),
+        ]
+        + [
+            pl.BlockSpec(
+                (events // COPIES, RB, samples), functools.partial(lambda c, g: (c, g, 0), c)
+            )
+            for c in range(COPIES)
         ],
         out_specs=[
             pl.BlockSpec((transmits // 2, 2, RB, diff), lambda g: (0, 0, g, 0)),
@@ -158,7 +166,7 @@
             + transmits * receivers * diff * 2,
             transcendentals=0,
         ),
-    )(st, encoded)
+    )(st, *[encoded] * COPIES)
 
 
 def beam_kernel(scale, mask_ref, delta_ref, dsum_ref, *refs):

time: 78.1 us -> 77.8 us (level)
  no operation moved by 1% of the time
where the time goes in v10:
time: 77.8 us; the launch traced here: 77.5 us
  Pallas kernels  43.4 us (56%)
  blocking collectives  19.8 us (25%)
  starting transfers between devices  10.3 us (13%)
  waiting for transfers between devices  2.62 us (3%)
    pallas_call x1, Pallas kernels, beamform(): pl.pallas_call(functools.partial(beam_kernel, scale), grid=(groups // som...  21.5 us
    all_to_all x1, blocking collectives, on_device(): parts = lax.all_to_all(parts, ('tx', 'img'), 0, 0, tiled=True)  19.8 us
    pallas_call x1, Pallas kernels, decode(): pl.pallas_call(decode_kernel, grid=(receivers // RB,), in_specs=[pl.Block...  19.4 us
    all_to_all x1, starting transfers between devices, on_device(): masks = lax.all_to_all(masks, 'img', 0, 0, tiled=True)  7.31 us
    ppermute x3, starting transfers between devices, on_device(): lax.ppermute(own, 'tx', [((t + d) % stripes, t) for t in range(stripes)])  2.95 us
    all_to_all x1, waiting for transfers between devices, on_device(): masks = lax.all_to_all(masks, 'img', 0, 0, tiled=True)  2.61 us
    pallas_call x1, Pallas kernels, cast(): pl.pallas_call(functools.partial(cast_kernel, stripes), grid_spec=pltpu.P...  2.46 us
  transfers between devices with their start and end apart: 4, of which 1 were waited for; matrix products, arithmetic and copies ran while one was open for 0% of the time, Pallas kernels for 25%

profile of v10, /device:TPU:0, one launch (start us, length us, event | category | flops | bytes accessed | tf_op | source)
XLA Modules:
  0.0 77.5 jit_solution(7030144671940640844)
XLA Ops:
  0.0 2.5 %shard_map.55 = (bf16[8,2,128,256]{3,2,1,0:T(8,128)(2,1)}, bf16[16,2048]{1,0:T(8,128)(2,1)}, bf16[64,256]{1,0:T(8,128)(2,1)}) custom-call(s32[1]{0:T(128)} %bitcast.at_ref, s32[8,128,256]{2,1,0:T(8,128)} %bitcast.8, s32[8,128,256]{2,1,0:T(8,128)} %bitcast.9, s32[16,2048]{1,0:T(8,128)} %tx_ref.1, s32[64,1024]{1,0:T(8,128)} %bitcast.10), custom_call_target="tpu_custom_call" | custom-call | tf_op jit(solution)/shard_map/pallas_call | solution.py:51
  2.5 7.3 %all-to-all-start = ((bf16[8,2,128,256]{3,2,1,0:T(8,128)(2,1)}), bf16[8,2,128,256]{3,2,1,0:T(8,128)(2,1)S(1)}, u32[]{:S(2)}, u32[]{:S(2)}) async-start(bf16[8,2,128,256]{3,2,1,0:T(8,128)(2,1)} %get-tuple-element.10), calls=%async_computation | async-start | bytes 2097152 | tf_op jit(solution)/shard_map/all_to_all | solution.py:289
  9.8 0.0 collective-permute-start.2
  9.8 1.6 %collective-permute-start.1 = (bf16[16,2048]{1,0:T(8,128)(2,1)}, bf16[16,2048]{1,0:T(8,128)(2,1)S(1)}, u32[]{:S(2)}, u32[]{:S(2)}) collective-permute-start(bf16[16,2048]{1,0:T(8,128)(2,1)} %get-tuple-element.14.refs_0_), channel_id=1, source_target_pairs={{16,0},{24,8},{0,16},{8,24},{17,1},{25,9},{1,17},{9,25},{18,2},{26... | collective-permute-start | bytes 196616 | tf_op jit(solution)/shard_map/ppermute | solution.py:291
  11.3 1.4 %collective-permute-start = (bf16[16,2048]{1,0:T(8,128)(2,1)}, bf16[16,2048]{1,0:T(8,128)(2,1)S(1)}, u32[]{:S(2)}, u32[]{:S(2)}) collective-permute-start(bf16[16,2048]{1,0:T(8,128)(2,1)} %get-tuple-element.14.refs_0_), channel_id=1, source_target_pairs={{8,0},{16,8},{24,16},{0,24},{9,1},{17,9},{25,17},{1,25},{10,2},{18... | collective-permute-start | bytes 196616 | tf_op jit(solution)/shard_map/ppermute | solution.py:291
  12.7 0.0 copy-start
  12.7 0.8 copy-done
  13.5 0.0 copy-start.1
  13.5 19.4 %shard_map.56 = (bf16[32,2,128,384]{3,2,1,0:T(8,128)(2,1)}, f32[128,384]{1,0:T(8,128)S(1)}) custom-call(bf16[64,256]{1,0:T(8,128)(2,1)S(1)} %copy-done, bf16[256,128,512]{2,1,0:T(8,128)(2,1)} %refs_3_.1, bf16[256,128,512]{2,1,0:T(8,128)(2,1)} %refs_3_.1, bf16[256,128,512]{2,1,0:T(8,128)(2,1)} %refs_3_.1, bf16[256,128,512]{2,1,0:T(8,128)(2,1)} %refs_3_.1), custom_call_target="tpu_custom_call" | custom-call | flops 17179869184 | bytes 39845888 | tf_op jit(solution)/shard_map/pallas_call | solution.py:138
  32.9 0.0 collective-permute-done.2.refs_3_
  32.9 0.0 collective-permute-done.1.refs_2_
  32.9 0.0 collective-permute-done.refs_1_
  32.9 2.6 %all-to-all-done.mask_ref = bf16[8,2,128,256]{3,2,1,0:T(8,128)(2,1)S(1)} async-done(((bf16[8,2,128,256]{3,2,1,0:T(8,128)(2,1)}), bf16[8,2,128,256]{3,2,1,0:T(8,128)(2,1)S(1)}, u32[]{:S(2)}, u32[]{:S(2)}) %all-to-all-start) | async-done | bytes 1048608 | tf_op jit(solution)/shard_map/all_to_all | solution.py:289
  35.5 0.0 copy-done.1
  35.5 21.5 %shard_map.57 = bf16[4,8,32,256]{3,2,1,0:T(8,128)(2,1)S(1)} custom-call(bf16[8,2,128,256]{3,2,1,0:T(8,128)(2,1)S(1)} %all-to-all-done.mask_ref, bf16[64,128,384]{2,1,0:T(8,128)(2,1)} %bitcast.11, f32[128,384]{1,0:T(8,128)S(1)} %get-tuple-element.13.dsum_ref, bf16[16,2048]{1,0:T(8,128)(2,1)S(1)} %copy-done.1, ...), custom_call_target="tpu_custom_call" | custom-call | flops 12884901888 | bytes 6291456 | tf_op jit(solution)/shard_map/pallas_call | solution.py:248
  57.0 19.8 %all_to_all.10 = bf16[32,32,256]{2,1,0:T(8,128)(2,1)S(1)} all-to-all(bf16[32,32,256]{2,1,0:T(8,128)(2,1)S(1)} %bitcast.7), channel_id=1, replica_groups=mesh['tx'=4,'img'=8] {'tx','img'}, dimensions={0} | all-to-all | bytes 1048576 | tf_op jit(solution)/shard_map/all_to_all | solution.py:299
  76.8 0.7 convert_reduce_fusion
Async XLA Ops:
  2.5 33.1 %all-to-all-start = ((bf16[8,2,128,256]{3,2,1,0:T(8,128)(2,1)}), bf16[8,2,128,256]{3,2,1,0:T(8,128)(2,1)S(1)}, u32[]{:S(2)}, u32[]{:S(2)}) async-start(bf16[8,2,128,256]{3,2,1,0:T(8,128)(2,1)} %get-tuple-element.10), calls=%async_computation | async-start | bytes 2097152 | tf_op jit(solution)/shard_map/all_to_all | solution.py:289
  9.8 23.1 %collective-permute-start.2 = (bf16[16,2048]{1,0:T(8,128)(2,1)}, bf16[16,2048]{1,0:T(8,128)(2,1)S(1)}, u32[]{:S(2)}, u32[]{:S(2)}) collective-permute-start(bf16[16,2048]{1,0:T(8,128)(2,1)} %get-tuple-element.14.refs_0_), channel_id=1, source_target_pairs={{24,0},{0,8},{8,16},{16,24},{25,1},{1,9},{9,17},{17,25},{26,2},{2,... | collective-permute-start | bytes 196616 | tf_op jit(solution)/shard_map/ppermute | solution.py:291
  9.8 23.1 %collective-permute-start.1 = (bf16[16,2048]{1,0:T(8,128)(2,1)}, bf16[16,2048]{1,0:T(8,128)(2,1)S(1)}, u32[]{:S(2)}, u32[]{:S(2)}) collective-permute-start(bf16[16,2048]{1,0:T(8,128)(2,1)} %get-tuple-element.14.refs_0_), channel_id=1, source_target_pairs={{16,0},{24,8},{0,16},{8,24},{17,1},{25,9},{1,17},{9,25},{18,2},{26... | collective-permute-start | bytes 196616 | tf_op jit(solution)/shard_map/ppermute | solution.py:291
  11.3 21.6 %collective-permute-start = (bf16[16,2048]{1,0:T(8,128)(2,1)}, bf16[16,2048]{1,0:T(8,128)(2,1)S(1)}, u32[]{:S(2)}, u32[]{:S(2)}) collective-permute-start(bf16[16,2048]{1,0:T(8,128)(2,1)} %get-tuple-element.14.refs_0_), channel_id=1, source_target_pairs={{8,0},{16,8},{24,16},{0,24},{9,1},{17,9},{25,17},{1,25},{10,2},{18... | collective-permute-start | bytes 196616 | tf_op jit(solution)/shard_map/ppermute | solution.py:291
  12.7 0.8 copy-start
  13.5 22.1 %copy-start.1 = (bf16[16,2048]{1,0:T(8,128)(2,1)S(1)}, bf16[16,2048]{1,0:T(8,128)(2,1)}, u32[]{:S(2)}) copy-start(bf16[16,2048]{1,0:T(8,128)(2,1)} %get-tuple-element.14.refs_0_) | copy-start | bytes 196612

commit v11 on v10

--- a/solution.py
+++ b/solution.py
@@ -184,11 +184,11 @@
             ].T
 
     def product(x_from, k0, beside):
-        for g in range(groups):
-            for k in range(g * half // groups, (g + 1) * half // groups):
+        for g in range(0, groups, 2):
+            for k in range(g * half // groups, (g + 2) * half // groups):
                 beside(k)
-            here = slice(g * wide, (g + 1) * wide)
-            y = dot(x_from[...], a_ref[:, here]).reshape(half, L // 8, 8, wide)
+            here = slice(g * wide, (g + 2) * wide)
+            y = dot(x_from[...], a_ref[:, here]).reshape(half, L // 8, 8, 2 * wide)
             acc = acc_ref[:, :, here]
             for k in range(half):
                 acc = acc + s_ref[k0 + k, :, here] * y[k]

time: 77.8 us -> 77.8 us (level)
  no operation moved by 1% of the time
where the time goes in v11:
time: 77.8 us; the launch traced here: 77.5 us
  Pallas kernels  43.4 us (56%)
  blocking collectives  19.8 us (25%)
  starting transfers between devices  10.3 us (13%)
  waiting for transfers between devices  2.62 us (3%)
    pallas_call x1, Pallas kernels, beamform(): pl.pallas_call(functools.partial(beam_kernel, scale), grid=(groups // som...  21.5 us
    all_to_all x1, blocking collectives, on_device(): parts = lax.all_to_all(parts, ('tx', 'img'), 0, 0, tiled=True)  19.8 us
    pallas_call x1, Pallas kernels, decode(): pl.pallas_call(decode_kernel, grid=(receivers // RB,), in_specs=[pl.Block...  19.4 us
    all_to_all x1, starting transfers between devices, on_device(): masks = lax.all_to_all(masks, 'img', 0, 0, tiled=True)  7.31 us
    ppermute x3, starting transfers between devices, on_device(): lax.ppermute(own, 'tx', [((t + d) % stripes, t) for t in range(stripes)])  2.95 us
    all_to_all x1, waiting for transfers between devices, on_device(): masks = lax.all_to_all(masks, 'img', 0, 0, tiled=True)  2.61 us
    pallas_call x1, Pallas kernels, cast(): pl.pallas_call(functools.partial(cast_kernel, stripes), grid_spec=pltpu.P...  2.46 us
  transfers between devices with their start and end apart: 4, of which 1 were waited for; matrix products, arithmetic and copies ran while one was open for 0% of the time, Pallas kernels for 25%

profile of v11, /device:TPU:0, one launch (start us, length us, event | category | flops | bytes accessed | tf_op | source)
XLA Modules:
  0.0 77.5 jit_solution(7030144671940640844)
XLA Ops:
  0.0 2.5 %shard_map.55 = (bf16[8,2,128,256]{3,2,1,0:T(8,128)(2,1)}, bf16[16,2048]{1,0:T(8,128)(2,1)}, bf16[64,256]{1,0:T(8,128)(2,1)}) custom-call(s32[1]{0:T(128)} %bitcast.at_ref, s32[8,128,256]{2,1,0:T(8,128)} %bitcast.8, s32[8,128,256]{2,1,0:T(8,128)} %bitcast.9, s32[16,2048]{1,0:T(8,128)} %tx_ref.1, s32[64,1024]{1,0:T(8,128)} %bitcast.10), custom_call_target="tpu_custom_call" | custom-call | tf_op jit(solution)/shard_map/pallas_call | solution.py:51
  2.5 7.3 %all-to-all-start = ((bf16[8,2,128,256]{3,2,1,0:T(8,128)(2,1)}), bf16[8,2,128,256]{3,2,1,0:T(8,128)(2,1)S(1)}, u32[]{:S(2)}, u32[]{:S(2)}) async-start(bf16[8,2,128,256]{3,2,1,0:T(8,128)(2,1)} %get-tuple-element.10), calls=%async_computation | async-start | bytes 2097152 | tf_op jit(solution)/shard_map/all_to_all | solution.py:289
  9.8 0.0 collective-permute-start.2
  9.8 1.6 %collective-permute-start.1 = (bf16[16,2048]{1,0:T(8,128)(2,1)}, bf16[16,2048]{1,0:T(8,128)(2,1)S(1)}, u32[]{:S(2)}, u32[]{:S(2)}) collective-permute-start(bf16[16,2048]{1,0:T(8,128)(2,1)} %get-tuple-element.14.refs_0_), channel_id=1, source_target_pairs={{16,0},{24,8},{0,16},{8,24},{17,1},{25,9},{1,17},{9,25},{18,2},{26... | collective-permute-start | bytes 196616 | tf_op jit(solution)/shard_map/ppermute | solution.py:291
  11.3 1.4 %collective-permute-start = (bf16[16,2048]{1,0:T(8,128)(2,1)}, bf16[16,2048]{1,0:T(8,128)(2,1)S(1)}, u32[]{:S(2)}, u32[]{:S(2)}) collective-permute-start(bf16[16,2048]{1,0:T(8,128)(2,1)} %get-tuple-element.14.refs_0_), channel_id=1, source_target_pairs={{8,0},{16,8},{24,16},{0,24},{9,1},{17,9},{25,17},{1,25},{10,2},{18... | collective-permute-start | bytes 196616 | tf_op jit(solution)/shard_map/ppermute | solution.py:291
  12.7 0.0 copy-start
  12.7 0.8 copy-done
  13.5 0.0 copy-start.1
  13.5 19.4 %shard_map.56 = (bf16[32,2,128,384]{3,2,1,0:T(8,128)(2,1)}, f32[128,384]{1,0:T(8,128)S(1)}) custom-call(bf16[64,256]{1,0:T(8,128)(2,1)S(1)} %copy-done, bf16[256,128,512]{2,1,0:T(8,128)(2,1)} %refs_3_.1, bf16[256,128,512]{2,1,0:T(8,128)(2,1)} %refs_3_.1, bf16[256,128,512]{2,1,0:T(8,128)(2,1)} %refs_3_.1, bf16[256,128,512]{2,1,0:T(8,128)(2,1)} %refs_3_.1), custom_call_target="tpu_custom_call" | custom-call | flops 17179869184 | bytes 39845888 | tf_op jit(solution)/shard_map/pallas_call | solution.py:138
  32.9 0.0 collective-permute-done.2.refs_3_
  32.9 0.0 collective-permute-done.1.refs_2_
  32.9 0.0 collective-permute-done.refs_1_
  32.9 2.6 %all-to-all-done.mask_ref = bf16[8,2,128,256]{3,2,1,0:T(8,128)(2,1)S(1)} async-done(((bf16[8,2,128,256]{3,2,1,0:T(8,128)(2,1)}), bf16[8,2,128,256]{3,2,1,0:T(8,128)(2,1)S(1)}, u32[]{:S(2)}, u32[]{:S(2)}) %all-to-all-start) | async-done | bytes 1048608 | tf_op jit(solution)/shard_map/all_to_all | solution.py:289
  35.5 0.0 copy-done.1
  35.5 21.5 %shard_map.57 = bf16[4,8,32,256]{3,2,1,0:T(8,128)(2,1)S(1)} custom-call(bf16[8,2,128,256]{3,2,1,0:T(8,128)(2,1)S(1)} %all-to-all-done.mask_ref, bf16[64,128,384]{2,1,0:T(8,128)(2,1)} %bitcast.11, f32[128,384]{1,0:T(8,128)S(1)} %get-tuple-element.13.dsum_ref, bf16[16,2048]{1,0:T(8,128)(2,1)S(1)} %copy-done.1, ...), custom_call_target="tpu_custom_call" | custom-call | flops 12884901888 | bytes 6291456 | tf_op jit(solution)/shard_map/pallas_call | solution.py:248
  57.0 19.8 %all_to_all.10 = bf16[32,32,256]{2,1,0:T(8,128)(2,1)S(1)} all-to-all(bf16[32,32,256]{2,1,0:T(8,128)(2,1)S(1)} %bitcast.7), channel_id=1, replica_groups=mesh['tx'=4,'img'=8] {'tx','img'}, dimensions={0} | all-to-all | bytes 1048576 | tf_op jit(solution)/shard_map/all_to_all | solution.py:299
  76.8 0.7 convert_reduce_fusion
Async XLA Ops:
  2.5 33.1 %all-to-all-start = ((bf16[8,2,128,256]{3,2,1,0:T(8,128)(2,1)}), bf16[8,2,128,256]{3,2,1,0:T(8,128)(2,1)S(1)}, u32[]{:S(2)}, u32[]{:S(2)}) async-start(bf16[8,2,128,256]{3,2,1,0:T(8,128)(2,1)} %get-tuple-element.10), calls=%async_computation | async-start | bytes 2097152 | tf_op jit(solution)/shard_map/all_to_all | solution.py:289
  9.8 23.1 %collective-permute-start.2 = (bf16[16,2048]{1,0:T(8,128)(2,1)}, bf16[16,2048]{1,0:T(8,128)(2,1)S(1)}, u32[]{:S(2)}, u32[]{:S(2)}) collective-permute-start(bf16[16,2048]{1,0:T(8,128)(2,1)} %get-tuple-element.14.refs_0_), channel_id=1, source_target_pairs={{24,0},{0,8},{8,16},{16,24},{25,1},{1,9},{9,17},{17,25},{26,2},{2,... | collective-permute-start | bytes 196616 | tf_op jit(solution)/shard_map/ppermute | solution.py:291
  9.8 23.1 %collective-permute-start.1 = (bf16[16,2048]{1,0:T(8,128)(2,1)}, bf16[16,2048]{1,0:T(8,128)(2,1)S(1)}, u32[]{:S(2)}, u32[]{:S(2)}) collective-permute-start(bf16[16,2048]{1,0:T(8,128)(2,1)} %get-tuple-element.14.refs_0_), channel_id=1, source_target_pairs={{16,0},{24,8},{0,16},{8,24},{17,1},{25,9},{1,17},{9,25},{18,2},{26... | collective-permute-start | bytes 196616 | tf_op jit(solution)/shard_map/ppermute | solution.py:291
  11.3 21.6 %collective-permute-start = (bf16[16,2048]{1,0:T(8,128)(2,1)}, bf16[16,2048]{1,0:T(8,128)(2,1)S(1)}, u32[]{:S(2)}, u32[]{:S(2)}) collective-permute-start(bf16[16,2048]{1,0:T(8,128)(2,1)} %get-tuple-element.14.refs_0_), channel_id=1, source_target_pairs={{8,0},{16,8},{24,16},{0,24},{9,1},{17,9},{25,17},{1,25},{10,2},{18... | collective-permute-start | bytes 196616 | tf_op jit(solution)/shard_map/ppermute | solution.py:291
  12.7 0.8 copy-start
  13.5 22.1 %copy-start.1 = (bf16[16,2048]{1,0:T(8,128)(2,1)S(1)}, bf16[16,2048]{1,0:T(8,128)(2,1)}, u32[]{:S(2)}) copy-start(bf16[16,2048]{1,0:T(8,128)(2,1)} %get-tuple-element.14.refs_0_) | copy-start | bytes 196612
